TPU v7x, 32 devices: a whole 2x2x4 slice. The times are simulated.
32 devices in a mesh: ctx: 8 (over y, x, core), head: 4 (over z).
Axes of the slice: x: 2, y: 2, z: 4, core: 2. Of those that a mesh axis runs over, the one named last changes fastest.
Arguments:
- queries: bfloat16 [4096, 4096], P('ctx', 'head'), may hold values from -6 to 6
- key_rows: bfloat16 [4096, 4096], P('ctx', 'head'), may hold values from -6 to 6
- value_rows: bfloat16 [4096, 4096], P('ctx', 'head'), may hold values from -6 to 6
- doc_lengths: int32 [4], replicated, may hold values from 1 to 2048, 4096 in all
- out_weight: bfloat16 [4096, 4096], P('head'), may hold values from -0.09375 to 0.09375
- out_grad: bfloat16 [4096, 4096], P('ctx', 'head'), may hold values from -6 to 6
Outputs:
- mixed: bfloat16 [4096, 4096], P('ctx', 'head')
- query_grad: bfloat16 [4096, 4096], P('ctx', 'head')
- key_grad: bfloat16 [4096, 4096], P('ctx', 'head')
- value_grad: bfloat16 [4096, 4096], P('ctx', 'head')
Inputs may be any that keep to these rules, and one draw needn't show every extreme that they name: `doc_lengths`: the lengths of the 4 documents packed in order from position 0; they sum to 4096 and the longest is exactly 2048.
All inputs are finite; a program needn't handle non-finite values.
Results may differ from a plain program's by a relative error of at most 0.015.
Values may be sent and summed in bfloat16 or wider, within the bound.
No kernel may reach another device: no remote copies, remote signals or barrier semaphores. Data moves between devices by JAX's collectives and lax.ppermute only.
A program may use at most 128 MiB of HBM per device.

v0:
```python
import jax
import jax.numpy as jnp
from jax import lax
from jax.sharding import PartitionSpec as P

DH = 128


epsilon = 1e-06


def entering_2(shard, axis, combine, identity):
    size, here = (lax.axis_size(axis), lax.axis_index(axis))
    everything = jax.tree.map(
        lambda part, kind: lax.all_gather(part.astype(kind), axis),
        shard,
        (jnp.bfloat16, jnp.bfloat16),
    )
    start = jax.tree.map(
        lambda part, zero: jnp.broadcast_to(jnp.asarray(zero, part.dtype), part.shape),
        shard,
        identity,
    )

    def lap(k, before):
        at = size - 1 - k
        reached = at > here
        new = combine(
            before, jax.tree.map(lambda part, own: part[at].astype(own.dtype), everything, shard)
        )
        return jax.tree.map(lambda a, b: jnp.where(reached, a, b), new, before)

    return lax.fori_loop(0, size, lap, start)


def doc_numbers(doc_lengths, positions):
    opening = jnp.cumsum(doc_lengths) - doc_lengths
    return jnp.sum((opening[None, :] <= positions[:, None]).astype(jnp.int32), axis=1) - 1


def join_states(earlier, latter):
    reset_early, state_early = earlier
    reset_late, state_late = latter
    keep_factor = (1.0 - reset_late).reshape((-1, 1, 1, 1))
    return (jnp.maximum(reset_early, reset_late), state_late + keep_factor * state_early)


def prefix_from_all(all_resets, all_states, device_index):
    member_ids = jnp.arange(all_resets.shape[0], dtype=jnp.int32)
    lowest = jnp.max(jnp.where((all_resets > 0.5) & (member_ids < device_index), member_ids, 0))
    weights = ((member_ids >= lowest) & (member_ids < device_index)).astype(jnp.float32)
    return jnp.einsum("k,khde->hde", weights, all_states, precision=lax.Precision.HIGHEST)


def head_major(matrix, heads_here):
    return matrix.reshape(matrix.shape[0], heads_here, DH).transpose(1, 0, 2)


def row_major(tensor):
    return tensor.transpose(1, 0, 2).reshape(tensor.shape[1], tensor.shape[0] * tensor.shape[2])


def shards(queries, key_rows, value_rows, doc_lengths, out_weight, out_grad):
    tok_rows = queries.shape[0]
    heads_here = queries.shape[1] // DH
    device_index = lax.axis_index("ctx")
    first_pos = device_index * tok_rows
    positions = first_pos + jnp.arange(tok_rows, dtype=jnp.int32)
    doc_here = doc_numbers(doc_lengths, positions)
    doc_before = doc_numbers(doc_lengths, (first_pos - 1).reshape((1,)))
    carry_in = (doc_here == doc_before).astype(jnp.float32)
    carry_out = (doc_here == doc_here[-1]).astype(jnp.float32)
    reset_flag = 1.0 - carry_in[-1:]
    causal = (positions[None, :] <= positions[:, None]) & (doc_here[None, :] == doc_here[:, None])
    query_heads = head_major(queries, heads_here)
    key_heads = head_major(key_rows, heads_here)
    value_heads = head_major(value_rows, heads_here)
    keep_in_col = carry_in[None, :, None]
    keep_out_col = carry_out[None, :, None]
    scores = jnp.einsum("htd,hsd->hts", query_heads, key_heads, preferred_element_type=jnp.float32)
    score_mask = jnp.where(causal[None], scores, 0.0).astype(jnp.bfloat16)
    intra_part = jnp.einsum(
        "hts,hsd->htd", score_mask, value_heads, preferred_element_type=jnp.float32
    )
    kept_keys = key_heads * carry_out.astype(jnp.bfloat16)[None, :, None]
    local_state = jnp.einsum(
        "hsd,hse->hde", kept_keys, value_heads, preferred_element_type=jnp.float32
    )
    identity_pair = (jnp.zeros((1,), jnp.float32), jnp.zeros((1,) + local_state.shape, jnp.float32))
    all_resets, all_states = (
        lax.all_gather(reset_flag.astype(jnp.bfloat16), "ctx", axis=0, tiled=True).astype(
            reset_flag.dtype
        ),
        lax.all_gather(local_state[None].astype(jnp.bfloat16), "ctx", axis=0, tiled=True).astype(
            jnp.float32
        ),
    )
    entering = prefix_from_all(all_resets, all_states, device_index)
    entering_b = entering.astype(jnp.bfloat16)
    inter_part = jnp.einsum(
        "htd,hde->hte", query_heads, entering_b, preferred_element_type=jnp.float32
    )
    attended = intra_part + inter_part * keep_in_col
    root_mean = jnp.sqrt(jnp.mean(attended * attended, axis=-1, keepdims=True) + epsilon)
    normed = attended / root_mean
    normed_b = row_major(normed.astype(jnp.bfloat16))
    partial_out = jnp.dot(normed_b, out_weight, preferred_element_type=jnp.float32)
    mixed = lax.psum_scatter(
        partial_out.astype(jnp.bfloat16), "head", scatter_dimension=1, tiled=True
    )
    normed_grad = lax.dot_general(
        lax.all_gather(out_grad, "head", axis=1, tiled=True),
        out_weight,
        (((1,), (1,)), ((), ())),
        preferred_element_type=jnp.float32,
    )
    normed_grad = head_major(normed_grad, heads_here)
    projection = jnp.mean(normed_grad * normed, axis=-1, keepdims=True)
    attended_grad = ((normed_grad - normed * projection) / root_mean).astype(jnp.bfloat16)
    kept_queries = query_heads * carry_in.astype(jnp.bfloat16)[None, :, None]
    local_grad = jnp.einsum(
        "htd,hte->hde", kept_queries, attended_grad, preferred_element_type=jnp.float32
    )
    scanned_back = entering_2((reset_flag, local_grad[None]), "ctx", join_states, identity_pair)
    leaving = scanned_back[1][0]
    leaving_b = leaving.astype(jnp.bfloat16)
    raw_grad = jnp.einsum(
        "hte,hse->hts", attended_grad, value_heads, preferred_element_type=jnp.float32
    )
    grad_scores = jnp.where(causal[None], raw_grad, 0.0).astype(jnp.bfloat16)
    query_grad = jnp.einsum(
        "hts,hsd->htd", grad_scores, key_heads, preferred_element_type=jnp.float32
    )
    query_grad = query_grad + keep_in_col * jnp.einsum(
        "hte,hde->htd", attended_grad, entering_b, preferred_element_type=jnp.float32
    )
    key_grad = jnp.einsum(
        "hts,htd->hsd", grad_scores, query_heads, preferred_element_type=jnp.float32
    )
    key_grad = key_grad + keep_out_col * jnp.einsum(
        "hse,hde->hsd", value_heads, leaving_b, preferred_element_type=jnp.float32
    )
    value_grad = jnp.einsum(
        "hts,hte->hse", score_mask, attended_grad, preferred_element_type=jnp.float32
    )
    value_grad = value_grad + keep_out_col * jnp.einsum(
        "hsd,hde->hse", key_heads, leaving_b, preferred_element_type=jnp.float32
    )
    return (
        mixed,
        row_major(query_grad.astype(jnp.bfloat16)),
        row_major(key_grad.astype(jnp.bfloat16)),
        row_major(value_grad.astype(jnp.bfloat16)),
    )


def solution(mesh):
    return jax.shard_map(
        shards,
        mesh=mesh,
        in_specs=(
            P("ctx", "head"),
            P("ctx", "head"),
            P("ctx", "head"),
            P(),
            P("head", None),
            P("ctx", "head"),
        ),
        out_specs=(P("ctx", "head"), P("ctx", "head"), P("ctx", "head"), P("ctx", "head")),
        check_vma=False,
    )
```

profile of v0, /device:TPU:0, one launch (start us, length us, event | category | flops | bytes accessed | tf_op | source)
XLA Modules:
  0.0 252.9 jit_solution(11345391929288264407)
XLA Ops:
  11.4 2.9 %convolution_convert_fusion.2 = bf16[8,128,128]{2,1,0:T(8,128)(2,1)} fusion(bf16[512]{0:T(512)(128)(2,1)S(1)} %get-tuple-element.202, bf16[512,1024]{1,0:T(8,128)(2,1)} %param.10, bf16[512,1024]{1,0:T(8,128)(2,1)} %param.9), kind=kOutput, calls=%fused_computation.21 | convolution fusion | flops 136445952 | bytes 2360320 | tf_op jit(solution)/shard_map/hsd,hse->hde/dot_general | solution.py:86
  17.7 15.3 %all-reduce = bf16[8]{0:T(256)(128)(2,1)S(1)} all-reduce(bf16[8]{0:T(256)(128)(2,1)S(1)} %dynamic-update-slice), channel_id=1, replica_groups=mesh['ctx'=8,'head'=4] {'ctx'}, use_global_device_ids=true, to_apply=%add | all-reduce | flops 8 | bytes 32
  36.7 3.4 %select_convert_fusion.1 = bf16[8,512,512]{2,1,0:T(8,128)(2,1)} fusion(pred[512,512]{1,0:T(8,128)(4,1)S(1)} %compare_and_fusion, bf16[8,512,128]{1,2,0:T(8,128)(2,1)S(1)} %bitcast.137, bf16[512,1024]{1,0:T(8,128)(2,1)S(1)} %copy-done.9), kind=kOutput, calls=%fused_computation.4 | convolution fusion | flops 541065216 | bytes 6553600 | tf_op jit(solution)/shard_map/htd,hsd->hts/dot_general | solution.py:80
  40.1 5.1 %all-gather.9.cloned.1.call-done = bf16[64,128,128]{2,1,0:T(8,128)(2,1)} async-done(((bf16[8,128,128]{2,1,0:T(8,128)(2,1)}), bf16[64,128,128]{2,1,0:T(8,128)(2,1)}) %all-gather.9.cloned.1.call-update) | async-done | bytes 2097168 | tf_op jit(solution)/shard_map/all_gather | solution.py:94
  45.2 4.0 %fusion.5 = f32[1,8,128,128]{3,0,2,1:T(1,128)S(1)} fusion(bf16[8,8,128,128]{3,2,1,0:T(8,128)(2,1)} %bitcast.150, s32[]{:T(128)} %fusion.37, s32[]{:T(128)} %axis_index.19), kind=kOutput, calls=%fused_computation.14 | convolution fusion | flops 2097176 | bytes 2621448 | tf_op jit(solution)/shard_map/k,khde->hde/dot_general | solution.py:52
  50.6 3.6 %multiply_reduce_fusion.1 = (f32[8,512]{1,0:T(8,128)S(1)}, f32[8,512,128]{1,2,0:T(8,128)}, f32[8,512,128]{1,2,0:T(8,128)}) fusion(f32[8,128,512]{2,1,0:T(8,128)S(1)} %fusion.29, f32[512]{0:T(512)S(1)} %get-tuple-element.193, bf16[8,512,512]{2,1,0:T(8,128)(2,1)S(1)} %copy-done.2, bf16[8,512,128]{2,0,1:T(8,128)(2,1)S(1)} %bitcast.145), kind=kOutput, calls=%fused_computation.19 | convolution fusion | flops 538963968 | bytes 11552768 | tf_op jit(solution)/shard_map/hts,hsd->htd/dot_general | solution.py:82
  54.2 73.4 %all-gather.7.cloned.1.call-done = bf16[512,4096]{1,0:T(8,128)(2,1)} async-done(((bf16[512,1024]{1,0:T(8,128)(2,1)}), bf16[512,4096]{1,0:T(8,128)(2,1)}) %all-gather.7.cloned.1.call-update) | async-done | bytes 4194320 | tf_op jit(solution)/shard_map/all_gather | solution.py:112
  127.5 9.8 %multiply_reduce_fusion = (f32[8,512]{1,0:T(8,128)S(1)}, f32[512,1024]{0,1:T(8,128)S(1)}) fusion(f32[8,512,128]{1,2,0:T(8,128)} %get-tuple-element.195, f32[8,512]{1,0:T(8,128)S(1)} %get-tuple-element.200, bf16[512,4096]{1,0:T(8,128)(2,1)} %all-gather.7.cloned.1.call-done, bf16[1024,4096]{1,0:T(8,128)(2,1)} %param.12), kind=kOutput, calls=%fused_computation.18 | convolution fusion | flops 4296536064 | bytes 16809984 | tf_op jit(solution)/shard_map/dot_general | solution.py:111
  140.5 2.1 fusion.4
  142.6 9.6 %convolution_convert_fusion = bf16[512,4096]{1,0:T(8,128)(2,1)} fusion(bf16[512,1024]{0,1:T(8,128)(2,1)S(1)} %bitcast.151, bf16[1024,4096]{1,0:T(8,128)(2,1)} %param.12), kind=kOutput, calls=%fused_computation.5 | convolution fusion | flops 4297064448 | bytes 13631488 | tf_op jit(solution)/shard_map/dot_general | solution.py:107
  159.0 2.3 copy.61
  161.3 5.5 %all-gather.11.cloned.1.call-done = bf16[64,128,128]{2,1,0:T(8,128)(2,1)} async-done(((bf16[8,128,128]{2,1,0:T(8,128)(2,1)}), bf16[64,128,128]{2,1,0:T(8,128)(2,1)}) %all-gather.11.cloned.1.call-update) | async-done | bytes 2097168 | tf_op jit(solution)/shard_map/all_gather | solution.py:15
  166.8 20.3 %while.16 = (s32[]{:T(128)}, f32[1,8,128,128]{3,2,1,0:T(8,128)S(1)}, s32[]{:T(128)}, bf16[8,1,8,128,128]{4,3,2,1,0:T(8,128)(2,1)}, bf16[8,1]{0,1:T(2,128)(2,1)S(...) while((s32[]{:T(128)}, f32[1,8,128,128]{3,2,1,0:T(8,128)S(1)}, s32[]{:T(128)}, ...), condition=%wide.region_8.9_spmd.clone, body=%wide.region_7.8_spmd.clone.sunk | while | flops 655369 | bytes 1310905 | solution.py:33
  167.4 1.9 fusion.69
  169.9 1.9 fusion.69
  172.5 1.9 fusion.69
  175.0 2.0 fusion.69
  177.6 1.9 fusion.69
  180.2 1.9 fusion.69
  182.7 1.9 fusion.69
  188.8 4.0 %fusion.2 = bf16[512,8,128]{0,2,1:T(8,128)(2,1)} fusion(f32[8,128,512]{2,1,0:T(8,128)S(1)} %fusion.7, bf16[8,512,128]{1,2,0:T(8,128)(2,1)S(1)} %bitcast.140, bf16[8,512,512]{2,1,0:T(8,128)(2,1)} %copy-done.1, f32[512]{0:T(512)S(1)} %get-tuple-element.203), kind=kOutput, calls=%fused_computation.9 | convolution fusion | flops 538443776 | bytes 8390656 | tf_op jit(solution)/shard_map/hts,htd->hsd/dot_general | solution.py:137
  192.8 2.4 copy.62
  195.7 3.0 %fusion.1 = bf16[512,8,128]{0,2,1:T(8,128)(2,1)S(1)} fusion(f32[8,128,512]{2,1,0:T(8,128)S(1)} %fusion.8, bf16[8,512,128]{1,2,0:T(8,128)(2,1)S(1)} %copy-done.4, bf16[8,512,512]{2,1,0:T(8,128)(2,1)} %select_convert_fusion.1, f32[512]{0:T(512)S(1)} %get-tuple-element.203), kind=kOutput, calls=%fused_computation.7 | convolution fusion | flops 538443776 | bytes 8390656 | tf_op jit(solution)/shard_map/hts,hte->hse/dot_general | solution.py:143
  200.0 46.3 %reduce-scatter.2.cloned.1.call-done = bf16[512,1024]{1,0:T(8,128)(2,1)} async-done(((bf16[512,4096]{1,0:T(8,128)(2,1)}), bf16[512,1024]{1,0:T(8,128)(2,1)}) %reduce-scatter.2.cloned.1.call-update) | async-done | bytes 1048592 | tf_op jit(solution)/shard_map/reduce_scatter | solution.py:108
  (71 shorter events, 31.8 us)
Async XLA Ops:
  7.2 38.0 %all-gather.9.cloned.1.call-start = ((), (), s32[]{:S(2)}) async-start(), calls=%async_computation.3 | async-start | bytes 2359296 | tf_op jit(solution)/shard_map/all_gather | solution.py:94
  11.3 4.3 %copy-start.12 = (u32[32]{0:T(128)S(1)}, u32[32]{0:T(128)}, u32[]{:S(2)}) copy-start(u32[32]{0:T(128)} %constant.91) | copy-start | bytes 388
  14.3 20.3 %copy-start.7 = (bf16[512,1024]{1,0:T(8,128)(2,1)S(1)}, bf16[512,1024]{1,0:T(8,128)(2,1)}, u32[]{:S(2)}) copy-start(bf16[512,1024]{1,0:T(8,128)(2,1)} %param.10) | copy-start | bytes 3145732
  14.3 113.3 %all-gather.7.cloned.1.call-start = ((), (), s32[]{:S(2)}) async-start(), calls=%async_computation.2 | async-start | bytes 5242880 | tf_op jit(solution)/shard_map/all_gather | solution.py:112
  15.0 151.8 %all-gather.11.cloned.1.call-start = ((), (), s32[]{:S(2)}) async-start(), calls=%async_computation.4 | async-start | bytes 2359296 | tf_op jit(solution)/shard_map/all_gather | solution.py:15
  32.9 3.8 %copy-start.9 = (bf16[512,1024]{1,0:T(8,128)(2,1)S(1)}, bf16[512,1024]{1,0:T(8,128)(2,1)}, u32[]{:S(2)}) copy-start(bf16[512,1024]{1,0:T(8,128)(2,1)} %param.9) | copy-start | bytes 3145732
  45.2 5.2 %copy-start.2 = (bf16[8,512,512]{2,1,0:T(8,128)(2,1)S(1)}, bf16[8,512,512]{2,1,0:T(8,128)(2,1)}, u32[]{:S(2)}) copy-start(bf16[8,512,512]{2,1,0:T(8,128)(2,1)} %select_convert_fusion.1) | copy-start | bytes 12582916
  49.1 0.8 copy-start.5
  49.1 1.4 copy-start.11
  127.5 9.9 %copy-start = (f32[8,512,128]{1,2,0:T(8,128)S(1)}, f32[8,512,128]{1,2,0:T(8,128)}, u32[]{:S(2)}) copy-start(f32[8,512,128]{1,2,0:T(8,128)} %get-tuple-element.195) | copy-start | bytes 6291460
  138.1 1.0 copy-start.3
  140.2 106.1 %reduce-scatter.2.cloned.1.call-start = ((), (), s32[]{:S(2)}) async-start(), calls=%async_computation.1 | async-start | bytes 5242880 | tf_op jit(solution)/shard_map/reduce_scatter | solution.py:108
  152.3 1.7 copy-start.4
  152.3 1.8 copy-start.8
  155.6 2.0 copy-start.1
  155.6 2.0 copy-start.6
  192.8 2.4 copy-start.10
Sparse Core Ops, SparseCore 0:
  14.4 30.7 all-gather.8
  46.7 80.7 all-gather.6
  140.4 26.4 all-gather.10
  169.5 76.7 reduce-scatter.1
where the time goes:
time: 254 us; the launch traced here: 253 us
  waiting for transfers between devices  131 us (52%)
  matrix products  48.5 us (19%)
  other arithmetic  27.3 us (11%)
  local copies, waits for them, and re-layouts  15.5 us (6%)
  blocking collectives  15.3 us (6%)
  between operations  14.7 us (6%)
    all_gather x1, waiting for transfers between devices, shards(): lax.all_gather(out_grad, 'head', axis=1, tiled=True)  73.4 us
    reduce_scatter x1, waiting for transfers between devices, shards(): lax.psum_scatter(partial_out.astype(jnp.bfloat16), 'head', scatter_dimens...  46.3 us
    select_n x8, other arithmetic, lap(): return jax.tree.map(lambda a, b: jnp.where(reached, a, b), new, before)  15.5 us
    unnamed x1, blocking collectives  15.3 us
    unnamed x34, local copies, waits for them, and re-layouts  13.3 us
    dot_general x1, matrix products, shards(): lax.dot_general(lax.all_gather(out_grad, 'head', axis=1, tiled=True), out...  9.85 us
    dot_general x1, matrix products, shards(): jnp.dot(normed_b, out_weight, preferred_element_type=jnp.float32)  9.64 us
    all_gather x1, waiting for transfers between devices, entering_2(): lax.all_gather(part.astype(kind), axis)  5.55 us
  transfers between devices with their start and end apart: 4, of which 4 were waited for; matrix products, arithmetic and copies ran while one was open for 28% of the time, Pallas kernels for 0%

commit v1 on v0

v1 whole, which is shorter than its diff:
```python
import functools

import jax
import jax.numpy as jnp
from jax import lax
from jax.experimental import pallas as pl
from jax.experimental.pallas import tpu as pltpu
from jax.sharding import PartitionSpec as P

DH = 128
EPS = 1e-06
F32 = jnp.float32
BF16 = jnp.bfloat16
VMEM_LIMIT = 48 * 1024 * 1024

I_BLK, I_HALF, I_DOC = 0, 1, 2


def params(n_axes=1):
    return pltpu.CompilerParams(
        vmem_limit_bytes=VMEM_LIMIT, dimension_semantics=("arbitrary",) * n_axes
    )


def cost(flops, nbytes):
    return pl.CostEstimate(flops=int(flops), bytes_accessed=int(nbytes), transcendentals=0)


def call(body, name, grid, n_scalar, in_specs, out_specs, out_shape, scratch=(), flops=0, nbytes=0):
    return pl.pallas_call(
        body,
        name=name,
        grid_spec=pltpu.PrefetchScalarGridSpec(
            num_scalar_prefetch=n_scalar,
            grid=grid,
            in_specs=in_specs,
            out_specs=out_specs,
            scratch_shapes=list(scratch),
        ),
        out_shape=out_shape,
        compiler_params=params(len(grid)),
        cost_estimate=cost(flops, nbytes),
    )


def dot(a, b, ca, cb):
    return lax.dot_general(a, b, (((ca,), (cb,)), ((), ())), preferred_element_type=F32)


def starts_of(lens_ref):
    out, at = [], jnp.int32(0)
    for j in range(lens_ref.shape[0]):
        out.append(at)
        at = at + lens_ref[j]
    return out


def start_at(starts, p):
    best = jnp.where(p >= 0, 0, -1) if not hasattr(p, "shape") or p.shape == () else None
    if best is None:
        best = jnp.where(p >= 0, jnp.zeros_like(p), -jnp.ones_like(p))
    for s in starts[1:]:
        best = jnp.where(p >= s, s, best)
    return best


def rows_pos(tok, first):
    return lax.broadcasted_iota(jnp.int32, (tok, 1), 0) + first


def carry_in_of(info_ref, lens_ref, tok):
    first = info_ref[I_BLK] * tok
    starts = starts_of(lens_ref)
    rows = start_at(starts, rows_pos(tok, first))
    return rows == start_at(starts, first - 1)


def carry_out_of(info_ref, lens_ref, tok):
    first = info_ref[I_BLK] * tok
    starts = starts_of(lens_ref)
    rows = start_at(starts, rows_pos(tok, first))
    return rows == start_at(starts, first + tok - 1)


def mask_of(info_ref, lens_ref, tok, r0, rn, cn):
    first = info_ref[I_BLK] * tok
    starts = starts_of(lens_ref)
    low = start_at(starts, rows_pos(rn, first + r0)) - first
    row = lax.broadcasted_iota(jnp.int32, (rn, cn), 0) + r0
    col = lax.broadcasted_iota(jnp.int32, (rn, cn), 1)
    return (col <= row) & (col >= low)


def state_body(info_ref, lens_ref, k_ref, v_ref, send_ref, keep_ref):
    i = pl.program_id(0)
    half = pl.num_programs(0) // 2
    tok = k_ref.shape[0]
    keep = carry_out_of(info_ref, lens_ref, tok)
    kept = jnp.where(keep, k_ref[...], jnp.zeros((), BF16))
    state = dot(kept, v_ref[...], 0, 0).astype(BF16)

    @pl.when(i < half)
    def _():
        send_ref[0] = state

    @pl.when(i >= half)
    def _():
        keep_ref[0] = state


def local_states(info, lens, k, v):
    tok, wide = k.shape
    heads = wide // DH
    half = heads // 2

    def head_of(i, info, lens):
        return (0, lax.rem(i + half * (1 - info[I_HALF]), heads))

    return call(
        state_body,
        "local_states",
        (heads,),
        2,
        [pl.BlockSpec((tok, DH), head_of), pl.BlockSpec((tok, DH), head_of)],
        [
            pl.BlockSpec((1, DH, DH), lambda i, *_: (jnp.minimum(i, half - 1), 0, 0)),
            pl.BlockSpec((1, DH, DH), lambda i, *_: (jnp.maximum(i - half, 0), 0, 0)),
        ],
        [jax.ShapeDtypeStruct((half, DH, DH), BF16)] * 2,
        flops=2 * tok * DH * wide,
        nbytes=4 * tok * wide,
    )(info, lens, k, v)


def intra_body(info_ref, lens_ref, q_ref, k_ref, v_ref, out_ref):
    tok = q_ref.shape[0]
    hb = tok // 2
    for part in range(2):
        r0, n = part * hb, (part + 1) * hb
        s = dot(q_ref[r0:r0 + hb, :], k_ref[:n, :], 1, 1)
        s = jnp.where(mask_of(info_ref, lens_ref, tok, r0, hb, n), s, 0.0).astype(BF16)
        out_ref[r0:r0 + hb, :] = dot(s, v_ref[:n, :], 1, 0)


def col(tok):
    return pl.BlockSpec((tok, DH), lambda h, *_: (0, h))


def state_spec():
    return pl.BlockSpec((1, DH, DH), lambda h, *_: (h, 0, 0))


def intra(info, lens, q, k, v):
    tok, wide = q.shape
    return call(
        intra_body,
        "intra",
        (wide // DH,),
        2,
        [col(tok)] * 3,
        col(tok),
        jax.ShapeDtypeStruct((tok, wide), F32),
        flops=3 * tok * tok * wide,
        nbytes=10 * tok * wide,
    )(info, lens, q, k, v)


def norm_body(info_ref, lens_ref, q_ref, e_ref, a_ref, att_ref, n_ref):
    tok = q_ref.shape[0]
    keep = carry_in_of(info_ref, lens_ref, tok)
    inter = dot(q_ref[...], e_ref[0], 1, 0)
    att = a_ref[...] + jnp.where(keep, inter, 0.0)
    att_ref[...] = att
    inv = lax.rsqrt(jnp.mean(att * att, axis=-1, keepdims=True) + EPS)
    n_ref[...] = (att * inv).astype(BF16)


def normalise(info, lens, q, entering, a):
    tok, wide = q.shape
    return call(
        norm_body,
        "normalise",
        (wide // DH,),
        2,
        [col(tok), state_spec(), col(tok)],
        [col(tok), col(tok)],
        [jax.ShapeDtypeStruct((tok, wide), F32), jax.ShapeDtypeStruct((tok, wide), BF16)],
        flops=2 * tok * DH * wide,
        nbytes=12 * tok * wide,
    )(info, lens, q, entering, a)


def proj_body(b_ref, n_ref, w_ref, o_ref):
    o_ref[...] = dot(n_ref[...], w_ref[...], 1, 0).astype(BF16)


def project(block, normed, w, width):
    tok, feats = normed.shape
    tile = 256
    steps = width // tile
    return call(
        proj_body,
        "project",
        (steps,),
        1,
        [
            pl.BlockSpec((tok, feats), lambda i, b: (0, 0)),
            pl.BlockSpec((feats, tile), lambda i, b: (0, b[0] * steps + i)),
        ],
        pl.BlockSpec((tok, tile), lambda i, b: (0, i)),
        jax.ShapeDtypeStruct((tok, width), BF16),
        flops=2 * tok * feats * width,
        nbytes=2 * (tok * feats + feats * width + tok * width),
    )(block, normed, w)


def back_body(n, b_ref, *refs):
    acc = None
    for i in range(n):
        part = dot(refs[2 * i][...], refs[2 * i + 1][...], 1, 1)
        acc = part if acc is None else acc + part
    if len(refs) == 2 * n + 2:
        acc = acc + refs[2 * n][...]
    refs[-1][...] = acc


def back_project(blocks, grads, w, base=None):
    tok, width = grads[0].shape
    feats = w.shape[0]
    tile = 256
    n = len(grads)
    specs = []
    args = []
    for i in range(n):
        specs.append(pl.BlockSpec((tok, width), lambda f, b: (0, 0)))
        specs.append(pl.BlockSpec((tile, width), lambda f, b, i=i: (f, b[i])))
        args += [grads[i], w]
    if base is not None:
        specs.append(pl.BlockSpec((tok, tile), lambda f, b: (0, f)))
        args.append(base)
    return call(
        functools.partial(back_body, n),
        "back_project",
        (feats // tile,),
        1,
        specs,
        pl.BlockSpec((tok, tile), lambda f, b: (0, f)),
        jax.ShapeDtypeStruct((tok, feats), F32),
        flops=2 * n * tok * feats * width,
        nbytes=n * 2 * (tok * width + feats * width) + 8 * tok * feats,
    )(blocks, *args)


def att_grad_body(info_ref, lens_ref, b_ref, x_ref, w_ref, base_ref, att_ref, q_ref, ag_ref, send_ref, keep_ref):
    i = pl.program_id(0)
    half = pl.num_programs(0) // 2
    tok = x_ref.shape[0]
    ng2 = base_ref[...] + dot(x_ref[...], w_ref[...], 1, 1)
    keep = carry_in_of(info_ref, lens_ref, tok)
    states = []
    for j in range(2):
        at = slice(j * DH, (j + 1) * DH)
        ng, att = ng2[:, at], att_ref[:, at]
        inv = lax.rsqrt(jnp.mean(att * att, axis=-1, keepdims=True) + EPS)
        normed = att * inv
        proj = jnp.mean(ng * normed, axis=-1, keepdims=True)
        ag = ((ng - normed * proj) * inv).astype(BF16)
        ag_ref[:, at] = ag
        kept = jnp.where(keep, q_ref[:, at], jnp.zeros((), BF16))
        states.append(dot(kept, ag, 0, 0).astype(BF16))

    @pl.when(i < half)
    def _():
        send_ref[0] = states[0]
        send_ref[1] = states[1]

    @pl.when(i >= half)
    def _():
        keep_ref[0] = states[0]
        keep_ref[1] = states[1]


def attended_grads(info, lens, block, x, w, base, att, q):
    tok, wide = q.shape
    width = x.shape[1]
    pairs = wide // DH // 2
    half = pairs // 2

    def pair_of(i, info, lens, b):
        return lax.rem(i + half * (1 - info[I_HALF]), pairs)

    def cols(i, info, lens, b):
        return (0, pair_of(i, info, lens, b))

    two = pl.BlockSpec((tok, 2 * DH), cols)
    return call(
        att_grad_body,
        "attended_grads",
        (pairs,),
        3,
        [
            pl.BlockSpec((tok, width), lambda i, *_: (0, 0)),
            pl.BlockSpec((2 * DH, width), lambda i, info, lens, b: (pair_of(i, info, lens, b), b[0])),
            two,
            two,
            two,
        ],
        [
            two,
            pl.BlockSpec((2, DH, DH), lambda i, *_: (jnp.minimum(i, half - 1), 0, 0)),
            pl.BlockSpec((2, DH, DH), lambda i, *_: (jnp.maximum(i - half, 0), 0, 0)),
        ],
        [
            jax.ShapeDtypeStruct((tok, wide), BF16),
            jax.ShapeDtypeStruct((2 * half, DH, DH), BF16),
            jax.ShapeDtypeStruct((2 * half, DH, DH), BF16),
        ],
        flops=2 * tok * wide * width + 2 * tok * DH * wide,
        nbytes=2 * (tok * width + width * wide) + 12 * tok * wide,
    )(info, lens, block, x, w, base, att, q)


def grads_body(info_ref, lens_ref, q_ref, k_ref, v_ref, ag_ref, e_ref, qg_ref, kg_ref, vg_ref):
    tok = q_ref.shape[0]
    hb = tok // 2
    keep = carry_in_of(info_ref, lens_ref, tok)
    inter = jnp.where(keep, dot(ag_ref[...], e_ref[0], 1, 1), 0.0)
    for part in range(2):
        r0, n = part * hb, (part + 1) * hb
        mask = mask_of(info_ref, lens_ref, tok, r0, hb, n)
        q, ag = q_ref[r0:n, :], ag_ref[r0:n, :]
        s = jnp.where(mask, dot(q, k_ref[:n, :], 1, 1), 0.0).astype(BF16)
        g = jnp.where(mask, dot(ag, v_ref[:n, :], 1, 1), 0.0).astype(BF16)
        qg_ref[r0:n, :] = (dot(g, k_ref[:n, :], 1, 0) + inter[r0:n]).astype(BF16)
        kg, vg = dot(g, q, 0, 0), dot(s, ag, 0, 0)
        if part == 0:
            kg_ref[:n, :] = kg
            vg_ref[:n, :] = vg
        else:
            kg_ref[:hb, :] += kg[:hb]
            vg_ref[:hb, :] += vg[:hb]
            kg_ref[hb:, :] = kg[hb:]
            vg_ref[hb:, :] = vg[hb:]


def block_grads(info, lens, q, k, v, ag, entering):
    tok, wide = q.shape
    return call(
        grads_body,
        "block_grads",
        (wide // DH,),
        2,
        [col(tok)] * 4 + [state_spec()],
        [col(tok)] * 3,
        [
            jax.ShapeDtypeStruct((tok, wide), BF16),
            jax.ShapeDtypeStruct((tok, wide), F32),
            jax.ShapeDtypeStruct((tok, wide), F32),
        ],
        flops=8 * tok * tok * wide,
        nbytes=18 * tok * wide,
    )(info, lens, q, k, v, ag, entering)


def last_body(info_ref, lens_ref, k_ref, v_ref, l_ref, kp_ref, vp_ref, kg_ref, vg_ref):
    tok = k_ref.shape[0]
    keep = carry_out_of(info_ref, lens_ref, tok)
    kg = jnp.where(keep, dot(v_ref[...], l_ref[0], 1, 1), 0.0)
    vg = jnp.where(keep, dot(k_ref[...], l_ref[0], 1, 0), 0.0)
    kg_ref[...] = (kp_ref[...] + kg).astype(BF16)
    vg_ref[...] = (vp_ref[...] + vg).astype(BF16)


def last_grads(info, lens, k, v, leaving, kp, vp):
    tok, wide = k.shape
    return call(
        last_body,
        "last_grads",
        (wide // DH,),
        2,
        [col(tok), col(tok), state_spec(), col(tok), col(tok)],
        [col(tok)] * 2,
        [jax.ShapeDtypeStruct((tok, wide), BF16)] * 2,
        flops=4 * tok * DH * wide,
        nbytes=16 * tok * wide,
    )(info, lens, k, v, leaving, kp, vp)


def doc_start_scalars(lens):
    out, at = [], jnp.int32(0)
    for j in range(lens.shape[0] - 1):
        at = at + lens[j]
        out.append(at)
    return out


def exchange(send, keep, lens, tok, forward):
    n = lax.axis_size("ctx")
    me = lax.axis_index("ctx")
    starts = doc_start_scalars(lens)

    def same(a, b):
        pa, pb = a * tok + tok - 1, b * tok + tok - 1
        one = (a >= 0) | (b < 0)
        for s in starts:
            one = one & ~((pa < s) & (s <= pb))
        return one.astype(F32)

    swap = [(i, i ^ 1) for i in range(n)]
    core = me % 2
    first, second = me - core, me - core + 1
    is_second = (core == 1).astype(F32)
    is_first = 1.0 - is_second
    got = lax.ppermute(send, "ctx", swap).astype(F32)
    mine = keep.astype(F32)
    if forward:
        link = same(first, second)
        total = mine * (is_second + is_first * link) + got * (is_first + is_second * link)
    else:
        link = same(first - 1, first)
        total = mine * (is_first + is_second * link) + got * (is_second + is_first * link)
    total = total.astype(BF16)
    entering = None
    low, high = first, second
    m = 2
    while m < n:
        last = 2 * m >= n
        up = (me // m) % 2 == 1
        if last:
            pairs = [(i, i ^ m) for i in range(n) if ((i // m) % 2 == 0) == forward]
        else:
            pairs = [(i, i ^ m) for i in range(n)]
        other = lax.ppermute(total, "ctx", pairs).astype(F32)
        group_low = (me // (2 * m)) * 2 * m
        edge = group_low + m - 1
        if forward:
            weight = jnp.where(up, same(edge, first - 1), 0.0)
        else:
            weight = jnp.where(up, 0.0, same(second, edge))
        part = other * weight
        if not last:
            if forward:
                through = same(edge, group_low + 2 * m - 1)
                near = up
            else:
                through = same(group_low - 1, edge)
                near = jnp.logical_not(up)
            own_w = jnp.where(near, 1.0, through)
            other_w = jnp.where(near, through, 1.0)
            total = (total.astype(F32) * own_w + other * other_w).astype(BF16)
        entering = part if entering is None else entering + part
        m *= 2
    if entering is None:
        entering = jnp.zeros_like(mine)
    if forward:
        link = same(first - 1, first)
        near, far = is_first, is_second
    else:
        link = same(first, second)
        near, far = is_second, is_first
    chained = mine * near + got * far + link * entering
    own = entering * near + chained * far
    away = chained * near + entering * far
    own, away = own.astype(BF16), away.astype(BF16)
    back = lax.ppermute(away, "ctx", swap)
    return jnp.where(
        core == 0, jnp.concatenate([own, back], 0), jnp.concatenate([back, own], 0)
    )


def add(*parts):
    total = parts[0].astype(F32)
    for part in parts[1:]:
        total = total + part.astype(F32)
    return total.astype(BF16)


def shards(q, k, v, lens, w, grad):
    tok, width = grad.shape
    blk = lax.axis_index("ctx").astype(jnp.int32)
    z = lax.axis_index("head").astype(jnp.int32)
    info = jnp.stack([blk, blk % 2])

    def at(*blocks):
        return jnp.stack(blocks).astype(jnp.int32)

    up = [(0, 1), (1, 2), (2, 3)]
    down = [(1, 0), (2, 1), (3, 2)]
    u1 = lax.ppermute(grad, "head", up)
    d1 = lax.ppermute(grad, "head", down)
    send, keep = local_states(info, lens, k, v)
    entering = exchange(send, keep, lens, tok, True)
    intra_part = intra(info, lens, q, k, v)
    att, normed = normalise(info, lens, q, entering, intra_part)
    u2 = lax.ppermute(u1, "head", [(1, 2), (2, 3)])
    d2 = lax.ppermute(d1, "head", [(2, 1), (1, 0)])
    pa = project(at(jnp.where(z == 0, 3, 0)), normed, w, width)
    ra = lax.ppermute(pa, "head", [(0, 1), (3, 2)])
    p2 = project(at((z + 2) % 4), normed, w, width)
    p1 = project(at((z + 1) % 4), normed, w, width)
    p3 = project(at((z + 3) % 4), normed, w, width)
    p0 = project(at(z), normed, w, width)
    base = back_project(at(z, (z + 3) % 4, (z + 1) % 4), [grad, u1, d1], w)
    bo = lax.ppermute(p2, "head", [(0, 1), (3, 2)])
    x2 = u2 + d2
    x3 = lax.ppermute(x2, "head", [(2, 3), (1, 0)])
    bi = lax.ppermute(add(p2, ra), "head", [(1, 2), (2, 1)])
    base = back_project(at((z + 2) % 4), [x2], w, base)
    cu = lax.ppermute(add(p1, jnp.where(z == 1, bo, bi)), "head", up)
    cd = lax.ppermute(add(p3, jnp.where(z == 2, bo, bi)), "head", down)
    ag, gsend, gkeep = attended_grads(
        info, lens, at(jnp.where(z == 3, 0, 3)), x3, w, base, att, q
    )
    leaving = exchange(gsend, gkeep, lens, tok, False)
    query_grad, kp, vp = block_grads(info, lens, q, k, v, ag, entering)
    key_grad, value_grad = last_grads(info, lens, k, v, leaving, kp, vp)
    mixed = add(p0, cu, cd)
    return mixed, query_grad, key_grad, value_grad


def solution(mesh):
    return jax.shard_map(
        shards,
        mesh=mesh,
        in_specs=(
            P("ctx", "head"),
            P("ctx", "head"),
            P("ctx", "head"),
            P(),
            P("head", None),
            P("ctx", "head"),
        ),
        out_specs=(P("ctx", "head"), P("ctx", "head"), P("ctx", "head"), P("ctx", "head")),
        check_vma=False,
    )
```

time: 254 us -> 167 us (0.66)
  waiting for transfers between devices: 131 us -> 14.7 us
  Pallas kernels: 0 us -> 71.3 us
  matrix products: 48.5 us -> 0 us
  starting transfers between devices: 0.34 us -> 43.2 us
  blocking collectives: 15.3 us -> 0 us
  other arithmetic: 27.3 us -> 15.7 us
  local copies, waits for them, and re-layouts: 15.5 us -> 8.95 us
  between operations: 14.7 us -> 10.8 us
    all_gather x3 -> x0, waiting for transfers between devices: 84 us -> none  [the longest x1 73.4 us: shards(): lax.all_gather(out_grad, 'head', axis=1, tiled=True)]
    pallas_call x0 -> x13, Pallas kernels: none -> 71.3 us  [the longest x5 19 us: project(): call(proj_body, 'project', (steps,), 1, [pl.BlockSpec((tok, feats), lambd...]
    dot_general x15 -> x0, matrix products: 48.5 us -> none  [the longest x1 9.85 us: shards(): lax.dot_general(lax.all_gather(out_grad, 'head', axis=1, tiled=True), out...]
    reduce_scatter x1 -> x0, waiting for transfers between devices: 46.3 us -> none  [shards(): lax.psum_scatter(partial_out.astype(jnp.bfloat16), 'head', scatter_dimens...]
    ppermute x0 -> x18, starting transfers between devices: none -> 43.2 us  [the longest x4 8.56 us: exchange(): other = lax.ppermute(total, 'ctx', pairs).astype(F32)]
    select_n x8 -> x2, other arithmetic: 15.5 us -> 0.05 us  [exchange(): jnp.where(core == 0, jnp.concatenate([own, back], 0), jnp.concatenate([ba...]
    unnamed x1 -> x0, blocking collectives: 15.3 us -> none
    ppermute x0 -> x18, waiting for transfers between devices: none -> 14.7 us  [the longest x1 8.59 us: shards(): d2 = lax.ppermute(d1, 'head', [(2, 1), (1, 0)])]
  transfers between devices with their start and end apart: 4 -> 18, of which waited for: 4 -> 5; matrix products, arithmetic and copies ran while one was open for 28% -> 8% of each run, Pallas kernels for 0% -> 41%
where the time goes in v1:
time: 167 us; the launch traced here: 165 us
  Pallas kernels  71.3 us (43%)
  starting transfers between devices  43.2 us (26%)
  other arithmetic  15.7 us (9%)
  waiting for transfers between devices  14.7 us (9%)
  between operations  10.8 us (6%)
  local copies, waits for them, and re-layouts  8.95 us (5%)
    pallas_call x5, Pallas kernels, project(): call(proj_body, 'project', (steps,), 1, [pl.BlockSpec((tok, feats), lambd...  19 us
    pallas_call x2, Pallas kernels, back_project(): call(functools.partial(back_body, n), 'back_project', (feats // tile,), 1...  11.5 us
    pallas_call x1, Pallas kernels, block_grads(): call(grads_body, 'block_grads', (wide // DH,), 2, [col(tok)] * 4 + [state...  10.9 us
    ppermute x1, waiting for transfers between devices, shards(): d2 = lax.ppermute(d1, 'head', [(2, 1), (1, 0)])  8.59 us
    ppermute x4, starting transfers between devices, exchange(): other = lax.ppermute(total, 'ctx', pairs).astype(F32)  8.56 us
    ppermute x1, starting transfers between devices, shards(): cu = lax.ppermute(add(p1, jnp.where(z == 1, bo, bi)), 'head', up)  8.49 us
    ppermute x1, starting transfers between devices, shards(): ra = lax.ppermute(pa, 'head', [(0, 1), (3, 2)])  7.73 us
    unnamed x32, local copies, waits for them, and re-layouts  7.53 us
  transfers between devices with their start and end apart: 18, of which 5 were waited for; matrix products, arithmetic and copies ran while one was open for 8% of the time, Pallas kernels for 41%

profile of v1, /device:TPU:0, one launch (start us, length us, event | category | flops | bytes accessed | tf_op | source)
XLA Modules:
  0.0 164.7 jit_solution(14341757459013660204)
XLA Ops:
  3.9 3.9 %local_states.1 = (bf16[4,128,128]{2,1,0:T(8,128)(2,1)S(1)}, bf16[4,128,128]{2,1,0:T(8,128)(2,1)S(1)}) custom-call(s32[2]{0:T(128)S(1)} %pad_add_fusion.info_ref, s32[4]{0:T(128)S(1)} %copy-done.10, bf16[512,1024]{1,0:T(8,128)(2,1)S(1)} %copy-done.1, bf16[512,1024]{1,0:T(8,128)(2,1)S(1)} %copy-done.3), custom_call_target="tpu_custom_call" | custom-call | flops 134217728 | bytes 2097152 | tf_op jit(solution)/shard_map/local_states/pallas_call | solution.py:119
  8.3 5.5 %collective-permute-start.9 = (bf16[512,1024]{1,0:T(8,128)(2,1)}, bf16[512,1024]{1,0:T(8,128)(2,1)}, u32[]{:S(2)}, u32[]{:S(2)}) collective-permute-start(bf16[512,1024]{1,0:T(8,128)(2,1)} %refs_0_.1), channel_id=1, source_target_pairs={{0,1},{1,2},{2,3},{4,5},{5,6},{6,7},{8,9},{9,10},{10,11},{12,13},{... | collective-permute-start | bytes 3145736 | tf_op jit(solution)/shard_map/ppermute | solution.py:489
  22.7 2.9 %collective-permute-done.1 = bf16[4,128,128]{2,1,0:T(8,128)(2,1)} collective-permute-done((bf16[4,128,128]{2,1,0:T(8,128)(2,1)S(1)}, bf16[4,128,128]{2,1,0:T(8,128)(2,1)}, u32[]{:S(2)}, u32[]{:S(2)}) %collective-permute-start.1) | collective-permute-done | bytes 131104 | tf_op jit(solution)/shard_map/ppermute | solution.py:433
  27.2 4.1 %collective-permute-start.2 = (bf16[4,128,128]{2,1,0:T(8,128)(2,1)}, bf16[4,128,128]{2,1,0:T(8,128)(2,1)}, u32[]{:S(2)}, u32[]{:S(2)}) collective-permute-start(bf16[4,128,128]{2,1,0:T(8,128)(2,1)} %fusion.6), channel_id=1, source_target_pairs={{0,16},{4,20},{8,24},{12,28},{1,17},{5,21},{9,25},{13,29},{2,18},{... | collective-permute-start | bytes 393224 | tf_op jit(solution)/shard_map/ppermute | solution.py:433
  33.9 1.8 %add_convert_fusion.7 = (bf16[4,128,128]{2,1,0:T(8,128)(2,1)S(1)}, bf16[4,128,128]{2,1,0:T(8,128)(2,1)}) fusion(bf16[4,128,128]{2,1,0:T(8,128)(2,1)S(1)} %collective-permute-done, bf16[4,128,128]{2,1,0:T(8,128)(2,1)S(1)} %get-tuple-element.16, bf16[4,128,128]{2,1,0:T(8,128)(2,1)} %collective-permute-done.2, bf16[4,128,128]{2,1,0:T(8,128)(2,1)} %collective-permute-done.1, ...), kind=kLoop, calls=%fused_computation.35 | loop fusion | flops 1310720 | bytes 786452 | tf_op jit(solution)/shard_map/convert_element_type | solution.py:464
  35.7 6.0 %intra.1.a_ref = f32[512,1024]{1,0:T(8,128)S(1)} custom-call(s32[2]{0:T(128)S(1)} %pad_add_fusion.info_ref, s32[4]{0:T(128)S(1)} %copy-done.11, bf16[512,1024]{1,0:T(8,128)(2,1)S(1)} %copy-done, bf16[512,1024]{1,0:T(8,128)(2,1)S(1)} %copy-done.2, bf16[512,1024]{1,0:T(8,128)(2,1)S(1)} %copy-done.4), custom_call_target="tpu_custom_call" | custom-call | flops 805306368 | bytes 5242880 | tf_op jit(solution)/shard_map/intra/pallas_call | solution.py:155
  45.2 6.4 %normalise.1 = (f32[512,1024]{1,0:T(8,128)S(1)}, bf16[512,1024]{1,0:T(8,128)(2,1)S(1)}) custom-call(s32[2]{0:T(128)S(1)} %pad_add_fusion.info_ref, s32[4]{0:T(128)S(1)} %copy-done.11, bf16[512,1024]{1,0:T(8,128)(2,1)S(1)} %copy-done, bf16[8,128,128]{2,1,0:T(8,128)(2,1)S(1)} %maximum_select_fusion.e_ref, f32[512,1024]{1,0:T(8,128)} %copy-done.6), custom_call_target="tpu_custom_call" | custom-call | flops 134217728 | bytes 6291456 | tf_op jit(solution)/shard_map/normalise/pallas_call | solution.py:180
  53.0 4.4 %project.8 = bf16[512,1024]{1,0:T(8,128)(2,1)} custom-call(s32[1]{0:T(128)} %bitcast.8.b_ref, bf16[512,1024]{1,0:T(8,128)(2,1)S(1)} %get-tuple-element.18.n_ref, bf16[1024,4096]{1,0:T(8,128)(2,1)} %w_ref.11), custom_call_target="tpu_custom_call" | custom-call | flops 1073741824 | bytes 4194304 | tf_op jit(solution)/shard_map/project/pallas_call | solution.py:201
  57.4 7.7 %collective-permute-start.5 = (bf16[512,1024]{1,0:T(8,128)(2,1)}, bf16[512,1024]{1,0:T(8,128)(2,1)}, u32[]{:S(2)}, u32[]{:S(2)}) collective-permute-start(bf16[512,1024]{1,0:T(8,128)(2,1)} %project.8), channel_id=1, source_target_pairs={{0,1},{3,2},{4,5},{7,6},{8,9},{11,10},{12,13},{15,14},{16,17},{19,... | collective-permute-start | bytes 3145736 | tf_op jit(solution)/shard_map/ppermute | solution.py:498
  65.1 8.6 %collective-permute-done.12 = bf16[512,1024]{1,0:T(8,128)(2,1)S(1)} collective-permute-done((bf16[512,1024]{1,0:T(8,128)(2,1)}, bf16[512,1024]{1,0:T(8,128)(2,1)S(1)}, u32[]{:S(2)}, u32[]{:S(2)}) %collective-permute-start.12) | collective-permute-done | bytes 1048608 | tf_op jit(solution)/shard_map/ppermute | solution.py:496
  76.4 3.5 %project.7 = bf16[512,1024]{1,0:T(8,128)(2,1)S(1)} custom-call(s32[1]{0:T(128)} %bitcast.7.b_ref, bf16[512,1024]{1,0:T(8,128)(2,1)S(1)} %get-tuple-element.18.n_ref, bf16[1024,4096]{1,0:T(8,128)(2,1)} %w_ref.11), custom_call_target="tpu_custom_call" | custom-call | flops 1073741824 | bytes 4194304 | tf_op jit(solution)/shard_map/project/pallas_call | solution.py:201
  80.0 5.7 %collective-permute-start.4 = (bf16[512,1024]{1,0:T(8,128)(2,1)S(1)}, bf16[512,1024]{1,0:T(8,128)(2,1)S(1)}, u32[]{:S(2)}, u32[]{:S(2)}) collective-permute-start(bf16[512,1024]{1,0:T(8,128)(2,1)S(1)} %project.7), channel_id=1, source_target_pairs={{0,1},{3,2},{4,5},{7,6},{8,9},{11,10},{12,13},{15,14},{16,17},{19,... | collective-permute-start | bytes 3145736 | tf_op jit(solution)/shard_map/ppermute | solution.py:504
  85.7 2.3 %collective-permute-done.5 = bf16[512,1024]{1,0:T(8,128)(2,1)} collective-permute-done((bf16[512,1024]{1,0:T(8,128)(2,1)}, bf16[512,1024]{1,0:T(8,128)(2,1)}, u32[]{:S(2)}, u32[]{:S(2)}) %collective-permute-start.5) | collective-permute-done | bytes 1048608 | tf_op jit(solution)/shard_map/ppermute | solution.py:498
  90.3 7.4 %back_project.2.refs_2_ = f32[512,1024]{1,0:T(8,128)S(1)} custom-call(s32[3]{0:T(128)S(1)} %pad_add_fusion.1.b_ref, bf16[512,1024]{1,0:T(8,128)(2,1)S(1)} %copy-done.9, bf16[1024,4096]{1,0:T(8,128)(2,1)} %w_ref.11, bf16[512,1024]{1,0:T(8,128)(2,1)} %collective-permute-done.9.refs_2_, bf16[1024,4096]{1,0:T(8,128)(2,1)} %w_ref.11, ...), custom_call_target="tpu_custom_call" | custom-call | flops 3221225472 | bytes 13631488 | tf_op jit(solution)/shard_map/back_project/pallas_call | solution.py:241
  97.7 4.1 %back_project.3.base_ref = f32[512,1024]{1,0:T(8,128)S(1)} custom-call(s32[1]{0:T(128)} %bitcast.7.b_ref, bf16[512,1024]{1,0:T(8,128)(2,1)} %add.208.refs_0_, bf16[1024,4096]{1,0:T(8,128)(2,1)} %w_ref.11, f32[512,1024]{1,0:T(8,128)S(1)} %back_project.2.refs_2_), custom_call_target="tpu_custom_call" | custom-call | flops 1073741824 | bytes 7340032 | tf_op jit(solution)/shard_map/back_project/pallas_call | solution.py:241
  102.0 6.5 %attended_grads.1 = (bf16[512,1024]{1,0:T(8,128)(2,1)S(1)}, bf16[4,128,128]{2,1,0:T(8,128)(2,1)S(1)}, bf16[4,128,128]{2,1,0:T(8,128)(2,1)S(1)}) custom-call(s32[2]{0:T(128)S(1)} %pad_add_fusion.info_ref, s32[4]{0:T(128)S(1)} %copy-done.11, s32[1]{0:T(128)} %bitcast.10.b_ref, bf16[512,1024]{1,0:T(8,128)(2,1)} %collective-permute-done.13.x_ref, ...), custom_call_target="tpu_custom_call" | custom-call | flops 1207959552 | bytes 9437184 | tf_op jit(solution)/shard_map/attended_grads/pallas_call | solution.py:296
  108.6 3.8 %project.9 = bf16[512,1024]{1,0:T(8,128)(2,1)S(1)} custom-call(s32[1]{0:T(128)} %bitcast.9.b_ref, bf16[512,1024]{1,0:T(8,128)(2,1)S(1)} %get-tuple-element.18.n_ref, bf16[1024,4096]{1,0:T(8,128)(2,1)} %w_ref.11), custom_call_target="tpu_custom_call" | custom-call | flops 1073741824 | bytes 4194304 | tf_op jit(solution)/shard_map/project/pallas_call | solution.py:201
  112.5 3.5 %project.6 = bf16[512,1024]{1,0:T(8,128)(2,1)S(1)} custom-call(s32[1]{0:T(128)} %bitcast.6.b_ref, bf16[512,1024]{1,0:T(8,128)(2,1)S(1)} %get-tuple-element.18.n_ref, bf16[1024,4096]{1,0:T(8,128)(2,1)} %w_ref.11), custom_call_target="tpu_custom_call" | custom-call | flops 1073741824 | bytes 4194304 | tf_op jit(solution)/shard_map/project/pallas_call | solution.py:201
  118.2 2.4 %add_convert_fusion.2 = (bf16[512,1024]{1,0:T(8,128)(2,1)}, bf16[512,1024]{1,0:T(8,128)(2,1)}) fusion(bf16[512,1024]{1,0:T(8,128)(2,1)S(1)} %project.6, bf16[512,1024]{1,0:T(8,128)(2,1)S(1)} %collective-permute-done.4, bf16[512,1024]{1,0:T(8,128)(2,1)S(1)} %collective-permute-done.6, pred[]{:T(512)S(6)} %eq.46, pred[]{:T(512)S(6)} %eq.48, ...), kind=kLoop, calls=%fused_computation.2 | loop fusion | flops 5242880 | bytes 6291458 | tf_op jit(solution)/shard_map/convert_element_type | solution.py:475
  120.6 8.5 %collective-permute-start.7 = (bf16[512,1024]{1,0:T(8,128)(2,1)}, bf16[512,1024]{1,0:T(8,128)(2,1)}, u32[]{:S(2)}, u32[]{:S(2)}) collective-permute-start(bf16[512,1024]{1,0:T(8,128)(2,1)} %get-tuple-element.28), channel_id=1, source_target_pairs={{0,1},{1,2},{2,3},{4,5},{5,6},{6,7},{8,9},{9,10},{10,11},{12,13},{... | collective-permute-start | bytes 3145736 | tf_op jit(solution)/shard_map/ppermute | solution.py:509
  136.2 3.7 %project.5 = bf16[512,1024]{1,0:T(8,128)(2,1)S(1)} custom-call(s32[1]{0:T(128)} %bitcast.b_ref, bf16[512,1024]{1,0:T(8,128)(2,1)S(1)} %get-tuple-element.18.n_ref, bf16[1024,4096]{1,0:T(8,128)(2,1)} %w_ref.11), custom_call_target="tpu_custom_call" | custom-call | flops 1073741824 | bytes 4194304 | tf_op jit(solution)/shard_map/project/pallas_call | solution.py:201
  141.8 10.9 %block_grads.1 = (bf16[512,1024]{1,0:T(8,128)(2,1)}, f32[512,1024]{1,0:T(8,128)}, f32[512,1024]{1,0:T(8,128)}) custom-call(s32[2]{0:T(128)S(1)} %pad_add_fusion.info_ref, s32[4]{0:T(128)S(1)} %copy-done.11, bf16[512,1024]{1,0:T(8,128)(2,1)S(1)} %copy-done, bf16[512,1024]{1,0:T(8,128)(2,1)S(1)} %copy-done.2, bf16[512,1024]{1,0:T(8,128)(2,1)S(1)} %copy-done.5, ...), custom_call_target="tpu_custom_call" | custom-call | flops 2147483648 | bytes 9437184 | tf_op jit(solution)/shard_map/block_grads/pallas_call | solution.py:348
  154.4 7.2 %last_grads.1 = (bf16[512,1024]{1,0:T(8,128)(2,1)}, bf16[512,1024]{1,0:T(8,128)(2,1)}) custom-call(s32[2]{0:T(128)S(1)} %pad_add_fusion.info_ref, s32[4]{0:T(128)S(1)} %copy-done.11, bf16[512,1024]{1,0:T(8,128)(2,1)S(1)} %copy-done.2, bf16[512,1024]{1,0:T(8,128)(2,1)S(1)} %copy-done.5, bf16[8,128,128]{2,1,0:T(8,128)(2,1)S(1)} %maximum_select_fusion.1.l_ref, ...), custom_call_target="tpu_custom_call" | custom-call | flops 268435456 | bytes 8388608 | tf_op jit(solution)/shard_map/last_grads/pallas_call | solution.py:376
  161.6 3.1 %add_convert_fusion = bf16[512,1024]{1,0:T(8,128)(2,1)} fusion(bf16[512,1024]{1,0:T(8,128)(2,1)} %collective-permute-done.8, bf16[512,1024]{1,0:T(8,128)(2,1)} %collective-permute-done.7, bf16[512,1024]{1,0:T(8,128)(2,1)S(1)} %project.5), kind=kLoop, calls=%fused_computation | loop fusion | flops 3145728 | bytes 4194304 | tf_op jit(solution)/shard_map/convert_element_type | solution.py:475
  (72 shorter events, 30.0 us)
Async XLA Ops:
  0.6 35.1 %copy-start = (bf16[512,1024]{1,0:T(8,128)(2,1)S(1)}, bf16[512,1024]{1,0:T(8,128)(2,1)}, u32[]{:S(2)}) copy-start(bf16[512,1024]{1,0:T(8,128)(2,1)} %q_ref.7) | copy-start | bytes 3145732
  3.9 31.8 %copy-start.2 = (bf16[512,1024]{1,0:T(8,128)(2,1)S(1)}, bf16[512,1024]{1,0:T(8,128)(2,1)}, u32[]{:S(2)}) copy-start(bf16[512,1024]{1,0:T(8,128)(2,1)} %k_ref.7) | copy-start | bytes 3145732
  3.9 31.8 %copy-start.4 = (bf16[512,1024]{1,0:T(8,128)(2,1)S(1)}, bf16[512,1024]{1,0:T(8,128)(2,1)}, u32[]{:S(2)}) copy-start(bf16[512,1024]{1,0:T(8,128)(2,1)} %v_ref.7) | copy-start | bytes 3145732
  3.9 31.8 %copy-start.11 = (s32[4]{0:T(128)S(1)}, s32[4]{0:T(128)}, u32[]{:S(2)}) copy-start(s32[4]{0:T(128)} %lens_ref.11) | copy-start | bytes 52
  7.8 12.0 %collective-permute-start = (bf16[4,128,128]{2,1,0:T(8,128)(2,1)S(1)}, bf16[4,128,128]{2,1,0:T(8,128)(2,1)S(1)}, u32[]{:S(2)}, u32[]{:S(2)}) collective-permute-start(bf16[4,128,128]{2,1,0:T(8,128)(2,1)S(1)} %get-tuple-element.17), channel_id=1, source_target_pairs={{0,4},{4,0},{8,12},{12,8},{16,20},{20,16},{24,28},{28,24},{1,5},{5... | collective-permute-start | bytes 393224 | tf_op jit(solution)/shard_map/ppermute | solution.py:414
  8.3 34.8 %collective-permute-start.9 = (bf16[512,1024]{1,0:T(8,128)(2,1)}, bf16[512,1024]{1,0:T(8,128)(2,1)}, u32[]{:S(2)}, u32[]{:S(2)}) collective-permute-start(bf16[512,1024]{1,0:T(8,128)(2,1)} %refs_0_.1), channel_id=1, source_target_pairs={{0,1},{1,2},{2,3},{4,5},{5,6},{6,7},{8,9},{9,10},{10,11},{12,13},{... | collective-permute-start | bytes 3145736 | tf_op jit(solution)/shard_map/ppermute | solution.py:489
  13.8 30.0 %collective-permute-start.11 = (bf16[512,1024]{1,0:T(8,128)(2,1)}, bf16[512,1024]{1,0:T(8,128)(2,1)}, u32[]{:S(2)}, u32[]{:S(2)}) collective-permute-start(bf16[512,1024]{1,0:T(8,128)(2,1)} %refs_0_.1), channel_id=1, source_target_pairs={{1,0},{2,1},{3,2},{5,4},{6,5},{7,6},{9,8},{10,9},{11,10},{13,12},{... | collective-permute-start | bytes 3145736 | tf_op jit(solution)/shard_map/ppermute | solution.py:490
  19.8 5.8 %collective-permute-start.1 = (bf16[4,128,128]{2,1,0:T(8,128)(2,1)S(1)}, bf16[4,128,128]{2,1,0:T(8,128)(2,1)}, u32[]{:S(2)}, u32[]{:S(2)}) collective-permute-start(bf16[4,128,128]{2,1,0:T(8,128)(2,1)S(1)} %fusion.1), channel_id=1, source_target_pairs={{0,8},{4,12},{8,0},{12,4},{16,24},{20,28},{24,16},{28,20},{1,9},{5... | collective-permute-start | bytes 393224 | tf_op jit(solution)/shard_map/ppermute | solution.py:433
  27.2 6.7 %collective-permute-start.2 = (bf16[4,128,128]{2,1,0:T(8,128)(2,1)}, bf16[4,128,128]{2,1,0:T(8,128)(2,1)}, u32[]{:S(2)}, u32[]{:S(2)}) collective-permute-start(bf16[4,128,128]{2,1,0:T(8,128)(2,1)} %fusion.6), channel_id=1, source_target_pairs={{0,16},{4,20},{8,24},{12,28},{1,17},{5,21},{9,25},{13,29},{2,18},{... | collective-permute-start | bytes 393224 | tf_op jit(solution)/shard_map/ppermute | solution.py:433
  35.7 9.5 %collective-permute-start.3 = (bf16[4,128,128]{2,1,0:T(8,128)(2,1)}, bf16[4,128,128]{2,1,0:T(8,128)(2,1)S(1)}, u32[]{:S(2)}, u32[]{:S(2)}) collective-permute-start(bf16[4,128,128]{2,1,0:T(8,128)(2,1)} %get-tuple-element.33), channel_id=1, source_target_pairs={{0,4},{4,0},{8,12},{12,8},{16,20},{20,16},{24,28},{28,24},{1,5},{5... | collective-permute-start | bytes 393224 | tf_op jit(solution)/shard_map/ppermute | solution.py:465
  43.1 22.0 %collective-permute-start.10 = (bf16[512,1024]{1,0:T(8,128)(2,1)}, bf16[512,1024]{1,0:T(8,128)(2,1)S(1)}, u32[]{:S(2)}, u32[]{:S(2)}) collective-permute-start(bf16[512,1024]{1,0:T(8,128)(2,1)} %collective-permute-done.9.refs_2_), channel_id=1, source_target_pairs={{1,2},{2,3},{5,6},{6,7},{9,10},{10,11},{13,14},{14,15},{17,18},{18... | collective-permute-start | bytes 3145736 | tf_op jit(solution)/shard_map/ppermute | solution.py:495
  43.8 29.9 %collective-permute-start.12 = (bf16[512,1024]{1,0:T(8,128)(2,1)}, bf16[512,1024]{1,0:T(8,128)(2,1)S(1)}, u32[]{:S(2)}, u32[]{:S(2)}) collective-permute-start(bf16[512,1024]{1,0:T(8,128)(2,1)} %collective-permute-done.11.refs_4_), channel_id=1, source_target_pairs={{2,1},{1,0},{6,5},{5,4},{10,9},{9,8},{14,13},{13,12},{18,17},{17,1... | collective-permute-start | bytes 3145736 | tf_op jit(solution)/shard_map/ppermute | solution.py:496
  57.4 30.5 %collective-permute-start.5 = (bf16[512,1024]{1,0:T(8,128)(2,1)}, bf16[512,1024]{1,0:T(8,128)(2,1)}, u32[]{:S(2)}, u32[]{:S(2)}) collective-permute-start(bf16[512,1024]{1,0:T(8,128)(2,1)} %project.8), channel_id=1, source_target_pairs={{0,1},{3,2},{4,5},{7,6},{8,9},{11,10},{12,13},{15,14},{16,17},{19,... | collective-permute-start | bytes 3145736 | tf_op jit(solution)/shard_map/ppermute | solution.py:498
  75.1 27.0 %collective-permute-start.13 = (bf16[512,1024]{1,0:T(8,128)(2,1)}, bf16[512,1024]{1,0:T(8,128)(2,1)}, u32[]{:S(2)}, u32[]{:S(2)}) collective-permute-start(bf16[512,1024]{1,0:T(8,128)(2,1)} %add.208.refs_0_), channel_id=1, source_target_pairs={{2,3},{1,0},{6,7},{5,4},{10,11},{9,8},{14,15},{13,12},{18,19},{17,... | collective-permute-start | bytes 3145736 | tf_op jit(solution)/shard_map/ppermute | solution.py:506
  79.9 10.4 %copy-start.9 = (bf16[512,1024]{1,0:T(8,128)(2,1)S(1)}, bf16[512,1024]{1,0:T(8,128)(2,1)}, u32[]{:S(2)}) copy-start(bf16[512,1024]{1,0:T(8,128)(2,1)} %refs_0_.1) | copy-start | bytes 3145732
  80.0 38.3 %collective-permute-start.4 = (bf16[512,1024]{1,0:T(8,128)(2,1)S(1)}, bf16[512,1024]{1,0:T(8,128)(2,1)S(1)}, u32[]{:S(2)}, u32[]{:S(2)}) collective-permute-start(bf16[512,1024]{1,0:T(8,128)(2,1)S(1)} %project.7), channel_id=1, source_target_pairs={{0,1},{3,2},{4,5},{7,6},{8,9},{11,10},{12,13},{15,14},{16,17},{19,... | collective-permute-start | bytes 3145736 | tf_op jit(solution)/shard_map/ppermute | solution.py:504
  89.5 28.7 %collective-permute-start.6 = (bf16[512,1024]{1,0:T(8,128)(2,1)S(1)}, bf16[512,1024]{1,0:T(8,128)(2,1)S(1)}, u32[]{:S(2)}, u32[]{:S(2)}) collective-permute-start(bf16[512,1024]{1,0:T(8,128)(2,1)S(1)} %add_convert_fusion.3), channel_id=1, source_target_pairs={{1,2},{2,1},{5,6},{6,5},{9,10},{10,9},{13,14},{14,13},{17,18},{18,... | collective-permute-start | bytes 3145736 | tf_op jit(solution)/shard_map/ppermute | solution.py:507
  108.5 7.5 %collective-permute-start.14 = (bf16[4,128,128]{2,1,0:T(8,128)(2,1)S(1)}, bf16[4,128,128]{2,1,0:T(8,128)(2,1)S(1)}, u32[]{:S(2)}, u32[]{:S(2)}) collective-permute-start(bf16[4,128,128]{2,1,0:T(8,128)(2,1)S(1)} %get-tuple-element.23), channel_id=1, source_target_pairs={{0,4},{4,0},{8,12},{12,8},{16,20},{20,16},{24,28},{28,24},{1,5},{5... | collective-permute-start | bytes 393224 | tf_op jit(solution)/shard_map/ppermute | solution.py:414
  116.7 14.9 %collective-permute-start.15 = (bf16[4,128,128]{2,1,0:T(8,128)(2,1)}, bf16[4,128,128]{2,1,0:T(8,128)(2,1)}, u32[]{:S(2)}, u32[]{:S(2)}) collective-permute-start(bf16[4,128,128]{2,1,0:T(8,128)(2,1)} %fusion.8), channel_id=1, source_target_pairs={{0,8},{4,12},{8,0},{12,4},{16,24},{20,28},{24,16},{28,20},{1,9},{5... | collective-permute-start | bytes 393224 | tf_op jit(solution)/shard_map/ppermute | solution.py:433
  120.6 41.0 %collective-permute-start.7 = (bf16[512,1024]{1,0:T(8,128)(2,1)}, bf16[512,1024]{1,0:T(8,128)(2,1)}, u32[]{:S(2)}, u32[]{:S(2)}) collective-permute-start(bf16[512,1024]{1,0:T(8,128)(2,1)} %get-tuple-element.28), channel_id=1, source_target_pairs={{0,1},{1,2},{2,3},{4,5},{5,6},{6,7},{8,9},{9,10},{10,11},{12,13},{... | collective-permute-start | bytes 3145736 | tf_op jit(solution)/shard_map/ppermute | solution.py:509
  129.1 32.5 %collective-permute-start.8 = (bf16[512,1024]{1,0:T(8,128)(2,1)}, bf16[512,1024]{1,0:T(8,128)(2,1)}, u32[]{:S(2)}, u32[]{:S(2)}) collective-permute-start(bf16[512,1024]{1,0:T(8,128)(2,1)} %get-tuple-element.29), channel_id=1, source_target_pairs={{1,0},{2,1},{3,2},{5,4},{6,5},{7,6},{9,8},{10,9},{11,10},{13,12},{... | collective-permute-start | bytes 3145736 | tf_op jit(solution)/shard_map/ppermute | solution.py:510
  133.4 7.2 %collective-permute-start.16 = (bf16[4,128,128]{2,1,0:T(8,128)(2,1)}, bf16[4,128,128]{2,1,0:T(8,128)(2,1)}, u32[]{:S(2)}, u32[]{:S(2)}) collective-permute-start(bf16[4,128,128]{2,1,0:T(8,128)(2,1)} %fusion.13), channel_id=1, source_target_pairs={{16,0},{20,4},{24,8},{28,12},{17,1},{21,5},{25,9},{29,13},{18,2},{... | collective-permute-start | bytes 393224 | tf_op jit(solution)/shard_map/ppermute | solution.py:433
  136.2 5.6 %copy-start.5 = (bf16[512,1024]{1,0:T(8,128)(2,1)S(1)}, bf16[512,1024]{1,0:T(8,128)(2,1)}, u32[]{:S(2)}) copy-start(bf16[512,1024]{1,0:T(8,128)(2,1)} %v_ref.7) | copy-start | bytes 3145732
  141.7 11.0 %collective-permute-start.17 = (bf16[4,128,128]{2,1,0:T(8,128)(2,1)S(1)}, bf16[4,128,128]{2,1,0:T(8,128)(2,1)S(1)}, u32[]{:S(2)}, u32[]{:S(2)}) collective-permute-start(bf16[4,128,128]{2,1,0:T(8,128)(2,1)S(1)} %get-tuple-element.31), channel_id=1, source_target_pairs={{0,4},{4,0},{8,12},{12,8},{16,20},{20,16},{24,28},{28,24},{1,5},{5... | collective-permute-start | bytes 393224 | tf_op jit(solution)/shard_map/ppermute | solution.py:465
  (10 other events, 26.1 us)

commit v2 on v0

v2 whole, which is shorter than its diff:
```python
import functools

import jax
import jax.numpy as jnp
from jax import lax
from jax.experimental import pallas as pl
from jax.experimental.pallas import tpu as pltpu
from jax.sharding import PartitionSpec as P

DH = 128
EPS = 1e-06
F32 = jnp.float32
BF16 = jnp.bfloat16
MIB = 1024 * 1024

I_BLK, I_CORE, I_Z = 0, 1, 2


def kernel(body, name, info, lens, ins, outs, deps=(), spare=8, scratch=()):
    n_in, n_dep = len(ins), len(deps)

    def inner(info_ref, lens_ref, *refs):
        body(info_ref, lens_ref, *refs[:n_in], *refs[n_in + n_dep:])

    size = sum(a.size * a.dtype.itemsize for a in list(ins) + list(outs))
    smem = pl.BlockSpec(memory_space=pltpu.SMEM)
    vmem = pl.BlockSpec(memory_space=pltpu.VMEM)
    hbm = pl.BlockSpec(memory_space=pl.ANY)
    return pl.pallas_call(
        inner,
        name=name,
        in_specs=[smem, smem] + [vmem] * n_in + [hbm] * n_dep,
        out_specs=[vmem] * len(outs),
        out_shape=list(outs),
        scratch_shapes=list(scratch),
        compiler_params=pltpu.CompilerParams(vmem_limit_bytes=size + spare * MIB),
    )(info, lens, *ins, *deps)


def like(shape, dtype):
    return jax.ShapeDtypeStruct(shape, dtype)


def dot(a, b, ca, cb):
    return lax.dot_general(a, b, (((ca,), (cb,)), ((), ())), preferred_element_type=F32)


def head(h):
    return slice(h * DH, (h + 1) * DH)


def starts_of(lens_ref):
    out, at = [], jnp.int32(0)
    for j in range(lens_ref.shape[0] - 1):
        at = at + lens_ref[j]
        out.append(at)
    return out


def start_at(starts, p):
    best = jnp.minimum(p, 0)
    best = jnp.maximum(best, -1)
    for s in starts:
        best = jnp.where(p >= s, s, best)
    return best


def line(tok, axis):
    return lax.broadcasted_iota(jnp.int32, (tok, 1) if axis == 0 else (1, tok), axis)


def carries_in(info_ref, lens_ref, tok):
    first = info_ref[I_BLK] * tok
    starts = starts_of(lens_ref)
    return start_at(starts, line(tok, 0) + first) == start_at(starts, first - 1)


def carries_out(info_ref, lens_ref, tok):
    first = info_ref[I_BLK] * tok
    starts = starts_of(lens_ref)
    return start_at(starts, line(tok, 0) + first) == start_at(starts, first + tok - 1)


def visible(info_ref, lens_ref, tok, axis):
    first = info_ref[I_BLK] * tok
    t, s = line(tok, axis), line(tok, 1 - axis)
    low = start_at(starts_of(lens_ref), t + first) - first
    return (s <= t) & (s >= low)


def same(starts, tok, a, b):
    pa, pb = a * tok + tok - 1, b * tok + tok - 1
    one = (a >= 0) | (b < 0)
    for s in starts:
        one = jnp.logical_and(one, jnp.logical_not(jnp.logical_and(pa < s, s <= pb)))
    return jnp.where(one, 1.0, 0.0).astype(F32)


def states_body(half, info_ref, lens_ref, k_ref, v_ref, send_ref, keep_ref):
    keep = carries_out(info_ref, lens_ref, k_ref.shape[0])
    zero = jnp.zeros((), BF16)
    core = info_ref[I_CORE]
    states = []
    for h in range(2 * half):
        kept = jnp.where(keep, k_ref[:, head(h)], zero)
        states.append(dot(kept, v_ref[:, head(h)], 0, 0).astype(BF16))
    for i in range(half):
        keep_ref[i] = jnp.where(core == 0, states[i], states[i + half])
        send_ref[i] = jnp.where(core == 0, states[i + half], states[i])


def intra_body(info_ref, lens_ref, q_ref, k_ref, v_ref, out_ref):
    tok, wide = q_ref.shape
    mask = visible(info_ref, lens_ref, tok, 0)
    for h in range(wide // DH):
        s = dot(q_ref[:, head(h)], k_ref[:, head(h)], 1, 1)
        s = jnp.where(mask, s, 0.0).astype(BF16)
        out_ref[:, head(h)] = dot(s, v_ref[:, head(h)], 1, 0)


def pick(info_ref, own_ref, back_ref, h):
    half = own_ref.shape[0]
    return jnp.where(info_ref[I_CORE] == h // half, own_ref[h % half], back_ref[h % half])


def norm_body(info_ref, lens_ref, q_ref, own_ref, back_ref, a_ref, att_ref, n_ref):
    tok, wide = q_ref.shape
    keep = carries_in(info_ref, lens_ref, tok)
    for h in range(wide // DH):
        inter = dot(q_ref[:, head(h)], pick(info_ref, own_ref, back_ref, h), 1, 0)
        att = a_ref[:, head(h)] + jnp.where(keep, inter, 0.0)
        att_ref[:, head(h)] = att
        inv = lax.rsqrt(jnp.mean(att * att, axis=-1, keepdims=True) + EPS)
        n_ref[:, head(h)] = (att * inv).astype(BF16)


TILE = 256


def project_body(blocks, info_ref, lens_ref, n_ref, w_ref, *out_refs):
    tok, width = out_refs[0].shape
    for block, out_ref in zip(blocks, out_refs, strict=True):
        base = block(info_ref[I_Z]) * width
        for i in range(width // TILE):
            at = pl.multiple_of(base + i * TILE, TILE)
            out_ref[:, i * TILE:(i + 1) * TILE] = dot(
                n_ref[...], w_ref[:, pl.ds(at, TILE)], 1, 0
            ).astype(BF16)


def back_body(blocks, based, info_ref, lens_ref, w_ref, *refs):
    out_ref = refs[-1]
    feats = out_ref.shape[1]
    for i in range(feats // TILE):
        rows = slice(i * TILE, (i + 1) * TILE)
        acc = refs[-2][:, rows] if based else None
        for block, g_ref in zip(blocks, refs, strict=False):
            width = g_ref.shape[1]
            at = pl.multiple_of(block(info_ref[I_Z]) * width, TILE)
            part = dot(g_ref[...], w_ref[rows, pl.ds(at, width)], 1, 1)
            acc = part if acc is None else acc + part
        out_ref[:, rows] = acc


def att_grad_body(block, info_ref, lens_ref, w_ref, x_ref, base_ref, att_ref, q_ref, ag_ref, send_ref, keep_ref):
    tok, wide = q_ref.shape
    width = x_ref.shape[1]
    keep = carries_in(info_ref, lens_ref, tok)
    core = info_ref[I_CORE]
    zero = jnp.zeros((), BF16)
    at = pl.multiple_of(block(info_ref[I_Z]) * width, TILE)
    states = []
    for i in range(wide // TILE):
        rows = slice(i * TILE, (i + 1) * TILE)
        ng2 = base_ref[:, rows] + dot(x_ref[...], w_ref[rows, pl.ds(at, width)], 1, 1)
        for j in range(TILE // DH):
            h = i * (TILE // DH) + j
            ng, att = ng2[:, head(j)], att_ref[:, head(h)]
            inv = lax.rsqrt(jnp.mean(att * att, axis=-1, keepdims=True) + EPS)
            normed = att * inv
            proj = jnp.mean(ng * normed, axis=-1, keepdims=True)
            ag = ((ng - normed * proj) * inv).astype(BF16)
            ag_ref[:, head(h)] = ag
            kept = jnp.where(keep, q_ref[:, head(h)], zero)
            states.append(dot(kept, ag, 0, 0).astype(BF16))
    half = len(states) // 2
    for i in range(half):
        keep_ref[i] = jnp.where(core == 0, states[i], states[i + half])
        send_ref[i] = jnp.where(core == 0, states[i + half], states[i])


def grads_body(info_ref, lens_ref, q_ref, k_ref, v_ref, ag_ref, own_ref, back_ref, qg_ref, kg_ref, vg_ref):
    tok, wide = q_ref.shape
    keep = carries_in(info_ref, lens_ref, tok)
    mask = visible(info_ref, lens_ref, tok, 0)
    mask_t = visible(info_ref, lens_ref, tok, 1)
    for h in range(wide // DH):
        q, k, v, ag = (r[:, head(h)] for r in (q_ref, k_ref, v_ref, ag_ref))
        inter = dot(ag, pick(info_ref, own_ref, back_ref, h), 1, 1)
        st = jnp.where(mask_t, dot(k, q, 1, 1), 0.0).astype(BF16)
        vg_ref[:, head(h)] = dot(st, ag, 1, 0)
        g = jnp.where(mask, dot(ag, v, 1, 1), 0.0).astype(BF16)
        qg_ref[:, head(h)] = (dot(g, k, 1, 0) + jnp.where(keep, inter, 0.0)).astype(BF16)
        kg_ref[:, head(h)] = dot(g, q, 0, 0)


def last_body(info_ref, lens_ref, k_ref, v_ref, own_ref, back_ref, kp_ref, vp_ref, kg_ref, vg_ref):
    tok, wide = k_ref.shape
    keep = carries_out(info_ref, lens_ref, tok)
    for h in range(wide // DH):
        leaving = pick(info_ref, own_ref, back_ref, h)
        kg = jnp.where(keep, dot(v_ref[:, head(h)], leaving, 1, 1), 0.0)
        vg = jnp.where(keep, dot(k_ref[:, head(h)], leaving, 1, 0), 0.0)
        kg_ref[:, head(h)] = (kp_ref[:, head(h)] + kg).astype(BF16)
        vg_ref[:, head(h)] = (vp_ref[:, head(h)] + vg).astype(BF16)


def sum_body(info_ref, lens_ref, *refs):
    total = refs[0][...].astype(F32)
    for r in refs[1:-1]:
        total = total + r[...].astype(F32)
    refs[-1][...] = total.astype(BF16)


def fold_body(info_ref, lens_ref, p1_ref, p3_ref, bo_ref, bi_ref, up_ref, down_ref):
    z = info_ref[I_Z]
    bo, bi = bo_ref[...], bi_ref[...]
    up_ref[...] = (p1_ref[...].astype(F32) + jnp.where(z == 1, bo, bi).astype(F32)).astype(BF16)
    down_ref[...] = (p3_ref[...].astype(F32) + jnp.where(z == 2, bo, bi).astype(F32)).astype(BF16)


def pair_body(forward, tok, info_ref, lens_ref, mine_ref, got_ref, total_ref):
    starts = starts_of(lens_ref)
    blk, core = info_ref[I_BLK], info_ref[I_CORE]
    first = blk - core
    if forward:
        far, link = core == 0, same(starts, tok, first, first + 1)
    else:
        far, link = core == 1, same(starts, tok, first - 1, first)
    a, b = jnp.where(far, link, 1.0), jnp.where(far, 1.0, link)
    total_ref[...] = (mine_ref[...].astype(F32) * a + got_ref[...].astype(F32) * b).astype(BF16)


def step_body(forward, tok, m, last, begun, info_ref, lens_ref, *refs):
    starts = starts_of(lens_ref)
    blk, core = info_ref[I_BLK], info_ref[I_CORE]
    first = blk - core
    second = first + 1
    up = lax.rem(blk // m, 2) == 1
    low = blk // (2 * m) * (2 * m)
    edge = low + m - 1
    refs = list(refs)
    other = refs.pop(0)[...].astype(F32)
    if forward:
        entering = other * jnp.where(up, same(starts, tok, edge, first - 1), 0.0)
    else:
        entering = other * jnp.where(up, 0.0, same(starts, tok, second, edge))
    if begun:
        entering = entering + refs.pop(0)[...]
    if not last:
        total_ref, new_total_ref, entering_ref = refs
        entering_ref[...] = entering
        if forward:
            near, through = up, same(starts, tok, edge, low + 2 * m - 1)
        else:
            near, through = jnp.logical_not(up), same(starts, tok, low - 1, edge)
        a, b = jnp.where(near, 1.0, through), jnp.where(near, through, 1.0)
        new_total_ref[...] = (total_ref[...].astype(F32) * a + other * b).astype(BF16)
        return
    mine_ref, got_ref, own_ref, away_ref = refs
    if forward:
        near, link = core == 0, same(starts, tok, first - 1, first)
    else:
        near, link = core == 1, same(starts, tok, first, second)
    nearer = jnp.where(near, mine_ref[...], got_ref[...]).astype(F32)
    chained = nearer + link * entering
    own_ref[...] = jnp.where(near, entering, chained).astype(BF16)
    away_ref[...] = jnp.where(near, chained, entering).astype(BF16)


def exchange(send, keep, info, lens, tok, forward, deps):
    n = lax.axis_size("ctx")
    swap = [(i, i ^ 1) for i in range(n)]
    half = like(keep.shape, BF16)
    deps = list(deps)
    got = lax.ppermute(send, "ctx", swap)
    (total,) = kernel(
        functools.partial(pair_body, forward, tok), "pair_total", info, lens, [keep, got], [half],
        deps.pop(0) if deps else (),
    )
    entering, m = [], 2
    while m < n:
        last = 2 * m >= n
        pairs = [(i, i ^ m) for i in range(n) if not last or ((i // m) % 2 == 0) == forward]
        other = lax.ppermute(total, "ctx", pairs)
        body = functools.partial(step_body, forward, tok, m, last, bool(entering))
        more = deps.pop(0) if deps else ()
        if last:
            own, away = kernel(
                body, "exchange_last", info, lens, [other, *entering, keep, got], [half, half], more
            )
        else:
            total, e = kernel(
                body, "exchange_step", info, lens, [other, *entering, total],
                [half, like(keep.shape, F32)], more,
            )
            entering = [e]
        m *= 2
    return own, lax.ppermute(away, "ctx", swap)


def shards(q, k, v, lens, w, grad):
    tok, width = grad.shape
    feats = w.shape[0]
    heads = feats // DH
    half = heads // 2
    blk = lax.axis_index("ctx").astype(jnp.int32)
    z = lax.axis_index("head").astype(jnp.int32)
    info = jnp.stack([blk, blk % 2, z])
    run = lambda body, name, ins, outs, deps=(), spare=8: kernel(
        body, name, info, lens, ins, outs, deps, spare
    )
    part = like((tok, width), BF16)
    wide_b, wide_f = like((tok, feats), BF16), like((tok, feats), F32)
    state = like((half, DH, DH), BF16)

    def project(blocks, name, deps=()):
        return run(functools.partial(project_body, blocks), name, [normed, w], [part] * len(blocks), deps)

    def back_project(blocks, name, grads, base=None, deps=()):
        body = functools.partial(back_body, blocks, base is not None)
        return run(body, name, [w, *grads] + ([] if base is None else [base]), [wide_f], deps)[0]

    up = [(0, 1), (1, 2), (2, 3)]
    down = [(1, 0), (2, 1), (3, 2)]
    outer = [(0, 1), (3, 2)]
    u1 = lax.ppermute(grad, "head", up)
    d1 = lax.ppermute(grad, "head", down)
    send, keep = run(functools.partial(states_body, half), "local_states", [k, v], [state, state])
    (inside,) = run(intra_body, "intra", [q, k, v], [wide_f], [send])
    base = back_project([lambda z: z], "back_own", [grad], None, [inside])
    own, other = exchange(send, keep, info, lens, tok, True, [(), (inside,), (base,)])
    att, normed = run(norm_body, "normalise", [q, own, other, inside], [wide_f, wide_b])
    u2 = lax.ppermute(u1, "head", [(1, 2), (2, 3)])
    d2 = lax.ppermute(d1, "head", [(2, 1), (1, 0)])
    (pa,) = project([lambda z: jnp.where(z == 0, 3, 0)], "project_far")
    ra = lax.ppermute(pa, "head", outer)
    p2, p1, p3, p0 = project(
        [lambda z: lax.rem(z + 2, 4), lambda z: lax.rem(z + 1, 4), lambda z: lax.rem(z + 3, 4), lambda z: z],
        "project_rest", [pa],
    )
    base = back_project(
        [lambda z: lax.rem(z + 3, 4), lambda z: lax.rem(z + 1, 4)], "back_near", [u1, d1], base, [p2]
    )
    (x2,) = run(sum_body, "join", [u2, d2], [part], [base])
    x3 = lax.ppermute(x2, "head", [(2, 3), (1, 0)])
    (b2,) = run(sum_body, "fold", [p2, ra], [part], [base])
    bo = lax.ppermute(p2, "head", outer)
    bi = lax.ppermute(b2, "head", [(1, 2), (2, 1)])
    base = back_project([lambda z: lax.rem(z + 2, 4)], "back_far", [x2], base, [b2])
    cu, cd = run(fold_body, "fold_both", [p1, p3, bo, bi], [part, part], [base])
    gu = lax.ppermute(cu, "head", up)
    gd = lax.ppermute(cd, "head", down)
    ag, gsend, gkeep = run(
        functools.partial(att_grad_body, lambda z: jnp.where(z == 3, 0, 3)), "attended_grads",
        [w, x3, base, att, q], [wide_b, state, state], [cu],
    )
    query_grad, kp, vp = run(
        grads_body, "block_grads", [q, k, v, ag, own, other], [wide_b, wide_f, wide_f], [gsend]
    )
    leaving, leaving_other = exchange(gsend, gkeep, info, lens, tok, False, [(), (query_grad,), ()])
    key_grad, value_grad = run(
        last_body, "last_grads", [k, v, leaving, leaving_other, kp, vp], [wide_b, wide_b]
    )
    (mixed,) = run(sum_body, "mixed", [p0, gu, gd], [part], [key_grad])
    return mixed, query_grad, key_grad, value_grad


def solution(mesh):
    return jax.shard_map(
        shards,
        mesh=mesh,
        in_specs=(
            P("ctx", "head"),
            P("ctx", "head"),
            P("ctx", "head"),
            P(),
            P("head", None),
            P("ctx", "head"),
        ),
        out_specs=(P("ctx", "head"), P("ctx", "head"), P("ctx", "head"), P("ctx", "head")),
        check_vma=False,
    )
```

time: 254 us -> 127 us (0.50)
  waiting for transfers between devices: 131 us -> 35.3 us
  matrix products: 48.5 us -> 0 us
  Pallas kernels: 0 us -> 42.5 us
  starting transfers between devices: 0.34 us -> 38 us
  other arithmetic: 27.3 us -> 0.08 us
  blocking collectives: 15.3 us -> 0 us
  between operations: 14.7 us -> 1.02 us
  local copies, waits for them, and re-layouts: 15.5 us -> 9.9 us
    all_gather x3 -> x0, waiting for transfers between devices: 84 us -> none  [the longest x1 73.4 us: shards(): lax.all_gather(out_grad, 'head', axis=1, tiled=True)]
    dot_general x15 -> x0, matrix products: 48.5 us -> none  [the longest x1 9.85 us: shards(): lax.dot_general(lax.all_gather(out_grad, 'head', axis=1, tiled=True), out...]
    reduce_scatter x1 -> x0, waiting for transfers between devices: 46.3 us -> none  [shards(): lax.psum_scatter(partial_out.astype(jnp.bfloat16), 'head', scatter_dimens...]
    pallas_call x0 -> x21, Pallas kernels: none -> 42.5 us  [kernel(): pl.pallas_call(inner, name=name, in_specs=[smem, smem] + [vmem] * n_in +...]
    ppermute x0 -> x18, starting transfers between devices: none -> 38 us  [the longest x1 9.04 us: shards(): gu = lax.ppermute(cu, 'head', up)]
    ppermute x0 -> x18, waiting for transfers between devices: none -> 35.3 us  [the longest x1 14.3 us: shards(): bo = lax.ppermute(p2, 'head', outer)]
    select_n x8 -> x0, other arithmetic: 15.5 us -> none  [lap(): return jax.tree.map(lambda a, b: jnp.where(reached, a, b), new, before)]
    unnamed x1 -> x0, blocking collectives: 15.3 us -> none
  transfers between devices with their start and end apart: 4 -> 18, of which waited for: 4 -> 8; matrix products, arithmetic and copies ran while one was open for 28% -> 0% of each run, Pallas kernels for 0% -> 32%
where the time goes in v2:
time: 127 us
  Pallas kernels  42.5 us (33%)
  starting transfers between devices  38 us (30%)
  waiting for transfers between devices  35.3 us (28%)
  local copies, waits for them, and re-layouts  9.9 us (8%)
    pallas_call x21, Pallas kernels, kernel(): pl.pallas_call(inner, name=name, in_specs=[smem, smem] + [vmem] * n_in +...  42.5 us
    ppermute x1, waiting for transfers between devices, shards(): bo = lax.ppermute(p2, 'head', outer)  14.3 us
    unnamed x28, local copies, waits for them, and re-layouts  9.9 us
    ppermute x1, starting transfers between devices, shards(): gu = lax.ppermute(cu, 'head', up)  9.04 us
    ppermute x1, waiting for transfers between devices, shards(): ra = lax.ppermute(pa, 'head', outer)  7.87 us
    ppermute x4, starting transfers between devices, exchange(): other = lax.ppermute(total, 'ctx', pairs)  6.88 us
    ppermute x4, waiting for transfers between devices, exchange(): other = lax.ppermute(total, 'ctx', pairs)  5.88 us
    ppermute x1, starting transfers between devices, shards(): bo = lax.ppermute(p2, 'head', outer)  5.42 us
  transfers between devices with their start and end apart: 18, of which 8 were waited for; matrix products, arithmetic and copies ran while one was open for 0% of the time, Pallas kernels for 32%

profile of v2, /device:TPU:0, one launch (start us, length us, event | category | flops | bytes accessed | tf_op | source)
XLA Modules:
  0.0 126.8 jit_solution(14410779296430150711)
XLA Ops:
  0.6 5.1 %collective-permute-start.6 = (bf16[512,1024]{1,0:T(8,128)(2,1)}, bf16[512,1024]{1,0:T(8,128)(2,1)S(1)}, u32[]{:S(2)}, u32[]{:S(2)}) collective-permute-start(bf16[512,1024]{1,0:T(8,128)(2,1)} %refs_1_.9), channel_id=1, source_target_pairs={{0,1},{1,2},{2,3},{4,5},{5,6},{6,7},{8,9},{9,10},{10,11},{12,13},{... | collective-permute-start | bytes 3145736 | tf_op jit(solution)/shard_map/ppermute | solution.py:337
  11.6 1.3 %collective-permute-done.refs_1_.refs_3_ = bf16[4,128,128]{2,1,0:T(8,128)(2,1)S(1)} collective-permute-done((bf16[4,128,128]{2,1,0:T(8,128)(2,1)S(1)}, bf16[4,128,128]{2,1,0:T(8,128)(2,1)S(1)}, u32[]{:S(2)}, u32[]{:S(2)}) %collective-permute-start) | collective-permute-done | bytes 131104 | tf_op jit(solution)/shard_map/ppermute | solution.py:286
  13.5 1.6 %collective-permute-start.1 = (bf16[4,128,128]{2,1,0:T(8,128)(2,1)S(1)}, bf16[4,128,128]{2,1,0:T(8,128)(2,1)S(1)}, u32[]{:S(2)}, u32[]{:S(2)}) collective-permute-start(bf16[4,128,128]{2,1,0:T(8,128)(2,1)S(1)} %pair_total.2.refs_1_), channel_id=1, source_target_pairs={{0,8},{4,12},{8,0},{12,4},{16,24},{20,28},{24,16},{28,20},{1,9},{5... | collective-permute-start | bytes 393224 | tf_op jit(solution)/shard_map/ppermute | solution.py:295
  18.2 3.0 %intra.1.refs_2_.refs_3_ = f32[512,1024]{1,0:T(8,128)S(1)} custom-call(s32[3]{0:T(128)S(1)} %pad_add_fusion.info_ref, s32[4]{0:T(128)S(1)} %copy-done.12, bf16[512,1024]{1,0:T(8,128)(2,1)S(1)} %copy-done.1, bf16[512,1024]{1,0:T(8,128)(2,1)S(1)} %copy-done.3, bf16[512,1024]{1,0:T(8,128)(2,1)S(1)} %copy-done.6, bf16[4,128,128]{2,1,0:T(8,128)(2,1)S(1)} %get-tuple-element.31.refs_3_), custom_call_target="tpu_custom_call" | custom-call | tf_op jit(solution)/shard_map/intra/pallas_call | solution.py:29
  21.9 3.4 %collective-permute-start.2 = (bf16[4,128,128]{2,1,0:T(8,128)(2,1)S(1)}, bf16[4,128,128]{2,1,0:T(8,128)(2,1)S(1)}, u32[]{:S(2)}, u32[]{:S(2)}) collective-permute-start(bf16[4,128,128]{2,1,0:T(8,128)(2,1)S(1)} %get-tuple-element.32), channel_id=1, source_target_pairs={{0,16},{4,20},{8,24},{12,28},{1,17},{5,21},{9,25},{13,29},{2,18},{... | collective-permute-start | bytes 393224 | tf_op jit(solution)/shard_map/ppermute | solution.py:295
  26.6 1.8 %back_own.1.refs_4_.refs_3_ = f32[512,1024]{1,0:T(8,128)S(1)} custom-call(s32[3]{0:T(128)S(1)} %pad_add_fusion.info_ref, s32[4]{0:T(128)S(1)} %copy-done.13, bf16[1024,4096]{1,0:T(8,128)(2,1)S(1)} %copy-done, bf16[512,1024]{1,0:T(8,128)(2,1)S(1)} %copy-done.10, f32[512,1024]{1,0:T(8,128)S(1)} %intra.1.refs_2_.refs_3_), custom_call_target="tpu_custom_call" | custom-call | tf_op jit(solution)/shard_map/back_own/pallas_call | solution.py:29
  29.2 1.3 %collective-permute-done.3.refs_2_.refs_5_ = bf16[4,128,128]{2,1,0:T(8,128)(2,1)S(1)} collective-permute-done((bf16[4,128,128]{2,1,0:T(8,128)(2,1)S(1)}, bf16[4,128,128]{2,1,0:T(8,128)(2,1)S(1)}, u32[]{:S(2)}, u32[]{:S(2)}) %collective-permute-start.3) | collective-permute-done | bytes 131104 | tf_op jit(solution)/shard_map/ppermute | solution.py:309
  30.5 1.5 %normalise.1 = (f32[512,1024]{1,0:T(8,128)S(1)}, bf16[512,1024]{1,0:T(8,128)(2,1)S(1)}) custom-call(s32[3]{0:T(128)S(1)} %pad_add_fusion.info_ref, s32[4]{0:T(128)S(1)} %copy-done.13, bf16[512,1024]{1,0:T(8,128)(2,1)S(1)} %copy-done.1, bf16[4,128,128]{2,1,0:T(8,128)(2,1)S(1)} %get-tuple-element.34.refs_1_.refs_4_, ...), custom_call_target="tpu_custom_call" | custom-call | tf_op jit(solution)/shard_map/normalise/pallas_call | solution.py:29
  32.1 1.8 %project_far.1.refs_2_ = bf16[512,1024]{1,0:T(8,128)(2,1)S(1)} custom-call(s32[3]{0:T(128)S(1)} %pad_add_fusion.info_ref, s32[4]{0:T(128)S(1)} %copy-done.13, bf16[512,1024]{1,0:T(8,128)(2,1)S(1)} %get-tuple-element.36.refs_0_, bf16[1024,4096]{1,0:T(8,128)(2,1)S(1)} %copy-done), custom_call_target="tpu_custom_call" | custom-call | tf_op jit(solution)/shard_map/project_far/pallas_call | solution.py:29
  33.9 4.6 %collective-permute-start.5 = (bf16[512,1024]{1,0:T(8,128)(2,1)S(1)}, bf16[512,1024]{1,0:T(8,128)(2,1)S(1)}, u32[]{:S(2)}, u32[]{:S(2)}) collective-permute-start(bf16[512,1024]{1,0:T(8,128)(2,1)S(1)} %project_far.1.refs_2_), channel_id=1, source_target_pairs={{0,1},{3,2},{4,5},{7,6},{8,9},{11,10},{12,13},{15,14},{16,17},{19,... | collective-permute-start | bytes 3145736 | tf_op jit(solution)/shard_map/ppermute | solution.py:347
  40.6 5.1 %project_rest.1 = (bf16[512,1024]{1,0:T(8,128)(2,1)S(1)}, bf16[512,1024]{1,0:T(8,128)(2,1)S(1)}, bf16[512,1024]{1,0:T(8,128)(2,1)S(1)}, bf16[512,1024]{1,0:T(8,128)(2,1)S(1)}) custom-call(s32[3]{0:T(128)S(1)} %pad_add_fusion.info_ref, s32[4]{0:T(128)S(1)} %copy-done.13, bf16[512,1024]{1,0:T(8,128)(2,1)S(1)} %get-tuple-element.36.refs_0_, ...), custom_call_target="tpu_custom_call" | custom-call | tf_op jit(solution)/shard_map/project_rest/pallas_call | solution.py:29
  45.7 5.4 %collective-permute-start.4 = (bf16[512,1024]{1,0:T(8,128)(2,1)S(1)}, bf16[512,1024]{1,0:T(8,128)(2,1)S(1)}, u32[]{:S(2)}, u32[]{:S(2)}) collective-permute-start(bf16[512,1024]{1,0:T(8,128)(2,1)S(1)} %get-tuple-element.40.refs_4_.refs_0_), channel_id=1, source_target_pairs={{0,1},{3,2},{4,5},{7,6},{8,9},{11,10},{12,13},{15,14},{16,17},{19,... | collective-permute-start | bytes 3145736 | tf_op jit(solution)/shard_map/ppermute | solution.py:358
  51.1 2.9 %back_near.1.refs_2_ = f32[512,1024]{1,0:T(8,128)S(1)} custom-call(s32[3]{0:T(128)S(1)} %pad_add_fusion.info_ref, s32[4]{0:T(128)S(1)} %copy-done.13, bf16[1024,4096]{1,0:T(8,128)(2,1)S(1)} %copy-done, bf16[512,1024]{1,0:T(8,128)(2,1)S(1)} %collective-permute-done.6.refs_1_, bf16[512,1024]{1,0:T(8,128)(2,1)S(1)} %collective-permute-done.7.refs_2_, ...), custom_call_target="tpu_custom_call" | custom-call | tf_op jit(solution)/shard_map/back_near/pallas_call | solution.py:29
  54.1 7.9 %collective-permute-done.5.refs_1_ = bf16[512,1024]{1,0:T(8,128)(2,1)S(1)} collective-permute-done((bf16[512,1024]{1,0:T(8,128)(2,1)S(1)}, bf16[512,1024]{1,0:T(8,128)(2,1)S(1)}, u32[]{:S(2)}, u32[]{:S(2)}) %collective-permute-start.5) | collective-permute-done | bytes 1048608 | tf_op jit(solution)/shard_map/ppermute | solution.py:347
  63.5 1.9 %collective-permute-done.10.refs_1_ = bf16[512,1024]{1,0:T(8,128)(2,1)S(1)} collective-permute-done((bf16[512,1024]{1,0:T(8,128)(2,1)S(1)}, bf16[512,1024]{1,0:T(8,128)(2,1)S(1)}, u32[]{:S(2)}, u32[]{:S(2)}) %collective-permute-start.10) | collective-permute-done | bytes 1048608 | tf_op jit(solution)/shard_map/ppermute | solution.py:345
  67.4 1.8 %back_far.1.refs_4_.refs_2_ = f32[512,1024]{1,0:T(8,128)S(1)} custom-call(s32[3]{0:T(128)S(1)} %pad_add_fusion.info_ref, s32[4]{0:T(128)S(1)} %copy-done.13, bf16[1024,4096]{1,0:T(8,128)(2,1)S(1)} %copy-done, bf16[512,1024]{1,0:T(8,128)(2,1)S(1)} %join.1.refs_1_, f32[512,1024]{1,0:T(8,128)S(1)} %back_near.1.refs_2_, bf16[512,1024]{1,0:T(8,128)(2,1)S(1)} %fold.1.refs_3_), custom_call_target="tpu_custom_call" | custom-call | tf_op jit(solution)/shard_map/back_far/pallas_call | solution.py:29
  69.3 14.3 %collective-permute-done.4.refs_2_ = bf16[512,1024]{1,0:T(8,128)(2,1)S(1)} collective-permute-done((bf16[512,1024]{1,0:T(8,128)(2,1)S(1)}, bf16[512,1024]{1,0:T(8,128)(2,1)S(1)}, u32[]{:S(2)}, u32[]{:S(2)}) %collective-permute-start.4) | collective-permute-done | bytes 1048608 | tf_op jit(solution)/shard_map/ppermute | solution.py:358
  84.7 9.0 %collective-permute-start.11 = (bf16[512,1024]{1,0:T(8,128)(2,1)S(1)}, bf16[512,1024]{1,0:T(8,128)(2,1)S(1)}, u32[]{:S(2)}, u32[]{:S(2)}) collective-permute-start(bf16[512,1024]{1,0:T(8,128)(2,1)S(1)} %get-tuple-element.41.refs_5_), channel_id=1, source_target_pairs={{0,1},{1,2},{2,3},{4,5},{5,6},{6,7},{8,9},{9,10},{10,11},{12,13},{... | collective-permute-start | bytes 3145736 | tf_op jit(solution)/shard_map/ppermute | solution.py:362
  95.1 4.2 %attended_grads.1 = (bf16[512,1024]{1,0:T(8,128)(2,1)S(1)}, bf16[4,128,128]{2,1,0:T(8,128)(2,1)S(1)}, bf16[4,128,128]{2,1,0:T(8,128)(2,1)S(1)}) custom-call(s32[3]{0:T(128)S(1)} %pad_add_fusion.info_ref, s32[4]{0:T(128)S(1)} %copy-done.13, bf16[1024,4096]{1,0:T(8,128)(2,1)S(1)} %copy-done, bf16[512,1024]{1,0:T(8,128)(2,1)S(1)} %collective-permute-done.13.refs_1_, ...), custom_call_target="tpu_custom_call" | custom-call | tf_op jit(solution)/shard_map/attended_grads/pallas_call | solution.py:29
  102.0 7.6 %block_grads.1 = (bf16[512,1024]{1,0:T(8,128)(2,1)}, f32[512,1024]{1,0:T(8,128)S(1)}, f32[512,1024]{1,0:T(8,128)S(1)}) custom-call(s32[3]{0:T(128)S(1)} %pad_add_fusion.info_ref, s32[4]{0:T(128)S(1)} %copy-done.13, bf16[512,1024]{1,0:T(8,128)(2,1)S(1)} %copy-done.1, bf16[512,1024]{1,0:T(8,128)(2,1)S(1)} %copy-done.4, bf16[512,1024]{1,0:T(8,128)(2,1)S(1)} %copy-done.7, ...), custom_call_target="tpu_custom_call" | custom-call | tf_op jit(solution)/shard_map/block_grads/pallas_call | solution.py:29
  112.8 5.9 %collective-permute-done.16.refs_0_ = bf16[4,128,128]{2,1,0:T(8,128)(2,1)S(1)} collective-permute-done((bf16[4,128,128]{2,1,0:T(8,128)(2,1)S(1)}, bf16[4,128,128]{2,1,0:T(8,128)(2,1)S(1)}, u32[]{:S(2)}, u32[]{:S(2)}) %collective-permute-start.16) | collective-permute-done | bytes 131104 | tf_op jit(solution)/shard_map/ppermute | solution.py:295
  119.4 1.3 %collective-permute-done.17.refs_3_ = bf16[4,128,128]{2,1,0:T(8,128)(2,1)S(1)} collective-permute-done((bf16[4,128,128]{2,1,0:T(8,128)(2,1)S(1)}, bf16[4,128,128]{2,1,0:T(8,128)(2,1)S(1)}, u32[]{:S(2)}, u32[]{:S(2)}) %collective-permute-start.17) | collective-permute-done | bytes 131104 | tf_op jit(solution)/shard_map/ppermute | solution.py:309
  120.7 3.0 %last_grads.1 = (bf16[512,1024]{1,0:T(8,128)(2,1)}, bf16[512,1024]{1,0:T(8,128)(2,1)}) custom-call(s32[3]{0:T(128)S(1)} %pad_add_fusion.info_ref, s32[4]{0:T(128)S(1)} %copy-done.13, bf16[512,1024]{1,0:T(8,128)(2,1)S(1)} %copy-done.4, bf16[512,1024]{1,0:T(8,128)(2,1)S(1)} %copy-done.7, bf16[4,128,128]{2,1,0:T(8,128)(2,1)S(1)} %get-tuple-element.50.refs_2_, ...), custom_call_target="tpu_custom_call" | custom-call | tf_op jit(solution)/shard_map/last_grads/pallas_call | solution.py:29
  124.9 1.9 %mixed.1 = bf16[512,1024]{1,0:T(8,128)(2,1)} custom-call(s32[3]{0:T(128)S(1)} %pad_add_fusion.info_ref, s32[4]{0:T(128)S(1)} %copy-done.13, bf16[512,1024]{1,0:T(8,128)(2,1)S(1)} %get-tuple-element.37.refs_0_, bf16[512,1024]{1,0:T(8,128)(2,1)S(1)} %collective-permute-done.11.refs_1_, bf16[512,1024]{1,0:T(8,128)(2,1)S(1)} %collective-permute-done.12.refs_2_, ...), custom_call_target="tpu_custom_call" | custom-call | tf_op jit(solution)/shard_map/mixed/pallas_call | solution.py:29
  (62 shorter events, 27.8 us)
Async XLA Ops:
  0.6 14.5 %copy-start.1 = (bf16[512,1024]{1,0:T(8,128)(2,1)S(1)}, bf16[512,1024]{1,0:T(8,128)(2,1)}, u32[]{:S(2)}) copy-start(bf16[512,1024]{1,0:T(8,128)(2,1)} %refs_0_.16) | copy-start | bytes 3145732
  0.6 39.2 %collective-permute-start.6 = (bf16[512,1024]{1,0:T(8,128)(2,1)}, bf16[512,1024]{1,0:T(8,128)(2,1)S(1)}, u32[]{:S(2)}, u32[]{:S(2)}) collective-permute-start(bf16[512,1024]{1,0:T(8,128)(2,1)} %refs_1_.9), channel_id=1, source_target_pairs={{0,1},{1,2},{2,3},{4,5},{5,6},{6,7},{8,9},{9,10},{10,11},{12,13},{... | collective-permute-start | bytes 3145736 | tf_op jit(solution)/shard_map/ppermute | solution.py:337
  5.8 32.7 %collective-permute-start.7 = (bf16[512,1024]{1,0:T(8,128)(2,1)}, bf16[512,1024]{1,0:T(8,128)(2,1)S(1)}, u32[]{:S(2)}, u32[]{:S(2)}) collective-permute-start(bf16[512,1024]{1,0:T(8,128)(2,1)} %refs_1_.9), channel_id=1, source_target_pairs={{1,0},{2,1},{3,2},{5,4},{6,5},{7,6},{9,8},{10,9},{11,10},{13,12},{... | collective-permute-start | bytes 3145736 | tf_op jit(solution)/shard_map/ppermute | solution.py:338
  10.3 15.1 %copy-start = (bf16[1024,4096]{1,0:T(8,128)(2,1)S(1)}, bf16[1024,4096]{1,0:T(8,128)(2,1)}, u32[]{:S(2)}) copy-start(bf16[1024,4096]{1,0:T(8,128)(2,1)} %refs_0_.15) | copy-start | bytes 25165828
  11.5 1.4 %collective-permute-start = (bf16[4,128,128]{2,1,0:T(8,128)(2,1)S(1)}, bf16[4,128,128]{2,1,0:T(8,128)(2,1)S(1)}, u32[]{:S(2)}, u32[]{:S(2)}) collective-permute-start(bf16[4,128,128]{2,1,0:T(8,128)(2,1)S(1)} %get-tuple-element.31.refs_3_), channel_id=1, source_target_pairs={{0,4},{4,0},{8,12},{12,8},{16,20},{20,16},{24,28},{28,24},{1,5},{5... | collective-permute-start | bytes 393224 | tf_op jit(solution)/shard_map/ppermute | solution.py:286
  13.5 7.7 %collective-permute-start.1 = (bf16[4,128,128]{2,1,0:T(8,128)(2,1)S(1)}, bf16[4,128,128]{2,1,0:T(8,128)(2,1)S(1)}, u32[]{:S(2)}, u32[]{:S(2)}) collective-permute-start(bf16[4,128,128]{2,1,0:T(8,128)(2,1)S(1)} %pair_total.2.refs_1_), channel_id=1, source_target_pairs={{0,8},{4,12},{8,0},{12,4},{16,24},{20,28},{24,16},{28,20},{1,9},{5... | collective-permute-start | bytes 393224 | tf_op jit(solution)/shard_map/ppermute | solution.py:295
  21.2 4.1 %copy-start.13 = (s32[4]{0:T(128)S(1)}, s32[4]{0:T(128)}, u32[]{:S(2)}) copy-start(s32[4]{0:T(128)} %lens_ref.41) | copy-start | bytes 52
  21.9 6.5 %collective-permute-start.2 = (bf16[4,128,128]{2,1,0:T(8,128)(2,1)S(1)}, bf16[4,128,128]{2,1,0:T(8,128)(2,1)S(1)}, u32[]{:S(2)}, u32[]{:S(2)}) collective-permute-start(bf16[4,128,128]{2,1,0:T(8,128)(2,1)S(1)} %get-tuple-element.32), channel_id=1, source_target_pairs={{0,16},{4,20},{8,24},{12,28},{1,17},{5,21},{9,25},{13,29},{2,18},{... | collective-permute-start | bytes 393224 | tf_op jit(solution)/shard_map/ppermute | solution.py:295
  25.4 1.2 copy-start.10
  29.1 1.4 %collective-permute-start.3 = (bf16[4,128,128]{2,1,0:T(8,128)(2,1)S(1)}, bf16[4,128,128]{2,1,0:T(8,128)(2,1)S(1)}, u32[]{:S(2)}, u32[]{:S(2)}) collective-permute-start(bf16[4,128,128]{2,1,0:T(8,128)(2,1)S(1)} %get-tuple-element.35), channel_id=1, source_target_pairs={{0,4},{4,0},{8,12},{12,8},{16,20},{20,16},{24,28},{28,24},{1,5},{5... | collective-permute-start | bytes 393224 | tf_op jit(solution)/shard_map/ppermute | solution.py:309
  33.9 28.1 %collective-permute-start.5 = (bf16[512,1024]{1,0:T(8,128)(2,1)S(1)}, bf16[512,1024]{1,0:T(8,128)(2,1)S(1)}, u32[]{:S(2)}, u32[]{:S(2)}) collective-permute-start(bf16[512,1024]{1,0:T(8,128)(2,1)S(1)} %project_far.1.refs_2_), channel_id=1, source_target_pairs={{0,1},{3,2},{4,5},{7,6},{8,9},{11,10},{12,13},{15,14},{16,17},{19,... | collective-permute-start | bytes 3145736 | tf_op jit(solution)/shard_map/ppermute | solution.py:347
  38.5 26.8 %collective-permute-start.10 = (bf16[512,1024]{1,0:T(8,128)(2,1)S(1)}, bf16[512,1024]{1,0:T(8,128)(2,1)S(1)}, u32[]{:S(2)}, u32[]{:S(2)}) collective-permute-start(bf16[512,1024]{1,0:T(8,128)(2,1)S(1)} %collective-permute-done.7.refs_2_), channel_id=1, source_target_pairs={{2,1},{1,0},{6,5},{5,4},{10,9},{9,8},{14,13},{13,12},{18,17},{17,1... | collective-permute-start | bytes 3145736 | tf_op jit(solution)/shard_map/ppermute | solution.py:345
  39.8 25.5 %collective-permute-start.9 = (bf16[512,1024]{1,0:T(8,128)(2,1)S(1)}, bf16[512,1024]{1,0:T(8,128)(2,1)S(1)}, u32[]{:S(2)}, u32[]{:S(2)}) collective-permute-start(bf16[512,1024]{1,0:T(8,128)(2,1)S(1)} %collective-permute-done.6.refs_1_), channel_id=1, source_target_pairs={{1,2},{2,3},{5,6},{6,7},{9,10},{10,11},{13,14},{14,15},{17,18},{18... | collective-permute-start | bytes 3145736 | tf_op jit(solution)/shard_map/ppermute | solution.py:344
  45.7 37.9 %collective-permute-start.4 = (bf16[512,1024]{1,0:T(8,128)(2,1)S(1)}, bf16[512,1024]{1,0:T(8,128)(2,1)S(1)}, u32[]{:S(2)}, u32[]{:S(2)}) collective-permute-start(bf16[512,1024]{1,0:T(8,128)(2,1)S(1)} %get-tuple-element.40.refs_4_.refs_0_), channel_id=1, source_target_pairs={{0,1},{3,2},{4,5},{7,6},{8,9},{11,10},{12,13},{15,14},{16,17},{19,... | collective-permute-start | bytes 3145736 | tf_op jit(solution)/shard_map/ppermute | solution.py:358
  62.7 20.9 %collective-permute-start.8 = (bf16[512,1024]{1,0:T(8,128)(2,1)S(1)}, bf16[512,1024]{1,0:T(8,128)(2,1)S(1)}, u32[]{:S(2)}, u32[]{:S(2)}) collective-permute-start(bf16[512,1024]{1,0:T(8,128)(2,1)S(1)} %fold.1.refs_3_), channel_id=1, source_target_pairs={{1,2},{2,1},{5,6},{6,5},{9,10},{10,9},{13,14},{14,13},{17,18},{18,... | collective-permute-start | bytes 3145736 | tf_op jit(solution)/shard_map/ppermute | solution.py:359
  66.1 28.9 %collective-permute-start.13 = (bf16[512,1024]{1,0:T(8,128)(2,1)S(1)}, bf16[512,1024]{1,0:T(8,128)(2,1)S(1)}, u32[]{:S(2)}, u32[]{:S(2)}) collective-permute-start(bf16[512,1024]{1,0:T(8,128)(2,1)S(1)} %join.1.refs_1_), channel_id=1, source_target_pairs={{2,3},{1,0},{6,7},{5,4},{10,11},{9,8},{14,15},{13,12},{18,19},{17,... | collective-permute-start | bytes 3145736 | tf_op jit(solution)/shard_map/ppermute | solution.py:356
  84.7 39.0 %collective-permute-start.11 = (bf16[512,1024]{1,0:T(8,128)(2,1)S(1)}, bf16[512,1024]{1,0:T(8,128)(2,1)S(1)}, u32[]{:S(2)}, u32[]{:S(2)}) collective-permute-start(bf16[512,1024]{1,0:T(8,128)(2,1)S(1)} %get-tuple-element.41.refs_5_), channel_id=1, source_target_pairs={{0,1},{1,2},{2,3},{4,5},{5,6},{6,7},{8,9},{9,10},{10,11},{12,13},{... | collective-permute-start | bytes 3145736 | tf_op jit(solution)/shard_map/ppermute | solution.py:362
  93.8 29.9 %collective-permute-start.12 = (bf16[512,1024]{1,0:T(8,128)(2,1)S(1)}, bf16[512,1024]{1,0:T(8,128)(2,1)S(1)}, u32[]{:S(2)}, u32[]{:S(2)}) collective-permute-start(bf16[512,1024]{1,0:T(8,128)(2,1)S(1)} %get-tuple-element.42), channel_id=1, source_target_pairs={{1,0},{2,1},{3,2},{5,4},{6,5},{7,6},{9,8},{10,9},{11,10},{13,12},{... | collective-permute-start | bytes 3145736 | tf_op jit(solution)/shard_map/ppermute | solution.py:363
  95.1 6.9 %copy-start.4 = (bf16[512,1024]{1,0:T(8,128)(2,1)S(1)}, bf16[512,1024]{1,0:T(8,128)(2,1)}, u32[]{:S(2)}) copy-start(bf16[512,1024]{1,0:T(8,128)(2,1)} %refs_0_.17) | copy-start | bytes 3145732
  95.1 6.9 %copy-start.7 = (bf16[512,1024]{1,0:T(8,128)(2,1)S(1)}, bf16[512,1024]{1,0:T(8,128)(2,1)}, u32[]{:S(2)}) copy-start(bf16[512,1024]{1,0:T(8,128)(2,1)} %refs_1_.13) | copy-start | bytes 3145732
  99.3 1.4 %collective-permute-start.14 = (bf16[4,128,128]{2,1,0:T(8,128)(2,1)S(1)}, bf16[4,128,128]{2,1,0:T(8,128)(2,1)S(1)}, u32[]{:S(2)}, u32[]{:S(2)}) collective-permute-start(bf16[4,128,128]{2,1,0:T(8,128)(2,1)S(1)} %get-tuple-element.45.refs_6_), channel_id=1, source_target_pairs={{0,4},{4,0},{8,12},{12,8},{16,20},{20,16},{24,28},{28,24},{1,5},{5... | collective-permute-start | bytes 393224 | tf_op jit(solution)/shard_map/ppermute | solution.py:286
  101.4 8.2 %collective-permute-start.15 = (bf16[4,128,128]{2,1,0:T(8,128)(2,1)S(1)}, bf16[4,128,128]{2,1,0:T(8,128)(2,1)S(1)}, u32[]{:S(2)}, u32[]{:S(2)}) collective-permute-start(bf16[4,128,128]{2,1,0:T(8,128)(2,1)S(1)} %pair_total.3.refs_1_), channel_id=1, source_target_pairs={{0,8},{4,12},{8,0},{12,4},{16,24},{20,28},{24,16},{28,20},{1,9},{5... | collective-permute-start | bytes 393224 | tf_op jit(solution)/shard_map/ppermute | solution.py:295
  111.5 7.2 %collective-permute-start.16 = (bf16[4,128,128]{2,1,0:T(8,128)(2,1)S(1)}, bf16[4,128,128]{2,1,0:T(8,128)(2,1)S(1)}, u32[]{:S(2)}, u32[]{:S(2)}) collective-permute-start(bf16[4,128,128]{2,1,0:T(8,128)(2,1)S(1)} %get-tuple-element.48), channel_id=1, source_target_pairs={{16,0},{20,4},{24,8},{28,12},{17,1},{21,5},{25,9},{29,13},{18,2},{... | collective-permute-start | bytes 393224 | tf_op jit(solution)/shard_map/ppermute | solution.py:295
  119.3 1.4 %collective-permute-start.17 = (bf16[4,128,128]{2,1,0:T(8,128)(2,1)S(1)}, bf16[4,128,128]{2,1,0:T(8,128)(2,1)S(1)}, u32[]{:S(2)}, u32[]{:S(2)}) collective-permute-start(bf16[4,128,128]{2,1,0:T(8,128)(2,1)S(1)} %get-tuple-element.51), channel_id=1, source_target_pairs={{0,4},{4,0},{8,12},{12,8},{16,20},{20,16},{24,28},{28,24},{1,5},{5... | collective-permute-start | bytes 393224 | tf_op jit(solution)/shard_map/ppermute | solution.py:309
  (8 other events, 8.7 us)

commit v3 on v0

v3 whole, which is shorter than its diff:
```python
import functools

import jax
import jax.numpy as jnp
from jax import lax
from jax.experimental import pallas as pl
from jax.experimental.pallas import tpu as pltpu
from jax.sharding import PartitionSpec as P

DH = 128
EPS = 1e-06
F32 = jnp.float32
BF16 = jnp.bfloat16
MIB = 1024 * 1024

RATE = 10**8
MICROSECONDS = {
    "setup": 100.0, "local_states": 0.8, "intra": 3.0, "back_own": 1.8, "pair_total": 0.1, "exchange_stage": 0.1,
    "exchange_last": 0.1, "normalise": 0.9, "project_3": 1.8, "project_2": 1.8, "project_1": 1.8,
    "project_0": 1.8, "back_1": 1.8, "pick": 0.3, "turn": 0.5, "back_2": 1.8, "attended_grads": 4.1,
    "query_grad": 3.0, "key_value_grads": 5.0, "last_grads": 2.5, "mixed": 1.3,
}

I_BLK, I_CORE, I_Z, I_DOCS = 0, 1, 2, 3


def kernel(body, name, smem, ins, outs, deps=(), spare=8):
    n, n_dep = len(smem) + len(ins), len(deps)

    def inner(*refs):
        body(*refs[:n], *refs[n + n_dep:])

    size = sum(a.size * a.dtype.itemsize for a in list(ins) + list(outs))
    spec = lambda space: pl.BlockSpec(memory_space=space)
    return pl.pallas_call(
        inner,
        name=name,
        in_specs=[spec(pltpu.SMEM)] * len(smem) + [spec(pltpu.VMEM)] * len(ins) + [spec(pl.ANY)] * n_dep,
        out_specs=[spec(pltpu.VMEM)] * len(outs),
        out_shape=list(outs),
        compiler_params=pltpu.CompilerParams(vmem_limit_bytes=size + spare * MIB),
        cost_estimate=pl.CostEstimate(
            flops=int(MICROSECONDS[name] * RATE), bytes_accessed=0, transcendentals=0
        ),
    )(*smem, *ins, *deps)


def like(shape, dtype):
    return jax.ShapeDtypeStruct(shape, dtype)


def dot(a, b, ca, cb):
    return lax.dot_general(a, b, (((ca,), (cb,)), ((), ())), preferred_element_type=F32)


def head(h):
    return slice(h * DH, (h + 1) * DH)


def starts_of(info_ref):
    out, at = [], jnp.int32(0)
    for j in range(I_DOCS, info_ref.shape[0] - 1):
        at = at + info_ref[j]
        out.append(at)
    return out


def start_at(starts, p):
    best = jnp.minimum(p, 0)
    best = jnp.maximum(best, -1)
    for s in starts:
        best = jnp.where(p >= s, s, best)
    return best


def line(tok, axis):
    return lax.broadcasted_iota(jnp.int32, (tok, 1) if axis == 0 else (1, tok), axis)


def carries(info_ref, tok):
    first = info_ref[I_BLK] * tok
    starts = starts_of(info_ref)
    rows = start_at(starts, line(tok, 0) + first)
    return rows == start_at(starts, first - 1), rows == start_at(starts, first + tok - 1)


def visible(low_ref, axis):
    if axis == 0:
        tok = low_ref.shape[0]
        low = low_ref[:, :1]
    else:
        tok = low_ref.shape[1]
        low = low_ref[:1, :]
    t, s = line(tok, axis), line(tok, 1 - axis)
    return (s <= t) & (s >= low)


def same(starts, tok, a, b):
    pa, pb = a * tok + tok - 1, b * tok + tok - 1
    one = (a >= 0) | (b < 0)
    for s in starts:
        one = jnp.logical_and(one, jnp.logical_not(jnp.logical_and(pa < s, s <= pb)))
    return jnp.where(one, 1.0, 0.0).astype(F32)


def stages(n, forward):
    out, m = [], 2
    while m < n:
        r = 2
        out.append((m, r, m * r >= n))
        m *= r
    return out


def coefficients(starts, tok, n, blk, forward):
    link = functools.partial(same, starts, tok)
    core = lax.rem(blk, 2)
    first = blk - core
    one, none = jnp.float32(1.0), jnp.float32(0.0)
    if forward:
        near, inner, outer = core == 0, link(first, first + 1), link(first - 1, first)
    else:
        near, inner, outer = core == 1, link(first - 1, first), link(first, first + 1)
    out = [jnp.where(near, inner, one), jnp.where(near, one, inner)]
    for m, r, last in stages(n, forward):
        low = blk // (m * r) * (m * r)
        digit = lax.rem(blk // m, r)
        for x in range(1, r):
            j = jnp.bitwise_xor(digit, x)
            if forward:
                out.append(jnp.where(j < digit, link(low + (j + 1) * m - 1, first - 1), none))
            else:
                out.append(jnp.where(j > digit, link(first + 1, low + j * m - 1), none))
        if not last:
            for x in range(r):
                j = jnp.bitwise_xor(digit, x)
                if forward:
                    out.append(link(low + (j + 1) * m - 1, low + r * m - 1))
                else:
                    out.append(link(low - 1, low + j * m - 1))
    return out + [jnp.where(near, one, none), outer]


def pair_body(c_ref, mine_ref, got_ref, total_ref):
    a, b = c_ref[0:1, :], c_ref[1:2, :]
    total_ref[...] = (mine_ref[...].astype(F32) * a + got_ref[...].astype(F32) * b).astype(BF16)


def stage_body(row, r, last, begun, c_ref, *refs):
    refs = list(refs)
    others = [refs.pop(0)[...].astype(F32) for _ in range(r - 1)]
    entering = refs.pop(0)[...] if begun else None
    for other in others:
        part = other * c_ref[row:row + 1, :]
        entering = part if entering is None else entering + part
        row += 1
    if not last:
        total_ref, new_total_ref, entering_ref = refs
        entering_ref[...] = entering
        total = total_ref[...].astype(F32) * c_ref[row:row + 1, :]
        for other in others:
            row += 1
            total = total + other * c_ref[row:row + 1, :]
        new_total_ref[...] = total.astype(BF16)
        return
    mine_ref, got_ref, own_ref, away_ref = refs
    near, outer = c_ref[row:row + 1, :], c_ref[row + 1:row + 2, :]
    nearer = mine_ref[...].astype(F32) * near + got_ref[...].astype(F32) * (1.0 - near)
    chained = nearer + outer * entering
    own_ref[...] = (entering * near + chained * (1.0 - near)).astype(BF16)
    away_ref[...] = (chained * near + entering * (1.0 - near)).astype(BF16)


def pair_total(send, keep, coef):
    n = lax.axis_size("ctx")
    got = lax.ppermute(send, "ctx", [(i, i ^ 1) for i in range(n)])
    (total,) = kernel(pair_body, "pair_total", [], [coef, keep, got], [like(keep.shape, BF16)])
    return got, total


def exchange(total, keep, got, coef, forward, beside):
    n = lax.axis_size("ctx")
    swap = [(i, i ^ 1) for i in range(n)]
    half = like(keep.shape, BF16)
    entering, row = [], 2
    for m, r, last in stages(n, forward):
        others = []
        for x in range(1, r):
            pairs = [
                (i, i ^ (x * m)) for i in range(n)
                if not last or ((i // m % r) < (i // m % r ^ x)) == forward
            ]
            others.append(lax.ppermute(total, "ctx", pairs))
        deps = beside.pop(0)(total) if beside else ()
        body = functools.partial(stage_body, row, r, last, bool(entering))
        if last:
            own, away = kernel(
                body, "exchange_last", [], [coef, *others, *entering, keep, got], [half, half], deps
            )
        else:
            total, e = kernel(
                body, "exchange_stage", [], [coef, *others, *entering, total],
                [half, like(keep.shape, F32)], deps,
            )
            entering = [e]
            row += 2 * r - 1
    return own, lax.ppermute(away, "ctx", swap)


TILE = 256
ROWS = 32
C_CORE, C_END = ROWS - 1, ROWS - 2


def put_states(states, c_ref, keep_ref, send_ref):
    half = len(states) // 2
    core0 = c_ref[C_CORE:C_CORE + 1, :] > 0.5
    for i in range(half):
        keep_ref[i] = jnp.where(core0, states[i], states[i + half]).astype(BF16)
        send_ref[i] = jnp.where(core0, states[i + half], states[i]).astype(BF16)


def setup_body(n, tok, info_ref, coef_ref, coefb_ref, cin_ref, cout_ref, low_ref, low_t_ref):
    blk, core = info_ref[I_BLK], info_ref[I_CORE]
    starts = starts_of(info_ref)
    for ref, forward in ((coef_ref, True), (coefb_ref, False)):
        ref[...] = jnp.zeros_like(ref)
        for i, c in enumerate(coefficients(starts, tok, n, blk, forward)):
            ref[i:i + 1, :] = jnp.full((1, DH), c, F32)
        ref[C_CORE:C_CORE + 1, :] = jnp.full((1, DH), jnp.where(core == 0, 1.0, 0.0), F32)
        end = jnp.logical_or(info_ref[I_Z] == 0, info_ref[I_Z] == 3)
        ref[C_END:C_END + 1, :] = jnp.full((1, DH), jnp.where(end, 1.0, 0.0), F32)
    cin, cout = carries(info_ref, tok)
    cin_ref[...] = jnp.broadcast_to(jnp.where(cin, 1.0, 0.0), cin_ref.shape)
    cout_ref[...] = jnp.broadcast_to(jnp.where(cout, 1.0, 0.0), cout_ref.shape)
    first = blk * tok
    for ref, axis in ((low_ref, 0), (low_t_ref, 1)):
        low = start_at(starts, line(tok, axis) + first) - first
        ref[...] = jnp.broadcast_to(low, ref.shape)


def states_body(c_ref, cout_ref, k_ref, v_ref, send_ref, keep_ref):
    zero = jnp.zeros((), BF16)
    cout = cout_ref[...] > 0.5
    states = []
    for h in range(k_ref.shape[1] // DH):
        kept = jnp.where(cout, k_ref[:, head(h)], zero)
        states.append(dot(kept, v_ref[:, head(h)], 0, 0))
    put_states(states, c_ref, keep_ref, send_ref)


def intra_body(low_ref, q_ref, k_ref, v_ref, out_ref):
    mask = visible(low_ref, 0)
    for h in range(q_ref.shape[1] // DH):
        s = dot(q_ref[:, head(h)], k_ref[:, head(h)], 1, 1)
        s = jnp.where(mask, s, 0.0).astype(BF16)
        out_ref[:, head(h)] = dot(s, v_ref[:, head(h)], 1, 0)


def pick(c_ref, own_ref, back_ref, h):
    half = own_ref.shape[0]
    core0 = c_ref[C_CORE:C_CORE + 1, :] > 0.5
    a, b = own_ref[h % half].astype(F32), back_ref[h % half].astype(F32)
    return (jnp.where(core0, a, b) if h < half else jnp.where(core0, b, a)).astype(BF16)


def norm_body(c_ref, cin_ref, q_ref, own_ref, back_ref, a_ref, normed_ref, inv_ref, n_ref):
    wide = q_ref.shape[1]
    for h in range(wide // DH):
        inter = dot(q_ref[:, head(h)], pick(c_ref, own_ref, back_ref, h), 1, 0)
        att = a_ref[:, head(h)] + cin_ref[...] * inter
        inv = lax.rsqrt(jnp.mean(att * att, axis=-1, keepdims=True) + EPS)
        normed = att * inv
        inv_ref[:, head(h)] = jnp.broadcast_to(inv, att.shape)
        normed_ref[:, head(h)] = normed
        n_ref[:, head(h)] = normed.astype(BF16)


def columns(info_ref, block, width):
    return pl.multiple_of(jnp.bitwise_xor(info_ref[I_Z], block) * width, width)


def project_body(block, info_ref, n_ref, w_ref, out_ref):
    width = out_ref.shape[1]
    base = columns(info_ref, block, width)
    for i in range(width // TILE):
        at = pl.multiple_of(base + i * TILE, TILE)
        out_ref[:, i * TILE:(i + 1) * TILE] = dot(
            n_ref[...], w_ref[:, pl.ds(at, TILE)], 1, 0
        ).astype(BF16)


def back_body(blocks, based, info_ref, w_ref, *refs):
    out_ref = refs[-1]
    feats = out_ref.shape[1]
    for i in range(feats // TILE):
        rows = slice(i * TILE, (i + 1) * TILE)
        acc = refs[-2][:, rows] if based else None
        for block, g_ref in zip(blocks, refs, strict=False):
            width = g_ref.shape[1]
            at = columns(info_ref, block, width)
            part = dot(g_ref[...], w_ref[rows, pl.ds(at, width)], 1, 1)
            acc = part if acc is None else acc + part
        out_ref[:, rows] = acc


def att_grad_body(block, info_ref, w_ref, x_ref, base_ref, normed_ref, inv_ref, q_ref, c_ref, cin_ref, ag_ref, send_ref, keep_ref):
    wide = q_ref.shape[1]
    width = x_ref.shape[1]
    at = columns(info_ref, block, width)
    zero = jnp.zeros((), BF16)
    cin = cin_ref[...] > 0.5
    states = []
    for i in range(wide // TILE):
        rows = slice(i * TILE, (i + 1) * TILE)
        ng2 = base_ref[:, rows] + dot(x_ref[...], w_ref[rows, pl.ds(at, width)], 1, 1)
        for j in range(TILE // DH):
            h = i * (TILE // DH) + j
            ng, normed = ng2[:, head(j)], normed_ref[:, head(h)]
            proj = jnp.mean(ng * normed, axis=-1, keepdims=True)
            ag = ((ng - normed * proj) * inv_ref[:, head(h)]).astype(BF16)
            ag_ref[:, head(h)] = ag
            kept = jnp.where(cin, q_ref[:, head(h)], zero)
            states.append(dot(kept, ag, 0, 0))
    put_states(states, c_ref, keep_ref, send_ref)


def query_grad_body(low_ref, c_ref, cin_ref, k_ref, v_ref, ag_ref, own_ref, back_ref, qg_ref, mark_ref):
    mask = visible(low_ref, 0)
    mark_ref[...] = jnp.zeros_like(mark_ref)
    for h in range(k_ref.shape[1] // DH):
        ag = ag_ref[:, head(h)]
        inter = dot(ag, pick(c_ref, own_ref, back_ref, h), 1, 1)
        g = jnp.where(mask, dot(ag, v_ref[:, head(h)], 1, 1), 0.0).astype(BF16)
        qg_ref[:, head(h)] = (dot(g, k_ref[:, head(h)], 1, 0) + cin_ref[...] * inter).astype(BF16)


def key_value_body(low_t_ref, q_ref, k_ref, v_ref, ag_ref, kg_ref, vg_ref):
    mask = visible(low_t_ref, 1)
    for h in range(q_ref.shape[1] // DH):
        q, k, v, ag = (r[:, head(h)] for r in (q_ref, k_ref, v_ref, ag_ref))
        st = jnp.where(mask, dot(k, q, 1, 1), 0.0).astype(BF16)
        vg_ref[:, head(h)] = dot(st, ag, 1, 0)
        gt = jnp.where(mask, dot(v, ag, 1, 1), 0.0).astype(BF16)
        kg_ref[:, head(h)] = dot(gt, q, 1, 0)


def last_body(c_ref, cout_ref, k_ref, v_ref, own_ref, back_ref, kp_ref, vp_ref, kg_ref, vg_ref, mark_ref):
    mark_ref[...] = jnp.zeros_like(mark_ref)
    wide = k_ref.shape[1]
    cout = cout_ref[...]
    for h in range(wide // DH):
        leaving = pick(c_ref, own_ref, back_ref, h)
        kg = cout * dot(v_ref[:, head(h)], leaving, 1, 1)
        vg = cout * dot(k_ref[:, head(h)], leaving, 1, 0)
        kg_ref[:, head(h)] = (kp_ref[:, head(h)] + kg).astype(BF16)
        vg_ref[:, head(h)] = (vp_ref[:, head(h)] + vg).astype(BF16)


def sum_body(*refs):
    total = refs[0][...].astype(F32)
    for r in refs[1:-1]:
        total = total + r[...].astype(F32)
    refs[-1][...] = total.astype(BF16)


def at_end(c_ref):
    return c_ref[C_END:C_END + 1, :].astype(BF16)


def end_body(c_ref, a_ref, b_ref, out_ref):
    end = at_end(c_ref)
    for i in range(out_ref.shape[1] // DH):
        out_ref[:, head(i)] = a_ref[:, head(i)] * end + b_ref[:, head(i)]


def turn_body(c_ref, n2_ref, p2_ref, i2_ref, s2_ref, n3_ref):
    s2_ref[...] = p2_ref[...] + n2_ref[...]
    end_body(c_ref, p2_ref, i2_ref, n3_ref)


def turn_again_body(n3_ref, i3_ref, p3_ref, p1_ref, s3_ref, s1_ref):
    s3_ref[...] = p3_ref[...] + n3_ref[...]
    s1_ref[...] = p1_ref[...] + i3_ref[...]


def shards(q, k, v, lens, w, grad):
    tok, width = grad.shape
    feats = w.shape[0]
    heads = feats // DH
    half = heads // 2
    n = lax.axis_size("ctx")
    blk = lax.axis_index("ctx").astype(jnp.int32)
    z = lax.axis_index("head").astype(jnp.int32)
    info = jnp.concatenate([jnp.stack([blk, blk % 2, z]), lens])
    part = like((tok, width), BF16)
    wide_b, wide_f = like((tok, feats), BF16), like((tok, feats), F32)
    state = like((half, DH, DH), BF16)
    lanes = like((tok, DH), F32)
    table = like((ROWS, DH), F32)

    def project(block, name, deps=()):
        body = functools.partial(project_body, block)
        return kernel(body, name, [info], [normed, w], [part], deps)[0]

    def back_project(blocks, name, grads, base=None, deps=()):
        body = functools.partial(back_body, blocks, base is not None)
        return kernel(body, name, [info], [w, *grads] + ([] if base is None else [base]), [wide_f], deps)[0]

    neighbours = [(0, 1), (1, 0), (2, 3), (3, 2)]
    inner = [(1, 2), (2, 1)]
    g1 = lax.ppermute(grad, "head", neighbours)
    g3_inner = lax.ppermute(grad, "head", inner)
    coef, coefb, cin, cout, low, low_t = kernel(
        functools.partial(setup_body, n, tok), "setup", [info], [],
        [table, table, lanes, lanes, like((tok, DH), jnp.int32), like((8, tok), jnp.int32)],
    )
    send, keep = kernel(states_body, "local_states", [], [coef, cout, k, v], [state, state])
    got, total = pair_total(send, keep, coef)
    (inside,) = kernel(intra_body, "intra", [], [low, q, k, v], [wide_f], [total])
    base = back_project([0], "back_own", [grad], None, [inside])
    own, other = exchange(total, keep, got, coef, True, [lambda _: [inside], lambda _: [base]])
    normed_f, inv, normed = kernel(
        norm_body, "normalise", [], [coef, cin, q, own, other, inside], [wide_f, wide_f, wide_b]
    )
    p3 = project(3, "project_3")
    g1, g3_inner, _ = lax.optimization_barrier((g1, g3_inner, p3))
    (n2,) = kernel(end_body, "pick", [], [coef, p3, g3_inner], [part], [g1])
    n2 = lax.ppermute(n2, "head", neighbours)
    i2 = lax.ppermute(g1, "head", inner)
    p2 = project(2, "project_2", [p3])
    p1 = project(1, "project_1", [p2])
    p0 = project(0, "project_0", [p1])
    base = back_project([1], "back_1", [g1], base, [p0])
    s2, n3 = kernel(turn_body, "turn", [], [coef, n2, p2, i2], [part, part], [base])
    i3 = lax.ppermute(s2, "head", inner)
    n3 = lax.ppermute(n3, "head", neighbours)
    (g2,) = kernel(end_body, "pick", [], [coef, n2, i2], [part], [s2])
    base = back_project([2], "back_2", [g2], base)
    s3, s1 = kernel(turn_again_body, "turn", [], [n3, i3, p3, p1], [part, part], [base])
    n4 = lax.ppermute(s1, "head", neighbours)
    i4 = lax.ppermute(s3, "head", inner)
    (g3,) = kernel(end_body, "pick", [], [coef, n3, g3_inner], [part], [s1])
    ag, gsend, gkeep = kernel(
        functools.partial(att_grad_body, 3), "attended_grads", [info],
        [w, g3, base, normed_f, inv, q, coef, cin], [wide_b, state, state], [s1],
    )
    ggot, gtotal = pair_total(gsend, gkeep, coefb)
    grads = []

    def beside_first(sent):
        grads.extend(kernel(
            query_grad_body, "query_grad", [], [low, coef, cin, k, v, ag, own, other],
            [wide_b, like((8, DH), F32)], [sent],
        ))
        return grads[1:2]

    def beside_second(sent):
        grads.extend(kernel(
            key_value_body, "key_value_grads", [], [low_t, q, k, v, ag], [wide_f, wide_f], [sent]
        ))
        return grads[2:3]

    leaving, leaving_other = exchange(gtotal, gkeep, ggot, coefb, False, [beside_first, beside_second])
    query_grad, _, kp, vp = grads
    key_grad, value_grad, mark = kernel(
        last_body, "last_grads", [], [coef, cout, k, v, leaving, leaving_other, kp, vp],
        [wide_b, wide_b, like((8, DH), F32)],
    )
    (mixed,) = kernel(sum_body, "turn", [], [p0, n4], [part], [mark])
    (mixed,) = kernel(sum_body, "mixed", [], [mixed, i4], [part])
    return mixed, query_grad, key_grad, value_grad


def solution(mesh):
    return jax.shard_map(
        shards,
        mesh=mesh,
        in_specs=(
            P("ctx", "head"),
            P("ctx", "head"),
            P("ctx", "head"),
            P(),
            P("head", None),
            P("ctx", "head"),
        ),
        out_specs=(P("ctx", "head"), P("ctx", "head"), P("ctx", "head"), P("ctx", "head")),
        check_vma=False,
    )
```

time: 254 us -> 109 us (0.43)
  waiting for transfers between devices: 131 us -> 43.4 us
  matrix products: 48.5 us -> 0 us
  Pallas kernels: 0 us -> 36.6 us
  other arithmetic: 27.3 us -> 0.73 us
  starting transfers between devices: 0.34 us -> 26.4 us
  blocking collectives: 15.3 us -> 0 us
  local copies, waits for them, and re-layouts: 15.5 us -> 0.81 us
  between operations: 14.7 us -> 0.9 us
    all_gather x3 -> x0, waiting for transfers between devices: 84 us -> none  [the longest x1 73.4 us: shards(): lax.all_gather(out_grad, 'head', axis=1, tiled=True)]
    dot_general x15 -> x0, matrix products: 48.5 us -> none  [the longest x1 9.85 us: shards(): lax.dot_general(lax.all_gather(out_grad, 'head', axis=1, tiled=True), out...]
    reduce_scatter x1 -> x0, waiting for transfers between devices: 46.3 us -> none  [shards(): lax.psum_scatter(partial_out.astype(jnp.bfloat16), 'head', scatter_dimens...]
    ppermute x0 -> x16, waiting for transfers between devices: none -> 43.4 us  [the longest x1 17.9 us: shards(): n3 = lax.ppermute(n3, 'head', neighbours)]
    pallas_call x0 -> x28, Pallas kernels: none -> 36.6 us  [kernel(): pl.pallas_call(inner, name=name, in_specs=[spec(pltpu.SMEM)] * len(smem)...]
    ppermute x0 -> x16, starting transfers between devices: none -> 26.4 us  [the longest x4 8.05 us: exchange(): others.append(lax.ppermute(total, 'ctx', pairs))]
    select_n x8 -> x0, other arithmetic: 15.5 us -> none  [lap(): return jax.tree.map(lambda a, b: jnp.where(reached, a, b), new, before)]
    unnamed x1 -> x0, blocking collectives: 15.3 us -> none
  transfers between devices with their start and end apart: 4 -> 16, of which waited for: 4 -> 11; matrix products, arithmetic and copies ran while one was open for 28% -> 1% of each run, Pallas kernels for 0% -> 31%
where the time goes in v3:
time: 109 us
  waiting for transfers between devices  43.4 us (40%)
  Pallas kernels  36.6 us (34%)
  starting transfers between devices  26.4 us (24%)
    pallas_call x28, Pallas kernels, kernel(): pl.pallas_call(inner, name=name, in_specs=[spec(pltpu.SMEM)] * len(smem)...  36.6 us
    ppermute x1, waiting for transfers between devices, shards(): n3 = lax.ppermute(n3, 'head', neighbours)  17.9 us
    ppermute x1, waiting for transfers between devices, shards(): n2 = lax.ppermute(n2, 'head', neighbours)  14.3 us
    ppermute x4, starting transfers between devices, exchange(): others.append(lax.ppermute(total, 'ctx', pairs))  8.05 us
    ppermute x1, starting transfers between devices, shards(): g1 = lax.ppermute(grad, 'head', neighbours)  5.85 us
    ppermute x1, starting transfers between devices, shards(): n4 = lax.ppermute(s1, 'head', neighbours)  3.71 us
    ppermute x1, starting transfers between devices, shards(): n3 = lax.ppermute(n3, 'head', neighbours)  3.69 us
    ppermute x4, waiting for transfers between devices, exchange(): others.append(lax.ppermute(total, 'ctx', pairs))  3.22 us
  transfers between devices with their start and end apart: 16, of which 11 were waited for; matrix products, arithmetic and copies ran while one was open for 1% of the time, Pallas kernels for 31%

profile of v3, /device:TPU:0, one launch (start us, length us, event | category | flops | bytes accessed | tf_op | source)
XLA Modules:
  0.0 108.9 jit_solution(14384515787280239825)
XLA Ops:
  1.4 5.8 %collective-permute-start.4 = (bf16[512,1024]{1,0:T(8,128)(2,1)}, bf16[512,1024]{1,0:T(8,128)(2,1)S(1)}, u32[]{:S(2)}, u32[]{:S(2)}) collective-permute-start(bf16[512,1024]{1,0:T(8,128)(2,1)} %refs_2_.12), channel_id=1, source_target_pairs={{0,1},{1,0},{2,3},{3,2},{4,5},{5,4},{6,7},{7,6},{8,9},{9,8},{10,11... | collective-permute-start | bytes 3145736 | tf_op jit(solution)/shard_map/ppermute | solution.py:412
  11.6 1.6 %collective-permute-start.1 = (bf16[4,128,128]{2,1,0:T(8,128)(2,1)S(1)}, bf16[4,128,128]{2,1,0:T(8,128)(2,1)S(1)}, u32[]{:S(2)}, u32[]{:S(2)}) collective-permute-start(bf16[4,128,128]{2,1,0:T(8,128)(2,1)S(1)} %pair_total.2.refs_4_.refs_2_), channel_id=1, source_target_pairs={{0,8},{4,12},{8,0},{12,4},{16,24},{20,28},{24,16},{28,20},{1,9},{5... | collective-permute-start | bytes 393224 | tf_op jit(solution)/shard_map/ppermute | solution.py:193
  13.1 2.5 %intra.1.refs_3_.refs_5_ = f32[512,1024]{1,0:T(8,128)S(1)} custom-call(s32[512,128]{1,0:T(8,128)S(1)} %get-tuple-element.44.refs_0_, bf16[512,1024]{1,0:T(8,128)(2,1)S(1)} %copy-done.3, bf16[512,1024]{1,0:T(8,128)(2,1)S(1)} %copy-done.1, bf16[512,1024]{1,0:T(8,128)(2,1)S(1)} %copy-done.2, bf16[4,128,128]{2,1,0:T(8,128)(2,1)S(1)} %pair_total.2.refs_4_.refs_2_), custom_call_target="tpu_custom_call" | custom-call | flops 300000000 | tf_op jit(solution)/shard_map/intra/pallas_call | solution.py:35
  15.6 1.6 %collective-permute-done.1.refs_1_ = bf16[4,128,128]{2,1,0:T(8,128)(2,1)S(1)} collective-permute-done((bf16[4,128,128]{2,1,0:T(8,128)(2,1)S(1)}, bf16[4,128,128]{2,1,0:T(8,128)(2,1)S(1)}, u32[]{:S(2)}, u32[]{:S(2)}) %collective-permute-start.1) | collective-permute-done | bytes 131104 | tf_op jit(solution)/shard_map/ppermute | solution.py:193
  17.3 3.4 %collective-permute-start.2 = (bf16[4,128,128]{2,1,0:T(8,128)(2,1)S(1)}, bf16[4,128,128]{2,1,0:T(8,128)(2,1)S(1)}, u32[]{:S(2)}, u32[]{:S(2)}) collective-permute-start(bf16[4,128,128]{2,1,0:T(8,128)(2,1)S(1)} %get-tuple-element.45), channel_id=1, source_target_pairs={{0,16},{4,20},{8,24},{12,28},{1,17},{5,21},{9,25},{13,29},{2,18},{... | collective-permute-start | bytes 393224 | tf_op jit(solution)/shard_map/ppermute | solution.py:193
  20.7 1.8 %back_own.1.refs_5_.refs_3_ = f32[512,1024]{1,0:T(8,128)S(1)} custom-call(s32[7]{0:T(128)S(1)} %pad_add_fusion.refs_0_, bf16[1024,4096]{1,0:T(8,128)(2,1)S(1)} %copy-done, bf16[512,1024]{1,0:T(8,128)(2,1)S(1)} %copy-done.4, f32[512,1024]{1,0:T(8,128)S(1)} %intra.1.refs_3_.refs_5_), custom_call_target="tpu_custom_call" | custom-call | flops 180000000 | tf_op jit(solution)/shard_map/back_own/pallas_call | solution.py:35
  25.8 1.8 %project_3.1.refs_3_.refs_1_.refs_2_ = bf16[512,1024]{1,0:T(8,128)(2,1)S(1)} custom-call(s32[7]{0:T(128)S(1)} %pad_add_fusion.refs_0_, bf16[512,1024]{1,0:T(8,128)(2,1)S(1)} %get-tuple-element.49.refs_1_, bf16[1024,4096]{1,0:T(8,128)(2,1)S(1)} %copy-done), custom_call_target="tpu_custom_call" | custom-call | flops 180000000 | tf_op jit(solution)/shard_map/project_3/pallas_call | solution.py:35
  27.6 2.7 %collective-permute-done.4.refs_3_.refs_2_ = bf16[512,1024]{1,0:T(8,128)(2,1)S(1)} collective-permute-done((bf16[512,1024]{1,0:T(8,128)(2,1)}, bf16[512,1024]{1,0:T(8,128)(2,1)S(1)}, u32[]{:S(2)}, u32[]{:S(2)}) %collective-permute-start.4) | collective-permute-done | bytes 1048608 | tf_op jit(solution)/shard_map/ppermute | solution.py:412
  30.7 1.8 %collective-permute-start.6 = (bf16[512,1024]{1,0:T(8,128)(2,1)S(1)}, bf16[512,1024]{1,0:T(8,128)(2,1)S(1)}, u32[]{:S(2)}, u32[]{:S(2)}) collective-permute-start(bf16[512,1024]{1,0:T(8,128)(2,1)S(1)} %pick.3), channel_id=1, source_target_pairs={{0,1},{1,0},{2,3},{3,2},{4,5},{5,4},{6,7},{7,6},{8,9},{9,8},{10,11... | collective-permute-start | bytes 3145736 | tf_op jit(solution)/shard_map/ppermute | solution.py:429
  33.3 1.8 %project_2.1.refs_3_.refs_2_ = bf16[512,1024]{1,0:T(8,128)(2,1)S(1)} custom-call(s32[7]{0:T(128)S(1)} %pad_add_fusion.refs_0_, bf16[512,1024]{1,0:T(8,128)(2,1)S(1)} %get-tuple-element.49.refs_1_, bf16[1024,4096]{1,0:T(8,128)(2,1)S(1)} %copy-done, bf16[512,1024]{1,0:T(8,128)(2,1)S(1)} %project_3.1.refs_3_.refs_1_.refs_2_), custom_call_target="tpu_custom_call" | custom-call | flops 180000000 | tf_op jit(solution)/shard_map/project_2/pallas_call | solution.py:35
  35.1 1.8 %project_1.1.refs_3_ = bf16[512,1024]{1,0:T(8,128)(2,1)S(1)} custom-call(s32[7]{0:T(128)S(1)} %pad_add_fusion.refs_0_, bf16[512,1024]{1,0:T(8,128)(2,1)S(1)} %get-tuple-element.49.refs_1_, bf16[1024,4096]{1,0:T(8,128)(2,1)S(1)} %copy-done, bf16[512,1024]{1,0:T(8,128)(2,1)S(1)} %project_2.1.refs_3_.refs_2_), custom_call_target="tpu_custom_call" | custom-call | flops 180000000 | tf_op jit(solution)/shard_map/project_1/pallas_call | solution.py:35
  36.9 1.8 %project_0.1.refs_4_.refs_0_ = bf16[512,1024]{1,0:T(8,128)(2,1)S(1)} custom-call(s32[7]{0:T(128)S(1)} %pad_add_fusion.refs_0_, bf16[512,1024]{1,0:T(8,128)(2,1)S(1)} %get-tuple-element.49.refs_1_, bf16[1024,4096]{1,0:T(8,128)(2,1)S(1)} %copy-done, bf16[512,1024]{1,0:T(8,128)(2,1)S(1)} %project_1.1.refs_3_), custom_call_target="tpu_custom_call" | custom-call | flops 180000000 | tf_op jit(solution)/shard_map/project_0/pallas_call | solution.py:35
  38.7 1.8 %back_1.1.refs_4_.refs_3_ = f32[512,1024]{1,0:T(8,128)S(1)} custom-call(s32[7]{0:T(128)S(1)} %pad_add_fusion.refs_0_, bf16[1024,4096]{1,0:T(8,128)(2,1)S(1)} %copy-done, bf16[512,1024]{1,0:T(8,128)(2,1)S(1)} %collective-permute-done.4.refs_3_.refs_2_, f32[512,1024]{1,0:T(8,128)S(1)} %back_own.1.refs_5_.refs_3_, bf16[512,1024]{1,0:T(8,128)(2,1)S(1)} %project_0.1.refs_4_.refs_0_), custom_call_target="tpu_custom_call" | custom-call | flops 180000000 | tf_op jit(solution)/shard_map/back_1/pallas_call | solution.py:35
  40.6 14.3 %collective-permute-done.6.refs_1_ = bf16[512,1024]{1,0:T(8,128)(2,1)S(1)} collective-permute-done((bf16[512,1024]{1,0:T(8,128)(2,1)S(1)}, bf16[512,1024]{1,0:T(8,128)(2,1)S(1)}, u32[]{:S(2)}, u32[]{:S(2)}) %collective-permute-start.6) | collective-permute-done | bytes 1048608 | tf_op jit(solution)/shard_map/ppermute | solution.py:429
  55.4 3.7 %collective-permute-start.8 = (bf16[512,1024]{1,0:T(8,128)(2,1)S(1)}, bf16[512,1024]{1,0:T(8,128)(2,1)S(1)}, u32[]{:S(2)}, u32[]{:S(2)}) collective-permute-start(bf16[512,1024]{1,0:T(8,128)(2,1)S(1)} %get-tuple-element.52), channel_id=1, source_target_pairs={{0,1},{1,0},{2,3},{3,2},{4,5},{5,4},{6,7},{7,6},{8,9},{9,8},{10,11... | collective-permute-start | bytes 3145736 | tf_op jit(solution)/shard_map/ppermute | solution.py:437
  60.5 1.8 %back_2.1.refs_4_.refs_3_ = f32[512,1024]{1,0:T(8,128)S(1)} custom-call(s32[7]{0:T(128)S(1)} %pad_add_fusion.refs_0_, bf16[1024,4096]{1,0:T(8,128)(2,1)S(1)} %copy-done, bf16[512,1024]{1,0:T(8,128)(2,1)S(1)} %pick.4.refs_2_, f32[512,1024]{1,0:T(8,128)S(1)} %back_1.1.refs_4_.refs_3_), custom_call_target="tpu_custom_call" | custom-call | flops 180000000 | tf_op jit(solution)/shard_map/back_2/pallas_call | solution.py:35
  62.3 17.9 %collective-permute-done.8.refs_0_.refs_1_ = bf16[512,1024]{1,0:T(8,128)(2,1)S(1)} collective-permute-done((bf16[512,1024]{1,0:T(8,128)(2,1)S(1)}, bf16[512,1024]{1,0:T(8,128)(2,1)S(1)}, u32[]{:S(2)}, u32[]{:S(2)}) %collective-permute-start.8) | collective-permute-done | bytes 1048608 | tf_op jit(solution)/shard_map/ppermute | solution.py:437
  80.4 3.7 %collective-permute-start.10 = (bf16[512,1024]{1,0:T(8,128)(2,1)S(1)}, bf16[512,1024]{1,0:T(8,128)(2,1)S(1)}, u32[]{:S(2)}, u32[]{:S(2)}) collective-permute-start(bf16[512,1024]{1,0:T(8,128)(2,1)S(1)} %get-tuple-element.54.refs_3_.refs_9_), channel_id=1, source_target_pairs={{0,1},{1,0},{2,3},{3,2},{4,5},{5,4},{6,7},{7,6},{8,9},{9,8},{10,11... | collective-permute-start | bytes 3145736 | tf_op jit(solution)/shard_map/ppermute | solution.py:441
  85.3 4.1 %attended_grads.1 = (bf16[512,1024]{1,0:T(8,128)(2,1)S(1)}, bf16[4,128,128]{2,1,0:T(8,128)(2,1)S(1)}, bf16[4,128,128]{2,1,0:T(8,128)(2,1)S(1)}) custom-call(s32[7]{0:T(128)S(1)} %pad_add_fusion.refs_0_, bf16[1024,4096]{1,0:T(8,128)(2,1)S(1)} %copy-done, bf16[512,1024]{1,0:T(8,128)(2,1)S(1)} %pick.5.refs_2_, f32[512,1024]{1,0:T(8,128)S(1)} %back_2.1.refs_4_.refs_3_, ...), custom_call_target="tpu_custom_call" | custom-call | flops 410000000 | tf_op jit(solution)/shard_map/attended_grads/pallas_call | solution.py:35
  90.9 1.6 %collective-permute-start.12 = (bf16[4,128,128]{2,1,0:T(8,128)(2,1)S(1)}, bf16[4,128,128]{2,1,0:T(8,128)(2,1)S(1)}, u32[]{:S(2)}, u32[]{:S(2)}) collective-permute-start(bf16[4,128,128]{2,1,0:T(8,128)(2,1)S(1)} %pair_total.3.refs_8_.refs_2_), channel_id=1, source_target_pairs={{0,8},{4,12},{8,0},{12,4},{16,24},{20,28},{24,16},{28,20},{1,9},{5... | collective-permute-start | bytes 393224 | tf_op jit(solution)/shard_map/ppermute | solution.py:193
  92.4 3.8 %query_grad.1 = (bf16[512,1024]{1,0:T(8,128)(2,1)}, f32[8,128]{1,0:T(8,128)S(1)}) custom-call(s32[512,128]{1,0:T(8,128)S(1)} %get-tuple-element.44.refs_0_, f32[32,128]{1,0:T(8,128)S(1)} %get-tuple-element.39.refs_0_.refs_7_.refs_1_, f32[512,128]{1,0:T(8,128)S(1)} %get-tuple-element.40.refs_1_.refs_8_.refs_2_, bf16[512,1024]{1,0:T(8,128)(2,1)S(1)} %copy-done.1, ...), custom_call_target="tpu_custom_call" | custom-call | flops 300000000 | tf_op jit(solution)/shard_map/query_grad/pallas_call | solution.py:35
  96.5 1.5 %collective-permute-start.13 = (bf16[4,128,128]{2,1,0:T(8,128)(2,1)S(1)}, bf16[4,128,128]{2,1,0:T(8,128)(2,1)S(1)}, u32[]{:S(2)}, u32[]{:S(2)}) collective-permute-start(bf16[4,128,128]{2,1,0:T(8,128)(2,1)S(1)} %get-tuple-element.62.refs_5_), channel_id=1, source_target_pairs={{16,0},{20,4},{24,8},{28,12},{17,1},{21,5},{25,9},{29,13},{18,2},{... | collective-permute-start | bytes 393224 | tf_op jit(solution)/shard_map/ppermute | solution.py:193
  98.1 4.7 %key_value_grads.1 = (f32[512,1024]{1,0:T(8,128)S(1)}, f32[512,1024]{1,0:T(8,128)S(1)}) custom-call(s32[8,512]{1,0:T(8,128)S(1)} %get-tuple-element.64.refs_0_, bf16[512,1024]{1,0:T(8,128)(2,1)S(1)} %copy-done.3, bf16[512,1024]{1,0:T(8,128)(2,1)S(1)} %copy-done.1, bf16[512,1024]{1,0:T(8,128)(2,1)S(1)} %copy-done.2, ...), custom_call_target="tpu_custom_call" | custom-call | flops 500000000 | tf_op jit(solution)/shard_map/key_value_grads/pallas_call | solution.py:35
  105.0 2.4 %last_grads.1 = (bf16[512,1024]{1,0:T(8,128)(2,1)}, bf16[512,1024]{1,0:T(8,128)(2,1)}, f32[8,128]{1,0:T(8,128)S(1)}) custom-call(f32[32,128]{1,0:T(8,128)S(1)} %get-tuple-element.39.refs_0_.refs_7_.refs_1_, f32[512,128]{1,0:T(8,128)S(1)} %get-tuple-element.41.refs_1_, bf16[512,1024]{1,0:T(8,128)(2,1)S(1)} %copy-done.1, bf16[512,1024]{1,0:T(8,128)(2,1)S(1)} %copy-done.2, ...), custom_call_target="tpu_custom_call" | custom-call | flops 250000000 | tf_op jit(solution)/shard_map/last_grads/pallas_call | solution.py:35
  (47 shorter events, 18.3 us)
Async XLA Ops:
  0.6 27.0 %collective-permute-start.5 = (bf16[512,1024]{1,0:T(8,128)(2,1)}, bf16[512,1024]{1,0:T(8,128)(2,1)S(1)}, u32[]{:S(2)}, u32[]{:S(2)}) collective-permute-start(bf16[512,1024]{1,0:T(8,128)(2,1)} %refs_2_.12), channel_id=1, source_target_pairs={{1,2},{2,1},{5,6},{6,5},{9,10},{10,9},{13,14},{14,13},{17,18},{18,... | collective-permute-start | bytes 3145736 | tf_op jit(solution)/shard_map/ppermute | solution.py:413
  1.4 28.9 %collective-permute-start.4 = (bf16[512,1024]{1,0:T(8,128)(2,1)}, bf16[512,1024]{1,0:T(8,128)(2,1)S(1)}, u32[]{:S(2)}, u32[]{:S(2)}) collective-permute-start(bf16[512,1024]{1,0:T(8,128)(2,1)} %refs_2_.12), channel_id=1, source_target_pairs={{0,1},{1,0},{2,3},{3,2},{4,5},{5,4},{6,7},{7,6},{8,9},{9,8},{10,11... | collective-permute-start | bytes 3145736 | tf_op jit(solution)/shard_map/ppermute | solution.py:412
  7.9 1.2 %copy-start.1 = (bf16[512,1024]{1,0:T(8,128)(2,1)S(1)}, bf16[512,1024]{1,0:T(8,128)(2,1)}, u32[]{:S(2)}) copy-start(bf16[512,1024]{1,0:T(8,128)(2,1)} %refs_2_.19) | copy-start | bytes 3145732
  7.9 1.5 %copy-start.2 = (bf16[512,1024]{1,0:T(8,128)(2,1)S(1)}, bf16[512,1024]{1,0:T(8,128)(2,1)}, u32[]{:S(2)}) copy-start(bf16[512,1024]{1,0:T(8,128)(2,1)} %refs_3_.9) | copy-start | bytes 3145732
  8.7 4.4 %copy-start.3 = (bf16[512,1024]{1,0:T(8,128)(2,1)S(1)}, bf16[512,1024]{1,0:T(8,128)(2,1)}, u32[]{:S(2)}) copy-start(bf16[512,1024]{1,0:T(8,128)(2,1)} %refs_1_.11) | copy-start | bytes 3145732
  9.5 11.2 %copy-start.4 = (bf16[512,1024]{1,0:T(8,128)(2,1)S(1)}, bf16[512,1024]{1,0:T(8,128)(2,1)}, u32[]{:S(2)}) copy-start(bf16[512,1024]{1,0:T(8,128)(2,1)} %refs_2_.12) | copy-start | bytes 3145732
  10.1 1.4 %collective-permute-start = (bf16[4,128,128]{2,1,0:T(8,128)(2,1)S(1)}, bf16[4,128,128]{2,1,0:T(8,128)(2,1)S(1)}, u32[]{:S(2)}, u32[]{:S(2)}) collective-permute-start(bf16[4,128,128]{2,1,0:T(8,128)(2,1)S(1)} %get-tuple-element.43), channel_id=1, source_target_pairs={{0,4},{4,0},{8,12},{12,8},{16,20},{20,16},{24,28},{28,24},{1,5},{5... | collective-permute-start | bytes 393224 | tf_op jit(solution)/shard_map/ppermute | solution.py:176
  11.5 9.2 %copy-start = (bf16[1024,4096]{1,0:T(8,128)(2,1)S(1)}, bf16[1024,4096]{1,0:T(8,128)(2,1)}, u32[]{:S(2)}) copy-start(bf16[1024,4096]{1,0:T(8,128)(2,1)} %refs_1_.10) | copy-start | bytes 25165828
  11.6 5.6 %collective-permute-start.1 = (bf16[4,128,128]{2,1,0:T(8,128)(2,1)S(1)}, bf16[4,128,128]{2,1,0:T(8,128)(2,1)S(1)}, u32[]{:S(2)}, u32[]{:S(2)}) collective-permute-start(bf16[4,128,128]{2,1,0:T(8,128)(2,1)S(1)} %pair_total.2.refs_4_.refs_2_), channel_id=1, source_target_pairs={{0,8},{4,12},{8,0},{12,4},{16,24},{20,28},{24,16},{28,20},{1,9},{5... | collective-permute-start | bytes 393224 | tf_op jit(solution)/shard_map/ppermute | solution.py:193
  17.3 5.9 %collective-permute-start.2 = (bf16[4,128,128]{2,1,0:T(8,128)(2,1)S(1)}, bf16[4,128,128]{2,1,0:T(8,128)(2,1)S(1)}, u32[]{:S(2)}, u32[]{:S(2)}) collective-permute-start(bf16[4,128,128]{2,1,0:T(8,128)(2,1)S(1)} %get-tuple-element.45), channel_id=1, source_target_pairs={{0,16},{4,20},{8,24},{12,28},{1,17},{5,21},{9,25},{13,29},{2,18},{... | collective-permute-start | bytes 393224 | tf_op jit(solution)/shard_map/ppermute | solution.py:193
  23.3 1.4 %collective-permute-start.3 = (bf16[4,128,128]{2,1,0:T(8,128)(2,1)S(1)}, bf16[4,128,128]{2,1,0:T(8,128)(2,1)S(1)}, u32[]{:S(2)}, u32[]{:S(2)}) collective-permute-start(bf16[4,128,128]{2,1,0:T(8,128)(2,1)S(1)} %get-tuple-element.48), channel_id=1, source_target_pairs={{0,4},{4,0},{8,12},{12,8},{16,20},{20,16},{24,28},{28,24},{1,5},{5... | collective-permute-start | bytes 393224 | tf_op jit(solution)/shard_map/ppermute | solution.py:207
  30.7 24.1 %collective-permute-start.6 = (bf16[512,1024]{1,0:T(8,128)(2,1)S(1)}, bf16[512,1024]{1,0:T(8,128)(2,1)S(1)}, u32[]{:S(2)}, u32[]{:S(2)}) collective-permute-start(bf16[512,1024]{1,0:T(8,128)(2,1)S(1)} %pick.3), channel_id=1, source_target_pairs={{0,1},{1,0},{2,3},{3,2},{4,5},{5,4},{6,7},{7,6},{8,9},{9,8},{10,11... | collective-permute-start | bytes 3145736 | tf_op jit(solution)/shard_map/ppermute | solution.py:429
  32.5 22.3 %collective-permute-start.7 = (bf16[512,1024]{1,0:T(8,128)(2,1)S(1)}, bf16[512,1024]{1,0:T(8,128)(2,1)S(1)}, u32[]{:S(2)}, u32[]{:S(2)}) collective-permute-start(bf16[512,1024]{1,0:T(8,128)(2,1)S(1)} %collective-permute-done.4.refs_3_.refs_2_), channel_id=1, source_target_pairs={{1,2},{2,1},{5,6},{6,5},{9,10},{10,9},{13,14},{14,13},{17,18},{18,... | collective-permute-start | bytes 3145736 | tf_op jit(solution)/shard_map/ppermute | solution.py:430
  55.4 24.8 %collective-permute-start.8 = (bf16[512,1024]{1,0:T(8,128)(2,1)S(1)}, bf16[512,1024]{1,0:T(8,128)(2,1)S(1)}, u32[]{:S(2)}, u32[]{:S(2)}) collective-permute-start(bf16[512,1024]{1,0:T(8,128)(2,1)S(1)} %get-tuple-element.52), channel_id=1, source_target_pairs={{0,1},{1,0},{2,3},{3,2},{4,5},{5,4},{6,7},{7,6},{8,9},{9,8},{10,11... | collective-permute-start | bytes 3145736 | tf_op jit(solution)/shard_map/ppermute | solution.py:437
  59.1 21.1 %collective-permute-start.9 = (bf16[512,1024]{1,0:T(8,128)(2,1)S(1)}, bf16[512,1024]{1,0:T(8,128)(2,1)S(1)}, u32[]{:S(2)}, u32[]{:S(2)}) collective-permute-start(bf16[512,1024]{1,0:T(8,128)(2,1)S(1)} %get-tuple-element.53.refs_3_), channel_id=1, source_target_pairs={{1,2},{2,1},{5,6},{6,5},{9,10},{10,9},{13,14},{14,13},{17,18},{18,... | collective-permute-start | bytes 3145736 | tf_op jit(solution)/shard_map/ppermute | solution.py:436
  80.4 27.0 %collective-permute-start.10 = (bf16[512,1024]{1,0:T(8,128)(2,1)S(1)}, bf16[512,1024]{1,0:T(8,128)(2,1)S(1)}, u32[]{:S(2)}, u32[]{:S(2)}) collective-permute-start(bf16[512,1024]{1,0:T(8,128)(2,1)S(1)} %get-tuple-element.54.refs_3_.refs_9_), channel_id=1, source_target_pairs={{0,1},{1,0},{2,3},{3,2},{4,5},{5,4},{6,7},{7,6},{8,9},{9,8},{10,11... | collective-permute-start | bytes 3145736 | tf_op jit(solution)/shard_map/ppermute | solution.py:441
  84.1 23.6 %collective-permute-start.15 = (bf16[512,1024]{1,0:T(8,128)(2,1)S(1)}, bf16[512,1024]{1,0:T(8,128)(2,1)S(1)}, u32[]{:S(2)}, u32[]{:S(2)}) collective-permute-start(bf16[512,1024]{1,0:T(8,128)(2,1)S(1)} %get-tuple-element.70), channel_id=1, source_target_pairs={{1,2},{2,1},{5,6},{6,5},{9,10},{10,9},{13,14},{14,13},{17,18},{18,... | collective-permute-start | bytes 3145736 | tf_op jit(solution)/shard_map/ppermute | solution.py:442
  89.4 1.4 %collective-permute-start.11 = (bf16[4,128,128]{2,1,0:T(8,128)(2,1)S(1)}, bf16[4,128,128]{2,1,0:T(8,128)(2,1)S(1)}, u32[]{:S(2)}, u32[]{:S(2)}) collective-permute-start(bf16[4,128,128]{2,1,0:T(8,128)(2,1)S(1)} %get-tuple-element.59), channel_id=1, source_target_pairs={{0,4},{4,0},{8,12},{12,8},{16,20},{20,16},{24,28},{28,24},{1,5},{5... | collective-permute-start | bytes 393224 | tf_op jit(solution)/shard_map/ppermute | solution.py:176
  90.9 5.6 %collective-permute-start.12 = (bf16[4,128,128]{2,1,0:T(8,128)(2,1)S(1)}, bf16[4,128,128]{2,1,0:T(8,128)(2,1)S(1)}, u32[]{:S(2)}, u32[]{:S(2)}) collective-permute-start(bf16[4,128,128]{2,1,0:T(8,128)(2,1)S(1)} %pair_total.3.refs_8_.refs_2_), channel_id=1, source_target_pairs={{0,8},{4,12},{8,0},{12,4},{16,24},{20,28},{24,16},{28,20},{1,9},{5... | collective-permute-start | bytes 393224 | tf_op jit(solution)/shard_map/ppermute | solution.py:193
  96.5 6.9 %collective-permute-start.13 = (bf16[4,128,128]{2,1,0:T(8,128)(2,1)S(1)}, bf16[4,128,128]{2,1,0:T(8,128)(2,1)S(1)}, u32[]{:S(2)}, u32[]{:S(2)}) collective-permute-start(bf16[4,128,128]{2,1,0:T(8,128)(2,1)S(1)} %get-tuple-element.62.refs_5_), channel_id=1, source_target_pairs={{16,0},{20,4},{24,8},{28,12},{17,1},{21,5},{25,9},{29,13},{18,2},{... | collective-permute-start | bytes 393224 | tf_op jit(solution)/shard_map/ppermute | solution.py:193
  103.6 1.4 %collective-permute-start.14 = (bf16[4,128,128]{2,1,0:T(8,128)(2,1)S(1)}, bf16[4,128,128]{2,1,0:T(8,128)(2,1)S(1)}, u32[]{:S(2)}, u32[]{:S(2)}) collective-permute-start(bf16[4,128,128]{2,1,0:T(8,128)(2,1)S(1)} %get-tuple-element.67), channel_id=1, source_target_pairs={{0,4},{4,0},{8,12},{12,8},{16,20},{20,16},{24,28},{28,24},{1,5},{5... | collective-permute-start | bytes 393224 | tf_op jit(solution)/shard_map/ppermute | solution.py:207

commit v4 on v3

--- a/solution.py
+++ b/solution.py
@@ -18,7 +18,7 @@
     "setup": 100.0, "local_states": 0.8, "intra": 3.0, "back_own": 1.8, "pair_total": 0.1, "exchange_stage": 0.1,
     "exchange_last": 0.1, "normalise": 0.9, "project_3": 1.8, "project_2": 1.8, "project_1": 1.8,
     "project_0": 1.8, "back_1": 1.8, "pick": 0.3, "turn": 0.5, "back_2": 1.8, "attended_grads": 4.1,
-    "query_grad": 3.0, "key_value_grads": 5.0, "last_grads": 2.5, "mixed": 1.3,
+    "query_grad": 0.01, "key_value_grads": 0.01, "last_grads": 0.01, "mixed": 1.3,
 }
 
 I_BLK, I_CORE, I_Z, I_DOCS = 0, 1, 2, 3
@@ -374,14 +374,48 @@
         out_ref[:, head(i)] = a_ref[:, head(i)] * end + b_ref[:, head(i)]
 
 
-def turn_body(c_ref, n2_ref, p2_ref, i2_ref, s2_ref, n3_ref):
-    s2_ref[...] = p2_ref[...] + n2_ref[...]
-    end_body(c_ref, p2_ref, i2_ref, n3_ref)
-
-
-def turn_again_body(n3_ref, i3_ref, p3_ref, p1_ref, s3_ref, s1_ref):
-    s3_ref[...] = p3_ref[...] + n3_ref[...]
-    s1_ref[...] = p1_ref[...] + i3_ref[...]
+def first_body(c_ref, g1_ref, p3_ref, g3_ref, *out_refs):
+    r0 = 0
+    for n_ref, i_ref in zip(out_refs[::2], out_refs[1::2], strict=True):
+        rows = slice(r0, r0 + n_ref.shape[0])
+        i_ref[...] = g1_ref[rows, :]
+        end_body(c_ref, p3_ref.at[rows, :], g3_ref.at[rows, :], n_ref)
+        r0 = rows.stop
+
+
+def ends_body(c_ref, *refs):
+    out_ref = refs[-1]
+    r0 = 0
+    for a_ref, b_ref in zip(refs[:-1:2], refs[1:-1:2], strict=True):
+        rows = slice(r0, r0 + a_ref.shape[0])
+        end_body(c_ref, a_ref, b_ref, out_ref.at[rows, :])
+        r0 = rows.stop
+
+
+def ends_whole_body(c_ref, a0_ref, a1_ref, b_ref, out_ref):
+    r1 = a0_ref.shape[0]
+    end_body(c_ref, a0_ref, b_ref.at[:r1, :], out_ref.at[:r1, :])
+    end_body(c_ref, a1_ref, b_ref.at[r1:, :], out_ref.at[r1:, :])
+
+
+def turn_body(rows, c_ref, n2_ref, p2_ref, i2_ref, s2_ref, n3_ref):
+    s2_ref[...] = p2_ref[rows, :] + n2_ref[...]
+    end_body(c_ref, p2_ref.at[rows, :], i2_ref, n3_ref)
+
+
+def turn_again_body(rows, n3_ref, i3_ref, p3_ref, p1_ref, s3_ref, s1_ref):
+    s3_ref[...] = p3_ref[rows, :] + n3_ref[...]
+    s1_ref[...] = p1_ref[rows, :] + i3_ref[...]
+
+
+def mixed_body(p_ref, *refs):
+    out_ref = refs[-1]
+    r0 = 0
+    for a_ref, b_ref in zip(refs[:-1:2], refs[1:-1:2], strict=True):
+        rows = slice(r0, r0 + a_ref.shape[0])
+        total = p_ref[rows, :].astype(F32) + a_ref[...].astype(F32) + b_ref[...].astype(F32)
+        out_ref[rows, :] = total.astype(BF16)
+        r0 = rows.stop
 
 
 def shards(q, k, v, lens, w, grad):
@@ -423,28 +457,44 @@
     normed_f, inv, normed = kernel(
         norm_body, "normalise", [], [coef, cin, q, own, other, inside], [wide_f, wide_f, wide_b]
     )
+    lot = like((tok // 2, width), BF16)
+    rows = [slice(0, tok // 2), slice(tok // 2, tok)]
+
+    def both(arrays, kind):
+        return [lax.ppermute(a, "head", kind) for a in arrays]
+
+    def turn(h, deps):
+        return kernel(functools.partial(turn_body, rows[h]), "turn", [], [coef, n2[h], p2, i2[h]], [lot, lot], deps)
+
+    def turn_again(h, deps):
+        return kernel(functools.partial(turn_again_body, rows[h]), "turn", [], [n3[h], i3[h], p3, p1], [lot, lot], deps)
+
     p3 = project(3, "project_3")
     g1, g3_inner, _ = lax.optimization_barrier((g1, g3_inner, p3))
-    (n2,) = kernel(end_body, "pick", [], [coef, p3, g3_inner], [part], [g1])
-    n2 = lax.ppermute(n2, "head", neighbours)
-    i2 = lax.ppermute(g1, "head", inner)
+    n2a, i2a, n2b, i2b = kernel(first_body, "pick", [], [coef, g1, p3, g3_inner], [lot] * 4)
+    n2a, i2a = lax.ppermute(n2a, "head", neighbours), lax.ppermute(i2a, "head", inner)
+    n2b, i2b = lax.ppermute(n2b, "head", neighbours), lax.ppermute(i2b, "head", inner)
+    n2, i2 = [n2a, n2b], [i2a, i2b]
     p2 = project(2, "project_2", [p3])
-    p1 = project(1, "project_1", [p2])
+    s2a, n3a = turn(0, [])
+    i3a, n3a = lax.ppermute(s2a, "head", inner), lax.ppermute(n3a, "head", neighbours)
+    p1 = project(1, "project_1", [s2a])
     p0 = project(0, "project_0", [p1])
     base = back_project([1], "back_1", [g1], base, [p0])
-    s2, n3 = kernel(turn_body, "turn", [], [coef, n2, p2, i2], [part, part], [base])
-    i3 = lax.ppermute(s2, "head", inner)
-    n3 = lax.ppermute(n3, "head", neighbours)
-    (g2,) = kernel(end_body, "pick", [], [coef, n2, i2], [part], [s2])
+    s2b, n3b = turn(1, [base])
+    i3b, n3b = lax.ppermute(s2b, "head", inner), lax.ppermute(n3b, "head", neighbours)
+    n3, i3 = [n3a, n3b], [i3a, i3b]
+    (g2,) = kernel(ends_body, "pick", [], [coef, n2a, i2a, n2b, i2b], [part], [s2b])
     base = back_project([2], "back_2", [g2], base)
-    s3, s1 = kernel(turn_again_body, "turn", [], [n3, i3, p3, p1], [part, part], [base])
-    n4 = lax.ppermute(s1, "head", neighbours)
-    i4 = lax.ppermute(s3, "head", inner)
-    (g3,) = kernel(end_body, "pick", [], [coef, n3, g3_inner], [part], [s1])
+    s3a, s1a = turn_again(0, [base])
+    n4a, i4a = lax.ppermute(s1a, "head", neighbours), lax.ppermute(s3a, "head", inner)
+    (g3,) = kernel(ends_whole_body, "pick", [], [coef, n3a, n3b, g3_inner], [part], [s1a])
     ag, gsend, gkeep = kernel(
         functools.partial(att_grad_body, 3), "attended_grads", [info],
-        [w, g3, base, normed_f, inv, q, coef, cin], [wide_b, state, state], [s1],
+        [w, g3, base, normed_f, inv, q, coef, cin], [wide_b, state, state],
     )
+    s3b, s1b = turn_again(1, [gsend])
+    n4b, i4b = lax.ppermute(s1b, "head", neighbours), lax.ppermute(s3b, "head", inner)
     ggot, gtotal = pair_total(gsend, gkeep, coefb)
     grads = []
 
@@ -467,8 +517,7 @@
         last_body, "last_grads", [], [coef, cout, k, v, leaving, leaving_other, kp, vp],
         [wide_b, wide_b, like((8, DH), F32)],
     )
-    (mixed,) = kernel(sum_body, "turn", [], [p0, n4], [part], [mark])
-    (mixed,) = kernel(sum_body, "mixed", [], [mixed, i4], [part])
+    (mixed,) = kernel(mixed_body, "mixed", [], [p0, n4a, i4a, n4b, i4b], [part], [mark])
     return mixed, query_grad, key_grad, value_grad
 
 

time: 109 us -> 105 us (0.963)
  waiting for transfers between devices: 43.4 us -> 27.5 us
  starting transfers between devices: 26.4 us -> 38.4 us
    ppermute x6 -> x12, waiting for transfers between devices: 32.2 us -> 17.6 us  [the longest x1 7.9 us: shards(): lax.ppermute(n2a, 'head', neighbours)]
    ppermute x6 -> x12, starting transfers between devices: 11.5 us -> 23.5 us  [the longest x1 5.63 us: shards(): lax.ppermute(s1a, 'head', neighbours)]
    ppermute x2, waiting for transfers between devices: 2.67 us -> 1.34 us  [pair_total(): got = lax.ppermute(send, 'ctx', [(i, i ^ 1) for i in range(n)])]
    pallas_call x28 -> x29, Pallas kernels: 36.6 us -> 36.1 us  [kernel(): pl.pallas_call(inner, name=name, in_specs=[spec(pltpu.SMEM)] * len(smem)...]
  transfers between devices with their start and end apart: 16 -> 22, of which waited for: 11 -> 12; matrix products, arithmetic and copies ran while one was open for 1% -> 1% of each run, Pallas kernels for 31% -> 33%
where the time goes in v4:
time: 105 us
  starting transfers between devices  38.4 us (37%)
  Pallas kernels  36.1 us (34%)
  waiting for transfers between devices  27.5 us (26%)
    pallas_call x29, Pallas kernels, kernel(): pl.pallas_call(inner, name=name, in_specs=[spec(pltpu.SMEM)] * len(smem)...  36.1 us
    ppermute x4, starting transfers between devices, exchange(): others.append(lax.ppermute(total, 'ctx', pairs))  8.05 us
    ppermute x1, waiting for transfers between devices, shards(): lax.ppermute(n2a, 'head', neighbours)  7.9 us
    ppermute x1, starting transfers between devices, shards(): g1 = lax.ppermute(grad, 'head', neighbours)  5.85 us
    ppermute x1, starting transfers between devices, shards(): lax.ppermute(s1a, 'head', neighbours)  5.63 us
    ppermute x1, waiting for transfers between devices, shards(): lax.ppermute(n3b, 'head', neighbours)  4.79 us
    ppermute x1, waiting for transfers between devices, shards(): lax.ppermute(n3a, 'head', neighbours)  4.01 us
    ppermute x1, starting transfers between devices, shards(): lax.ppermute(n3a, 'head', neighbours)  3.97 us
  transfers between devices with their start and end apart: 22, of which 12 were waited for; matrix products, arithmetic and copies ran while one was open for 1% of the time, Pallas kernels for 33%

profile of v4, /device:TPU:0, one launch (start us, length us, event | category | flops | bytes accessed | tf_op | source)
XLA Modules:
  0.0 104.5 jit_solution(16307635861789862701)
XLA Ops:
  1.4 5.8 %collective-permute-start.4 = (bf16[512,1024]{1,0:T(8,128)(2,1)}, bf16[512,1024]{1,0:T(8,128)(2,1)S(1)}, u32[]{:S(2)}, u32[]{:S(2)}) collective-permute-start(bf16[512,1024]{1,0:T(8,128)(2,1)} %refs_2_.12), channel_id=1, source_target_pairs={{0,1},{1,0},{2,3},{3,2},{4,5},{5,4},{6,7},{7,6},{8,9},{9,8},{10,11... | collective-permute-start | bytes 3145736 | tf_op jit(solution)/shard_map/ppermute | solution.py:446
  13.1 2.5 %intra.1.refs_3_.refs_5_ = f32[512,1024]{1,0:T(8,128)S(1)} custom-call(s32[512,128]{1,0:T(8,128)S(1)} %get-tuple-element.52.refs_0_, bf16[512,1024]{1,0:T(8,128)(2,1)S(1)} %copy-done.3, bf16[512,1024]{1,0:T(8,128)(2,1)S(1)} %copy-done.1, bf16[512,1024]{1,0:T(8,128)(2,1)S(1)} %copy-done.2, bf16[4,128,128]{2,1,0:T(8,128)(2,1)S(1)} %pair_total.2.refs_4_.refs_2_), custom_call_target="tpu_custom_call" | custom-call | flops 300000000 | tf_op jit(solution)/shard_map/intra/pallas_call | solution.py:35
  17.3 3.4 %collective-permute-start.2 = (bf16[4,128,128]{2,1,0:T(8,128)(2,1)S(1)}, bf16[4,128,128]{2,1,0:T(8,128)(2,1)S(1)}, u32[]{:S(2)}, u32[]{:S(2)}) collective-permute-start(bf16[4,128,128]{2,1,0:T(8,128)(2,1)S(1)} %get-tuple-element.53), channel_id=1, source_target_pairs={{0,16},{4,20},{8,24},{12,28},{1,17},{5,21},{9,25},{13,29},{2,18},{... | collective-permute-start | bytes 393224 | tf_op jit(solution)/shard_map/ppermute | solution.py:193
  20.7 1.8 %back_own.1.refs_5_.refs_3_ = f32[512,1024]{1,0:T(8,128)S(1)} custom-call(s32[7]{0:T(128)S(1)} %pad_add_fusion.refs_0_, bf16[1024,4096]{1,0:T(8,128)(2,1)S(1)} %copy-done, bf16[512,1024]{1,0:T(8,128)(2,1)S(1)} %copy-done.4, f32[512,1024]{1,0:T(8,128)S(1)} %intra.1.refs_3_.refs_5_), custom_call_target="tpu_custom_call" | custom-call | flops 180000000 | tf_op jit(solution)/shard_map/back_own/pallas_call | solution.py:35
  25.8 1.8 %project_3.1.refs_2_.refs_3_ = bf16[512,1024]{1,0:T(8,128)(2,1)S(1)} custom-call(s32[7]{0:T(128)S(1)} %pad_add_fusion.refs_0_, bf16[512,1024]{1,0:T(8,128)(2,1)S(1)} %get-tuple-element.57.refs_1_, bf16[1024,4096]{1,0:T(8,128)(2,1)S(1)} %copy-done), custom_call_target="tpu_custom_call" | custom-call | flops 180000000 | tf_op jit(solution)/shard_map/project_3/pallas_call | solution.py:35
  27.7 2.7 %collective-permute-done.4.refs_1_.refs_2_ = bf16[512,1024]{1,0:T(8,128)(2,1)S(1)} collective-permute-done((bf16[512,1024]{1,0:T(8,128)(2,1)}, bf16[512,1024]{1,0:T(8,128)(2,1)S(1)}, u32[]{:S(2)}, u32[]{:S(2)}) %collective-permute-start.4) | collective-permute-done | bytes 1048608 | tf_op jit(solution)/shard_map/ppermute | solution.py:446
  30.7 1.8 %collective-permute-start.6 = (bf16[256,1024]{1,0:T(8,128)(2,1)S(1)}, bf16[256,1024]{1,0:T(8,128)(2,1)S(1)}, u32[]{:S(2)}, u32[]{:S(2)}) collective-permute-start(bf16[256,1024]{1,0:T(8,128)(2,1)S(1)} %get-tuple-element.60), channel_id=1, source_target_pairs={{0,1},{1,0},{2,3},{3,2},{4,5},{5,4},{6,7},{7,6},{8,9},{9,8},{10,11... | collective-permute-start | bytes 1572872 | tf_op jit(solution)/shard_map/ppermute | solution.py:475
  33.2 2.0 %collective-permute-start.10 = (bf16[256,1024]{1,0:T(8,128)(2,1)S(1)}, bf16[256,1024]{1,0:T(8,128)(2,1)S(1)}, u32[]{:S(2)}, u32[]{:S(2)}) collective-permute-start(bf16[256,1024]{1,0:T(8,128)(2,1)S(1)} %get-tuple-element.64), channel_id=1, source_target_pairs={{0,1},{1,0},{2,3},{3,2},{4,5},{5,4},{6,7},{7,6},{8,9},{9,8},{10,11... | collective-permute-start | bytes 1572872 | tf_op jit(solution)/shard_map/ppermute | solution.py:476
  35.9 1.8 %project_2.1.refs_2_ = bf16[512,1024]{1,0:T(8,128)(2,1)S(1)} custom-call(s32[7]{0:T(128)S(1)} %pad_add_fusion.refs_0_, bf16[512,1024]{1,0:T(8,128)(2,1)S(1)} %get-tuple-element.57.refs_1_, bf16[1024,4096]{1,0:T(8,128)(2,1)S(1)} %copy-done, bf16[512,1024]{1,0:T(8,128)(2,1)S(1)} %project_3.1.refs_2_.refs_3_), custom_call_target="tpu_custom_call" | custom-call | flops 180000000 | tf_op jit(solution)/shard_map/project_2/pallas_call | solution.py:35
  37.7 7.9 %collective-permute-done.6.refs_1_ = bf16[256,1024]{1,0:T(8,128)(2,1)S(1)} collective-permute-done((bf16[256,1024]{1,0:T(8,128)(2,1)S(1)}, bf16[256,1024]{1,0:T(8,128)(2,1)S(1)}, u32[]{:S(2)}, u32[]{:S(2)}) %collective-permute-start.6) | collective-permute-done | bytes 524320 | tf_op jit(solution)/shard_map/ppermute | solution.py:475
  45.8 4.0 %collective-permute-start.8 = (bf16[256,1024]{1,0:T(8,128)(2,1)S(1)}, bf16[256,1024]{1,0:T(8,128)(2,1)S(1)}, u32[]{:S(2)}, u32[]{:S(2)}) collective-permute-start(bf16[256,1024]{1,0:T(8,128)(2,1)S(1)} %get-tuple-element.63), channel_id=1, source_target_pairs={{0,1},{1,0},{2,3},{3,2},{4,5},{5,4},{6,7},{7,6},{8,9},{9,8},{10,11... | collective-permute-start | bytes 1572872 | tf_op jit(solution)/shard_map/ppermute | solution.py:480
  50.5 1.8 %project_1.1.refs_3_ = bf16[512,1024]{1,0:T(8,128)(2,1)S(1)} custom-call(s32[7]{0:T(128)S(1)} %pad_add_fusion.refs_0_, bf16[512,1024]{1,0:T(8,128)(2,1)S(1)} %get-tuple-element.57.refs_1_, bf16[1024,4096]{1,0:T(8,128)(2,1)S(1)} %copy-done, bf16[256,1024]{1,0:T(8,128)(2,1)S(1)} %get-tuple-element.62.refs_3_), custom_call_target="tpu_custom_call" | custom-call | flops 180000000 | tf_op jit(solution)/shard_map/project_1/pallas_call | solution.py:35
  52.3 1.8 %project_0.1.refs_4_.refs_0_ = bf16[512,1024]{1,0:T(8,128)(2,1)S(1)} custom-call(s32[7]{0:T(128)S(1)} %pad_add_fusion.refs_0_, bf16[512,1024]{1,0:T(8,128)(2,1)S(1)} %get-tuple-element.57.refs_1_, bf16[1024,4096]{1,0:T(8,128)(2,1)S(1)} %copy-done, bf16[512,1024]{1,0:T(8,128)(2,1)S(1)} %project_1.1.refs_3_), custom_call_target="tpu_custom_call" | custom-call | flops 180000000 | tf_op jit(solution)/shard_map/project_0/pallas_call | solution.py:35
  54.1 1.8 %back_1.1.refs_4_.refs_3_ = f32[512,1024]{1,0:T(8,128)S(1)} custom-call(s32[7]{0:T(128)S(1)} %pad_add_fusion.refs_0_, bf16[1024,4096]{1,0:T(8,128)(2,1)S(1)} %copy-done, bf16[512,1024]{1,0:T(8,128)(2,1)S(1)} %collective-permute-done.4.refs_1_.refs_2_, f32[512,1024]{1,0:T(8,128)S(1)} %back_own.1.refs_5_.refs_3_, bf16[512,1024]{1,0:T(8,128)(2,1)S(1)} %project_0.1.refs_4_.refs_0_), custom_call_target="tpu_custom_call" | custom-call | flops 180000000 | tf_op jit(solution)/shard_map/back_1/pallas_call | solution.py:35
  57.1 4.0 %collective-permute-start.14 = (bf16[256,1024]{1,0:T(8,128)(2,1)S(1)}, bf16[256,1024]{1,0:T(8,128)(2,1)S(1)}, u32[]{:S(2)}, u32[]{:S(2)}) collective-permute-start(bf16[256,1024]{1,0:T(8,128)(2,1)S(1)} %get-tuple-element.69), channel_id=1, source_target_pairs={{0,1},{1,0},{2,3},{3,2},{4,5},{5,4},{6,7},{7,6},{8,9},{9,8},{10,11... | collective-permute-start | bytes 1572872 | tf_op jit(solution)/shard_map/ppermute | solution.py:485
  62.2 1.8 %back_2.1.refs_4_.refs_3_ = f32[512,1024]{1,0:T(8,128)S(1)} custom-call(s32[7]{0:T(128)S(1)} %pad_add_fusion.refs_0_, bf16[1024,4096]{1,0:T(8,128)(2,1)S(1)} %copy-done, bf16[512,1024]{1,0:T(8,128)(2,1)S(1)} %pick.4.refs_2_, f32[512,1024]{1,0:T(8,128)S(1)} %back_1.1.refs_4_.refs_3_), custom_call_target="tpu_custom_call" | custom-call | flops 180000000 | tf_op jit(solution)/shard_map/back_2/pallas_call | solution.py:35
  64.1 4.0 %collective-permute-done.8.refs_0_.refs_1_ = bf16[256,1024]{1,0:T(8,128)(2,1)S(1)} collective-permute-done((bf16[256,1024]{1,0:T(8,128)(2,1)S(1)}, bf16[256,1024]{1,0:T(8,128)(2,1)S(1)}, u32[]{:S(2)}, u32[]{:S(2)}) %collective-permute-start.8) | collective-permute-done | bytes 524320 | tf_op jit(solution)/shard_map/ppermute | solution.py:480
  68.9 5.6 %collective-permute-start.12 = (bf16[256,1024]{1,0:T(8,128)(2,1)S(1)}, bf16[256,1024]{1,0:T(8,128)(2,1)S(1)}, u32[]{:S(2)}, u32[]{:S(2)}) collective-permute-start(bf16[256,1024]{1,0:T(8,128)(2,1)S(1)} %get-tuple-element.67.refs_4_), channel_id=1, source_target_pairs={{0,1},{1,0},{2,3},{3,2},{4,5},{5,4},{6,7},{7,6},{8,9},{9,8},{10,11... | collective-permute-start | bytes 1572872 | tf_op jit(solution)/shard_map/ppermute | solution.py:490
  74.5 4.8 %collective-permute-done.14.refs_2_.refs_0_ = bf16[256,1024]{1,0:T(8,128)(2,1)S(1)} collective-permute-done((bf16[256,1024]{1,0:T(8,128)(2,1)S(1)}, bf16[256,1024]{1,0:T(8,128)(2,1)S(1)}, u32[]{:S(2)}, u32[]{:S(2)}) %collective-permute-start.14) | collective-permute-done | bytes 524320 | tf_op jit(solution)/shard_map/ppermute | solution.py:485
  79.7 4.1 %attended_grads.1 = (bf16[512,1024]{1,0:T(8,128)(2,1)S(1)}, bf16[4,128,128]{2,1,0:T(8,128)(2,1)S(1)}, bf16[4,128,128]{2,1,0:T(8,128)(2,1)S(1)}) custom-call(s32[7]{0:T(128)S(1)} %pad_add_fusion.refs_0_, bf16[1024,4096]{1,0:T(8,128)(2,1)S(1)} %copy-done, bf16[512,1024]{1,0:T(8,128)(2,1)S(1)} %pick.5.refs_2_, f32[512,1024]{1,0:T(8,128)S(1)} %back_2.1.refs_4_.refs_3_, ...), custom_call_target="tpu_custom_call" | custom-call | flops 410000000 | tf_op jit(solution)/shard_map/attended_grads/pallas_call | solution.py:35
  84.0 1.8 %collective-permute-start.16 = (bf16[256,1024]{1,0:T(8,128)(2,1)S(1)}, bf16[256,1024]{1,0:T(8,128)(2,1)S(1)}, u32[]{:S(2)}, u32[]{:S(2)}) collective-permute-start(bf16[256,1024]{1,0:T(8,128)(2,1)S(1)} %get-tuple-element.73), channel_id=1, source_target_pairs={{0,1},{1,0},{2,3},{3,2},{4,5},{5,4},{6,7},{7,6},{8,9},{9,8},{10,11... | collective-permute-start | bytes 1572872 | tf_op jit(solution)/shard_map/ppermute | solution.py:497
  88.1 3.8 %query_grad.1 = (bf16[512,1024]{1,0:T(8,128)(2,1)}, f32[8,128]{1,0:T(8,128)S(1)}) custom-call(s32[512,128]{1,0:T(8,128)S(1)} %get-tuple-element.52.refs_0_, f32[32,128]{1,0:T(8,128)S(1)} %get-tuple-element.47.refs_0_.refs_7_.refs_1_, f32[512,128]{1,0:T(8,128)S(1)} %get-tuple-element.48.refs_1_.refs_8_.refs_2_, bf16[512,1024]{1,0:T(8,128)(2,1)S(1)} %copy-done.1, ...), custom_call_target="tpu_custom_call" | custom-call | flops 1000000 | tf_op jit(solution)/shard_map/query_grad/pallas_call | solution.py:35
  93.8 4.7 %key_value_grads.1 = (f32[512,1024]{1,0:T(8,128)S(1)}, f32[512,1024]{1,0:T(8,128)S(1)}) custom-call(s32[8,512]{1,0:T(8,128)S(1)} %get-tuple-element.81.refs_0_, bf16[512,1024]{1,0:T(8,128)(2,1)S(1)} %copy-done.3, bf16[512,1024]{1,0:T(8,128)(2,1)S(1)} %copy-done.1, bf16[512,1024]{1,0:T(8,128)(2,1)S(1)} %copy-done.2, ...), custom_call_target="tpu_custom_call" | custom-call | flops 1000000 | tf_op jit(solution)/shard_map/key_value_grads/pallas_call | solution.py:35
  100.7 2.4 %last_grads.1 = (bf16[512,1024]{1,0:T(8,128)(2,1)}, bf16[512,1024]{1,0:T(8,128)(2,1)}, f32[8,128]{1,0:T(8,128)S(1)}) custom-call(f32[32,128]{1,0:T(8,128)S(1)} %get-tuple-element.47.refs_0_.refs_7_.refs_1_, f32[512,128]{1,0:T(8,128)S(1)} %get-tuple-element.49.refs_1_, bf16[512,1024]{1,0:T(8,128)(2,1)S(1)} %copy-done.1, bf16[512,1024]{1,0:T(8,128)(2,1)S(1)} %copy-done.2, ...), custom_call_target="tpu_custom_call" | custom-call | flops 1000000 | tf_op jit(solution)/shard_map/last_grads/pallas_call | solution.py:35
  (60 shorter events, 25.6 us)
Async XLA Ops:
  0.6 27.0 %collective-permute-start.5 = (bf16[512,1024]{1,0:T(8,128)(2,1)}, bf16[512,1024]{1,0:T(8,128)(2,1)S(1)}, u32[]{:S(2)}, u32[]{:S(2)}) collective-permute-start(bf16[512,1024]{1,0:T(8,128)(2,1)} %refs_2_.12), channel_id=1, source_target_pairs={{1,2},{2,1},{5,6},{6,5},{9,10},{10,9},{13,14},{14,13},{17,18},{18,... | collective-permute-start | bytes 3145736 | tf_op jit(solution)/shard_map/ppermute | solution.py:447
  1.4 28.9 %collective-permute-start.4 = (bf16[512,1024]{1,0:T(8,128)(2,1)}, bf16[512,1024]{1,0:T(8,128)(2,1)S(1)}, u32[]{:S(2)}, u32[]{:S(2)}) collective-permute-start(bf16[512,1024]{1,0:T(8,128)(2,1)} %refs_2_.12), channel_id=1, source_target_pairs={{0,1},{1,0},{2,3},{3,2},{4,5},{5,4},{6,7},{7,6},{8,9},{9,8},{10,11... | collective-permute-start | bytes 3145736 | tf_op jit(solution)/shard_map/ppermute | solution.py:446
  9.5 11.2 %copy-start.4 = (bf16[512,1024]{1,0:T(8,128)(2,1)S(1)}, bf16[512,1024]{1,0:T(8,128)(2,1)}, u32[]{:S(2)}) copy-start(bf16[512,1024]{1,0:T(8,128)(2,1)} %refs_2_.12) | copy-start | bytes 3145732
  10.1 1.4 %collective-permute-start = (bf16[4,128,128]{2,1,0:T(8,128)(2,1)S(1)}, bf16[4,128,128]{2,1,0:T(8,128)(2,1)S(1)}, u32[]{:S(2)}, u32[]{:S(2)}) collective-permute-start(bf16[4,128,128]{2,1,0:T(8,128)(2,1)S(1)} %get-tuple-element.51), channel_id=1, source_target_pairs={{0,4},{4,0},{8,12},{12,8},{16,20},{20,16},{24,28},{28,24},{1,5},{5... | collective-permute-start | bytes 393224 | tf_op jit(solution)/shard_map/ppermute | solution.py:176
  11.5 9.2 %copy-start = (bf16[1024,4096]{1,0:T(8,128)(2,1)S(1)}, bf16[1024,4096]{1,0:T(8,128)(2,1)}, u32[]{:S(2)}) copy-start(bf16[1024,4096]{1,0:T(8,128)(2,1)} %refs_1_.10) | copy-start | bytes 25165828
  11.6 5.6 %collective-permute-start.1 = (bf16[4,128,128]{2,1,0:T(8,128)(2,1)S(1)}, bf16[4,128,128]{2,1,0:T(8,128)(2,1)S(1)}, u32[]{:S(2)}, u32[]{:S(2)}) collective-permute-start(bf16[4,128,128]{2,1,0:T(8,128)(2,1)S(1)} %pair_total.2.refs_4_.refs_2_), channel_id=1, source_target_pairs={{0,8},{4,12},{8,0},{12,4},{16,24},{20,28},{24,16},{28,20},{1,9},{5... | collective-permute-start | bytes 393224 | tf_op jit(solution)/shard_map/ppermute | solution.py:193
  17.3 5.9 %collective-permute-start.2 = (bf16[4,128,128]{2,1,0:T(8,128)(2,1)S(1)}, bf16[4,128,128]{2,1,0:T(8,128)(2,1)S(1)}, u32[]{:S(2)}, u32[]{:S(2)}) collective-permute-start(bf16[4,128,128]{2,1,0:T(8,128)(2,1)S(1)} %get-tuple-element.53), channel_id=1, source_target_pairs={{0,16},{4,20},{8,24},{12,28},{1,17},{5,21},{9,25},{13,29},{2,18},{... | collective-permute-start | bytes 393224 | tf_op jit(solution)/shard_map/ppermute | solution.py:193
  23.3 1.4 %collective-permute-start.3 = (bf16[4,128,128]{2,1,0:T(8,128)(2,1)S(1)}, bf16[4,128,128]{2,1,0:T(8,128)(2,1)S(1)}, u32[]{:S(2)}, u32[]{:S(2)}) collective-permute-start(bf16[4,128,128]{2,1,0:T(8,128)(2,1)S(1)} %get-tuple-element.56), channel_id=1, source_target_pairs={{0,4},{4,0},{8,12},{12,8},{16,20},{20,16},{24,28},{28,24},{1,5},{5... | collective-permute-start | bytes 393224 | tf_op jit(solution)/shard_map/ppermute | solution.py:207
  30.7 14.9 %collective-permute-start.6 = (bf16[256,1024]{1,0:T(8,128)(2,1)S(1)}, bf16[256,1024]{1,0:T(8,128)(2,1)S(1)}, u32[]{:S(2)}, u32[]{:S(2)}) collective-permute-start(bf16[256,1024]{1,0:T(8,128)(2,1)S(1)} %get-tuple-element.60), channel_id=1, source_target_pairs={{0,1},{1,0},{2,3},{3,2},{4,5},{5,4},{6,7},{7,6},{8,9},{9,8},{10,11... | collective-permute-start | bytes 1572872 | tf_op jit(solution)/shard_map/ppermute | solution.py:475
  32.5 13.1 %collective-permute-start.7 = (bf16[256,1024]{1,0:T(8,128)(2,1)S(1)}, bf16[256,1024]{1,0:T(8,128)(2,1)S(1)}, u32[]{:S(2)}, u32[]{:S(2)}) collective-permute-start(bf16[256,1024]{1,0:T(8,128)(2,1)S(1)} %get-tuple-element.61), channel_id=1, source_target_pairs={{1,2},{2,1},{5,6},{6,5},{9,10},{10,9},{13,14},{14,13},{17,18},{18,... | collective-permute-start | bytes 1572872 | tf_op jit(solution)/shard_map/ppermute | solution.py:475
  33.2 23.7 %collective-permute-start.10 = (bf16[256,1024]{1,0:T(8,128)(2,1)S(1)}, bf16[256,1024]{1,0:T(8,128)(2,1)S(1)}, u32[]{:S(2)}, u32[]{:S(2)}) collective-permute-start(bf16[256,1024]{1,0:T(8,128)(2,1)S(1)} %get-tuple-element.64), channel_id=1, source_target_pairs={{0,1},{1,0},{2,3},{3,2},{4,5},{5,4},{6,7},{7,6},{8,9},{9,8},{10,11... | collective-permute-start | bytes 1572872 | tf_op jit(solution)/shard_map/ppermute | solution.py:476
  35.2 21.7 %collective-permute-start.11 = (bf16[256,1024]{1,0:T(8,128)(2,1)S(1)}, bf16[256,1024]{1,0:T(8,128)(2,1)S(1)}, u32[]{:S(2)}, u32[]{:S(2)}) collective-permute-start(bf16[256,1024]{1,0:T(8,128)(2,1)S(1)} %get-tuple-element.65), channel_id=1, source_target_pairs={{1,2},{2,1},{5,6},{6,5},{9,10},{10,9},{13,14},{14,13},{17,18},{18,... | collective-permute-start | bytes 1572872 | tf_op jit(solution)/shard_map/ppermute | solution.py:476
  45.8 22.2 %collective-permute-start.8 = (bf16[256,1024]{1,0:T(8,128)(2,1)S(1)}, bf16[256,1024]{1,0:T(8,128)(2,1)S(1)}, u32[]{:S(2)}, u32[]{:S(2)}) collective-permute-start(bf16[256,1024]{1,0:T(8,128)(2,1)S(1)} %get-tuple-element.63), channel_id=1, source_target_pairs={{0,1},{1,0},{2,3},{3,2},{4,5},{5,4},{6,7},{7,6},{8,9},{9,8},{10,11... | collective-permute-start | bytes 1572872 | tf_op jit(solution)/shard_map/ppermute | solution.py:480
  49.8 18.3 %collective-permute-start.9 = (bf16[256,1024]{1,0:T(8,128)(2,1)S(1)}, bf16[256,1024]{1,0:T(8,128)(2,1)S(1)}, u32[]{:S(2)}, u32[]{:S(2)}) collective-permute-start(bf16[256,1024]{1,0:T(8,128)(2,1)S(1)} %get-tuple-element.62.refs_3_), channel_id=1, source_target_pairs={{1,2},{2,1},{5,6},{6,5},{9,10},{10,9},{13,14},{14,13},{17,18},{18,... | collective-permute-start | bytes 1572872 | tf_op jit(solution)/shard_map/ppermute | solution.py:480
  57.1 22.2 %collective-permute-start.14 = (bf16[256,1024]{1,0:T(8,128)(2,1)S(1)}, bf16[256,1024]{1,0:T(8,128)(2,1)S(1)}, u32[]{:S(2)}, u32[]{:S(2)}) collective-permute-start(bf16[256,1024]{1,0:T(8,128)(2,1)S(1)} %get-tuple-element.69), channel_id=1, source_target_pairs={{0,1},{1,0},{2,3},{3,2},{4,5},{5,4},{6,7},{7,6},{8,9},{9,8},{10,11... | collective-permute-start | bytes 1572872 | tf_op jit(solution)/shard_map/ppermute | solution.py:485
  61.0 22.8 %collective-permute-start.15 = (bf16[256,1024]{1,0:T(8,128)(2,1)S(1)}, bf16[256,1024]{1,0:T(8,128)(2,1)S(1)}, u32[]{:S(2)}, u32[]{:S(2)}) collective-permute-start(bf16[256,1024]{1,0:T(8,128)(2,1)S(1)} %get-tuple-element.66.refs_5_), channel_id=1, source_target_pairs={{1,2},{2,1},{5,6},{6,5},{9,10},{10,9},{13,14},{14,13},{17,18},{18,... | collective-permute-start | bytes 1572872 | tf_op jit(solution)/shard_map/ppermute | solution.py:485
  68.2 34.9 %collective-permute-start.13 = (bf16[256,1024]{1,0:T(8,128)(2,1)S(1)}, bf16[256,1024]{1,0:T(8,128)(2,1)S(1)}, u32[]{:S(2)}, u32[]{:S(2)}) collective-permute-start(bf16[256,1024]{1,0:T(8,128)(2,1)S(1)} %get-tuple-element.68), channel_id=1, source_target_pairs={{1,2},{2,1},{5,6},{6,5},{9,10},{10,9},{13,14},{14,13},{17,18},{18,... | collective-permute-start | bytes 1572872 | tf_op jit(solution)/shard_map/ppermute | solution.py:490
  68.9 34.2 %collective-permute-start.12 = (bf16[256,1024]{1,0:T(8,128)(2,1)S(1)}, bf16[256,1024]{1,0:T(8,128)(2,1)S(1)}, u32[]{:S(2)}, u32[]{:S(2)}) collective-permute-start(bf16[256,1024]{1,0:T(8,128)(2,1)S(1)} %get-tuple-element.67.refs_4_), channel_id=1, source_target_pairs={{0,1},{1,0},{2,3},{3,2},{4,5},{5,4},{6,7},{7,6},{8,9},{9,8},{10,11... | collective-permute-start | bytes 1572872 | tf_op jit(solution)/shard_map/ppermute | solution.py:490
  83.8 2.7 %collective-permute-start.18 = (bf16[4,128,128]{2,1,0:T(8,128)(2,1)S(1)}, bf16[4,128,128]{2,1,0:T(8,128)(2,1)S(1)}, u32[]{:S(2)}, u32[]{:S(2)}) collective-permute-start(bf16[4,128,128]{2,1,0:T(8,128)(2,1)S(1)} %get-tuple-element.72.refs_4_), channel_id=1, source_target_pairs={{0,4},{4,0},{8,12},{12,8},{16,20},{20,16},{24,28},{28,24},{1,5},{5... | collective-permute-start | bytes 393224 | tf_op jit(solution)/shard_map/ppermute | solution.py:176
  84.0 19.2 %collective-permute-start.16 = (bf16[256,1024]{1,0:T(8,128)(2,1)S(1)}, bf16[256,1024]{1,0:T(8,128)(2,1)S(1)}, u32[]{:S(2)}, u32[]{:S(2)}) collective-permute-start(bf16[256,1024]{1,0:T(8,128)(2,1)S(1)} %get-tuple-element.73), channel_id=1, source_target_pairs={{0,1},{1,0},{2,3},{3,2},{4,5},{5,4},{6,7},{7,6},{8,9},{9,8},{10,11... | collective-permute-start | bytes 1572872 | tf_op jit(solution)/shard_map/ppermute | solution.py:497
  85.8 17.4 %collective-permute-start.17 = (bf16[256,1024]{1,0:T(8,128)(2,1)S(1)}, bf16[256,1024]{1,0:T(8,128)(2,1)S(1)}, u32[]{:S(2)}, u32[]{:S(2)}) collective-permute-start(bf16[256,1024]{1,0:T(8,128)(2,1)S(1)} %get-tuple-element.74), channel_id=1, source_target_pairs={{1,2},{2,1},{5,6},{6,5},{9,10},{10,9},{13,14},{14,13},{17,18},{18,... | collective-permute-start | bytes 1572872 | tf_op jit(solution)/shard_map/ppermute | solution.py:497
  86.5 5.7 %collective-permute-start.19 = (bf16[4,128,128]{2,1,0:T(8,128)(2,1)S(1)}, bf16[4,128,128]{2,1,0:T(8,128)(2,1)S(1)}, u32[]{:S(2)}, u32[]{:S(2)}) collective-permute-start(bf16[4,128,128]{2,1,0:T(8,128)(2,1)S(1)} %pair_total.3.refs_8_.refs_2_), channel_id=1, source_target_pairs={{0,8},{4,12},{8,0},{12,4},{16,24},{20,28},{24,16},{28,20},{1,9},{5... | collective-permute-start | bytes 393224 | tf_op jit(solution)/shard_map/ppermute | solution.py:193
  92.3 6.9 %collective-permute-start.20 = (bf16[4,128,128]{2,1,0:T(8,128)(2,1)S(1)}, bf16[4,128,128]{2,1,0:T(8,128)(2,1)S(1)}, u32[]{:S(2)}, u32[]{:S(2)}) collective-permute-start(bf16[4,128,128]{2,1,0:T(8,128)(2,1)S(1)} %get-tuple-element.79.refs_5_), channel_id=1, source_target_pairs={{16,0},{20,4},{24,8},{28,12},{17,1},{21,5},{25,9},{29,13},{18,2},{... | collective-permute-start | bytes 393224 | tf_op jit(solution)/shard_map/ppermute | solution.py:193
  99.3 1.4 %collective-permute-start.21 = (bf16[4,128,128]{2,1,0:T(8,128)(2,1)S(1)}, bf16[4,128,128]{2,1,0:T(8,128)(2,1)S(1)}, u32[]{:S(2)}, u32[]{:S(2)}) collective-permute-start(bf16[4,128,128]{2,1,0:T(8,128)(2,1)S(1)} %get-tuple-element.84), channel_id=1, source_target_pairs={{0,4},{4,0},{8,12},{12,8},{16,20},{20,16},{24,28},{28,24},{1,5},{5... | collective-permute-start | bytes 393224 | tf_op jit(solution)/shard_map/ppermute | solution.py:207
  (3 other events, 7.2 us)

commit v5 on v4

--- a/solution.py
+++ b/solution.py
@@ -17,7 +17,7 @@
 MICROSECONDS = {
     "setup": 100.0, "local_states": 0.8, "intra": 3.0, "back_own": 1.8, "pair_total": 0.1, "exchange_stage": 0.1,
     "exchange_last": 0.1, "normalise": 0.9, "project_3": 1.8, "project_2": 1.8, "project_1": 1.8,
-    "project_0": 1.8, "back_1": 1.8, "pick": 0.3, "turn": 0.5, "back_2": 1.8, "attended_grads": 4.1,
+    "project_0": 1.8, "back_1": 1.8, "pick": 0.3, "turn": 0.5, "back_2": 1.8, "attended_grads": 2.0, "first_grads": 2.0, "block": 0.5,
     "query_grad": 0.01, "key_value_grads": 0.01, "last_grads": 0.01, "mixed": 1.3,
 }
 
@@ -84,14 +84,9 @@
     return rows == start_at(starts, first - 1), rows == start_at(starts, first + tok - 1)
 
 
-def visible(low_ref, axis):
-    if axis == 0:
-        tok = low_ref.shape[0]
-        low = low_ref[:, :1]
-    else:
-        tok = low_ref.shape[1]
-        low = low_ref[:1, :]
-    t, s = line(tok, axis), line(tok, 1 - axis)
+def visible(low_ref, axis, t0, t1, s1):
+    low = low_ref[t0:t1, :1] if axis == 0 else low_ref[:1, t0:t1]
+    t, s = line(t1 - t0, axis) + t0, line(s1, 1 - axis)
     return (s <= t) & (s >= low)
 
 
@@ -250,7 +245,8 @@
 
 
 def intra_body(low_ref, q_ref, k_ref, v_ref, out_ref):
-    mask = visible(low_ref, 0)
+    tok = q_ref.shape[0]
+    mask = visible(low_ref, 0, 0, tok, tok)
     for h in range(q_ref.shape[1] // DH):
         s = dot(q_ref[:, head(h)], k_ref[:, head(h)], 1, 1)
         s = jnp.where(mask, s, 0.0).astype(BF16)
@@ -304,45 +300,84 @@
         out_ref[:, rows] = acc
 
 
-def att_grad_body(block, info_ref, w_ref, x_ref, base_ref, normed_ref, inv_ref, q_ref, c_ref, cin_ref, ag_ref, send_ref, keep_ref):
+def block_body(block, info_ref, w_ref, out_ref):
+    width = out_ref.shape[1]
+    out_ref[...] = w_ref[:, pl.ds(columns(info_ref, block, width), width)]
+
+
+def att_grad(rows, c_ref, cin_ref, w_ref, n_ref, g_ref, base_ref, normed_ref, inv_ref, q_ref, ag_ref):
     wide = q_ref.shape[1]
-    width = x_ref.shape[1]
-    at = columns(info_ref, block, width)
+    x = n_ref[...] * at_end(c_ref)[:, :1] + g_ref[rows, :]
     zero = jnp.zeros((), BF16)
-    cin = cin_ref[...] > 0.5
+    cin = cin_ref[rows, :] > 0.5
     states = []
     for i in range(wide // TILE):
-        rows = slice(i * TILE, (i + 1) * TILE)
-        ng2 = base_ref[:, rows] + dot(x_ref[...], w_ref[rows, pl.ds(at, width)], 1, 1)
+        feats = slice(i * TILE, (i + 1) * TILE)
+        ng2 = base_ref[rows, feats] + dot(x, w_ref[feats, :], 1, 1)
         for j in range(TILE // DH):
-            h = i * (TILE // DH) + j
-            ng, normed = ng2[:, head(j)], normed_ref[:, head(h)]
+            at = head(i * (TILE // DH) + j)
+            ng, normed = ng2[:, head(j)], normed_ref[rows, at]
             proj = jnp.mean(ng * normed, axis=-1, keepdims=True)
-            ag = ((ng - normed * proj) * inv_ref[:, head(h)]).astype(BF16)
-            ag_ref[:, head(h)] = ag
-            kept = jnp.where(cin, q_ref[:, head(h)], zero)
-            states.append(dot(kept, ag, 0, 0))
-    put_states(states, c_ref, keep_ref, send_ref)
-
-
-def query_grad_body(low_ref, c_ref, cin_ref, k_ref, v_ref, ag_ref, own_ref, back_ref, qg_ref, mark_ref):
-    mask = visible(low_ref, 0)
+            ag = ((ng - normed * proj) * inv_ref[rows, at]).astype(BF16)
+            ag_ref[:, at] = ag
+            states.append(dot(jnp.where(cin, q_ref[rows, at], zero), ag, 0, 0))
+    return states
+
+
+def att_grad_first_body(rows, *refs):
+    for h, state in enumerate(att_grad(rows, *refs[:-1])):
+        refs[-1][h] = state
+
+
+def att_grad_second_body(rows, before_ref, *refs):
+    send_ref, keep_ref = refs[-2:]
+    states = att_grad(rows, *refs[:-2])
+    put_states([before_ref[h] + state for h, state in enumerate(states)], refs[0], keep_ref, send_ref)
+
+
+def query_grad(h, rows, s1, mask, c_ref, cin_ref, k_ref, v_ref, ag_ref, own_ref, back_ref):
+    ag, at = ag_ref[:, head(h)], head(h)
+    inter = dot(ag, pick(c_ref, own_ref, back_ref, h), 1, 1)
+    g = jnp.where(mask, dot(ag, v_ref[:s1, at], 1, 1), 0.0).astype(BF16)
+    return (dot(g, k_ref[:s1, at], 1, 0) + cin_ref[rows, :] * inter).astype(BF16)
+
+
+def key_value_grad(h, rows, s1, mask, q_ref, k_ref, v_ref, ag_ref):
+    at = head(h)
+    q, ag = q_ref[rows, at], ag_ref[:, at]
+    st = jnp.where(mask, dot(k_ref[:s1, at], q, 1, 1), 0.0).astype(BF16)
+    gt = jnp.where(mask, dot(v_ref[:s1, at], ag, 1, 1), 0.0).astype(BF16)
+    return dot(gt, q, 1, 0), dot(st, ag, 1, 0)
+
+
+def first_grads_body(rows, low_ref, low_t_ref, c_ref, cin_ref, q_ref, k_ref, v_ref, ag_ref, own_ref, back_ref, qg_ref, kg_ref, vg_ref):
+    r1 = rows.stop
+    mask, mask_t = visible(low_ref, 0, 0, r1, r1), visible(low_t_ref, 1, 0, r1, r1)
+    for h in range(q_ref.shape[1] // DH):
+        qg_ref[:, head(h)] = query_grad(h, rows, r1, mask, c_ref, cin_ref, k_ref, v_ref, ag_ref, own_ref, back_ref)
+        kg, vg = key_value_grad(h, rows, r1, mask_t, q_ref, k_ref, v_ref, ag_ref)
+        kg_ref[:, head(h)] = kg
+        vg_ref[:, head(h)] = vg
+
+
+def query_grad_body(rows, low_ref, c_ref, cin_ref, k_ref, v_ref, ag_ref, own_ref, back_ref, first_ref, qg_ref, mark_ref):
+    r0, r1 = rows.start, rows.stop
+    mask = visible(low_ref, 0, r0, r1, r1)
     mark_ref[...] = jnp.zeros_like(mark_ref)
+    qg_ref[:r0, :] = first_ref[...]
     for h in range(k_ref.shape[1] // DH):
-        ag = ag_ref[:, head(h)]
-        inter = dot(ag, pick(c_ref, own_ref, back_ref, h), 1, 1)
-        g = jnp.where(mask, dot(ag, v_ref[:, head(h)], 1, 1), 0.0).astype(BF16)
-        qg_ref[:, head(h)] = (dot(g, k_ref[:, head(h)], 1, 0) + cin_ref[...] * inter).astype(BF16)
-
-
-def key_value_body(low_t_ref, q_ref, k_ref, v_ref, ag_ref, kg_ref, vg_ref):
-    mask = visible(low_t_ref, 1)
+        qg_ref[rows, head(h)] = query_grad(h, rows, r1, mask, c_ref, cin_ref, k_ref, v_ref, ag_ref, own_ref, back_ref)
+
+
+def key_value_body(rows, low_t_ref, q_ref, k_ref, v_ref, ag_ref, k_first_ref, v_first_ref, kg_ref, vg_ref):
+    r0, r1 = rows.start, rows.stop
+    mask = visible(low_t_ref, 1, r0, r1, r1)
     for h in range(q_ref.shape[1] // DH):
-        q, k, v, ag = (r[:, head(h)] for r in (q_ref, k_ref, v_ref, ag_ref))
-        st = jnp.where(mask, dot(k, q, 1, 1), 0.0).astype(BF16)
-        vg_ref[:, head(h)] = dot(st, ag, 1, 0)
-        gt = jnp.where(mask, dot(v, ag, 1, 1), 0.0).astype(BF16)
-        kg_ref[:, head(h)] = dot(gt, q, 1, 0)
+        at = head(h)
+        kg, vg = key_value_grad(h, rows, r1, mask, q_ref, k_ref, v_ref, ag_ref)
+        for ref, first_ref, new in ((kg_ref, k_first_ref, kg), (vg_ref, v_first_ref, vg)):
+            ref[:r0, at] = first_ref[:, at] + new[:r0]
+            ref[r0:, at] = new[r0:]
 
 
 def last_body(c_ref, cout_ref, k_ref, v_ref, own_ref, back_ref, kp_ref, vp_ref, kg_ref, vg_ref, mark_ref):
@@ -390,12 +425,6 @@
         rows = slice(r0, r0 + a_ref.shape[0])
         end_body(c_ref, a_ref, b_ref, out_ref.at[rows, :])
         r0 = rows.stop
-
-
-def ends_whole_body(c_ref, a0_ref, a1_ref, b_ref, out_ref):
-    r1 = a0_ref.shape[0]
-    end_body(c_ref, a0_ref, b_ref.at[:r1, :], out_ref.at[:r1, :])
-    end_body(c_ref, a1_ref, b_ref.at[r1:, :], out_ref.at[r1:, :])
 
 
 def turn_body(rows, c_ref, n2_ref, p2_ref, i2_ref, s2_ref, n3_ref):
@@ -486,12 +515,24 @@
     n3, i3 = [n3a, n3b], [i3a, i3b]
     (g2,) = kernel(ends_body, "pick", [], [coef, n2a, i2a, n2b, i2b], [part], [s2b])
     base = back_project([2], "back_2", [g2], base)
-    s3a, s1a = turn_again(0, [base])
-    n4a, i4a = lax.ppermute(s1a, "head", neighbours), lax.ppermute(s3a, "head", inner)
-    (g3,) = kernel(ends_whole_body, "pick", [], [coef, n3a, n3b, g3_inner], [part], [s1a])
+    (w3,) = kernel(functools.partial(block_body, 3), "block", [info], [w], [like((feats, width), BF16)], [base])
+    s3a, s1a = turn_again(0, [w3])
+    n4a = lax.ppermute(s1a, "head", neighbours)
+    ag_ins = [g3_inner, base, normed_f, inv, q]
+    aga, states = kernel(
+        functools.partial(att_grad_first_body, rows[0]), "attended_grads", [], [coef, cin, w3, n3a, *ag_ins],
+        [like((tok // 2, feats), BF16), like((heads, DH, DH), F32)], [s1a],
+    )
+    s3a, _ = lax.optimization_barrier((s3a, aga))
+    i4a = lax.ppermute(s3a, "head", inner)
+    half_f = like((tok // 2, feats), F32)
+    qga, kga, vga = kernel(
+        functools.partial(first_grads_body, rows[0]), "first_grads", [],
+        [low, low_t, coef, cin, q, k, v, aga, own, other], [like((tok // 2, feats), BF16), half_f, half_f],
+    )
     ag, gsend, gkeep = kernel(
-        functools.partial(att_grad_body, 3), "attended_grads", [info],
-        [w, g3, base, normed_f, inv, q, coef, cin], [wide_b, state, state],
+        functools.partial(att_grad_second_body, rows[1]), "attended_grads", [],
+        [states, coef, cin, w3, n3b, *ag_ins], [like((tok // 2, feats), BF16), state, state], [qga],
     )
     s3b, s1b = turn_again(1, [gsend])
     n4b, i4b = lax.ppermute(s1b, "head", neighbours), lax.ppermute(s3b, "head", inner)
@@ -500,14 +541,16 @@
 
     def beside_first(sent):
         grads.extend(kernel(
-            query_grad_body, "query_grad", [], [low, coef, cin, k, v, ag, own, other],
+            functools.partial(query_grad_body, rows[1]), "query_grad", [],
+            [low, coef, cin, k, v, ag, own, other, qga],
             [wide_b, like((8, DH), F32)], [sent],
         ))
         return grads[1:2]
 
     def beside_second(sent):
         grads.extend(kernel(
-            key_value_body, "key_value_grads", [], [low_t, q, k, v, ag], [wide_f, wide_f], [sent]
+            functools.partial(key_value_body, rows[1]), "key_value_grads", [],
+            [low_t, q, k, v, ag, kga, vga], [wide_f, wide_f], [sent],
         ))
         return grads[2:3]
 

time: 105 us -> 103 us (0.981)
  starting transfers between devices: 38.4 us -> 36.7 us
    ppermute x1, waiting for transfers between devices: 4.79 us -> 1.32 us  [shards(): lax.ppermute(n3b, 'head', neighbours)]
    ppermute x4, waiting for transfers between devices: 3.28 us -> 6.37 us  [exchange(): others.append(lax.ppermute(total, 'ctx', pairs))]
    ppermute x2, starting transfers between devices: 6.33 us -> 4.66 us  [the longest x1 3.97 us: shards(): n4a = lax.ppermute(s1a, 'head', neighbours)]
    pallas_call x29 -> x31, Pallas kernels: 36.1 us -> 36.6 us  [kernel(): pl.pallas_call(inner, name=name, in_specs=[spec(pltpu.SMEM)] * len(smem)...]
  transfers between devices with their start and end apart: 22 -> 22, of which waited for: 12 -> 12; matrix products, arithmetic and copies ran while one was open for 1% -> 1% of each run, Pallas kernels for 33% -> 34%
where the time goes in v5:
time: 103 us; the launch traced here: 102 us
  starting transfers between devices  36.7 us (36%)
  Pallas kernels  36.6 us (36%)
  waiting for transfers between devices  26.5 us (26%)
    pallas_call x31, Pallas kernels, kernel(): pl.pallas_call(inner, name=name, in_specs=[spec(pltpu.SMEM)] * len(smem)...  36.6 us
    ppermute x4, starting transfers between devices, exchange(): others.append(lax.ppermute(total, 'ctx', pairs))  8.05 us
    ppermute x1, waiting for transfers between devices, shards(): lax.ppermute(n2a, 'head', neighbours)  7.9 us
    ppermute x4, waiting for transfers between devices, exchange(): others.append(lax.ppermute(total, 'ctx', pairs))  6.37 us
    ppermute x1, starting transfers between devices, shards(): g1 = lax.ppermute(grad, 'head', neighbours)  5.85 us
    ppermute x1, starting transfers between devices, shards(): lax.ppermute(n3a, 'head', neighbours)  3.97 us
    ppermute x1, starting transfers between devices, shards(): lax.ppermute(n3b, 'head', neighbours)  3.97 us
    ppermute x1, starting transfers between devices, shards(): n4a = lax.ppermute(s1a, 'head', neighbours)  3.97 us
  transfers between devices with their start and end apart: 22, of which 12 were waited for; matrix products, arithmetic and copies ran while one was open for 1% of the time, Pallas kernels for 34%

profile of v5, /device:TPU:0, one launch (start us, length us, event | category | flops | bytes accessed | tf_op | source)
XLA Modules:
  0.0 102.4 jit_solution(10355333396468556083)
XLA Ops:
  1.4 5.8 %collective-permute-start.4 = (bf16[512,1024]{1,0:T(8,128)(2,1)}, bf16[512,1024]{1,0:T(8,128)(2,1)S(1)}, u32[]{:S(2)}, u32[]{:S(2)}) collective-permute-start(bf16[512,1024]{1,0:T(8,128)(2,1)} %refs_2_.12), channel_id=1, source_target_pairs={{0,1},{1,0},{2,3},{3,2},{4,5},{5,4},{6,7},{7,6},{8,9},{9,8},{10,11... | collective-permute-start | bytes 3145736 | tf_op jit(solution)/shard_map/ppermute | solution.py:475
  13.1 2.5 %intra.1.refs_3_.refs_5_ = f32[512,1024]{1,0:T(8,128)S(1)} custom-call(s32[512,128]{1,0:T(8,128)S(1)} %get-tuple-element.58.refs_0_, bf16[512,1024]{1,0:T(8,128)(2,1)S(1)} %copy-done.1, bf16[512,1024]{1,0:T(8,128)(2,1)S(1)} %copy-done.2, bf16[512,1024]{1,0:T(8,128)(2,1)S(1)} %copy-done.3, bf16[4,128,128]{2,1,0:T(8,128)(2,1)S(1)} %pair_total.2.refs_4_.refs_2_), custom_call_target="tpu_custom_call" | custom-call | flops 300000000 | tf_op jit(solution)/shard_map/intra/pallas_call | solution.py:35
  17.3 3.4 %collective-permute-start.2 = (bf16[4,128,128]{2,1,0:T(8,128)(2,1)S(1)}, bf16[4,128,128]{2,1,0:T(8,128)(2,1)S(1)}, u32[]{:S(2)}, u32[]{:S(2)}) collective-permute-start(bf16[4,128,128]{2,1,0:T(8,128)(2,1)S(1)} %get-tuple-element.59), channel_id=1, source_target_pairs={{0,16},{4,20},{8,24},{12,28},{1,17},{5,21},{9,25},{13,29},{2,18},{... | collective-permute-start | bytes 393224 | tf_op jit(solution)/shard_map/ppermute | solution.py:188
  20.7 1.8 %back_own.1.refs_5_.refs_3_ = f32[512,1024]{1,0:T(8,128)S(1)} custom-call(s32[7]{0:T(128)S(1)} %pad_add_fusion.refs_0_, bf16[1024,4096]{1,0:T(8,128)(2,1)S(1)} %copy-done, bf16[512,1024]{1,0:T(8,128)(2,1)S(1)} %copy-done.4, f32[512,1024]{1,0:T(8,128)S(1)} %intra.1.refs_3_.refs_5_), custom_call_target="tpu_custom_call" | custom-call | flops 180000000 | tf_op jit(solution)/shard_map/back_own/pallas_call | solution.py:35
  25.7 1.8 %project_3.1.refs_2_.refs_3_ = bf16[512,1024]{1,0:T(8,128)(2,1)S(1)} custom-call(s32[7]{0:T(128)S(1)} %pad_add_fusion.refs_0_, bf16[512,1024]{1,0:T(8,128)(2,1)S(1)} %get-tuple-element.63.refs_1_, bf16[1024,4096]{1,0:T(8,128)(2,1)S(1)} %copy-done), custom_call_target="tpu_custom_call" | custom-call | flops 180000000 | tf_op jit(solution)/shard_map/project_3/pallas_call | solution.py:35
  27.6 2.7 %collective-permute-done.4.refs_1_.refs_2_ = bf16[512,1024]{1,0:T(8,128)(2,1)S(1)} collective-permute-done((bf16[512,1024]{1,0:T(8,128)(2,1)}, bf16[512,1024]{1,0:T(8,128)(2,1)S(1)}, u32[]{:S(2)}, u32[]{:S(2)}) %collective-permute-start.4) | collective-permute-done | bytes 1048608 | tf_op jit(solution)/shard_map/ppermute | solution.py:475
  33.2 2.0 %collective-permute-start.10 = (bf16[256,1024]{1,0:T(8,128)(2,1)S(1)}, bf16[256,1024]{1,0:T(8,128)(2,1)S(1)}, u32[]{:S(2)}, u32[]{:S(2)}) collective-permute-start(bf16[256,1024]{1,0:T(8,128)(2,1)S(1)} %get-tuple-element.70), channel_id=1, source_target_pairs={{0,1},{1,0},{2,3},{3,2},{4,5},{5,4},{6,7},{7,6},{8,9},{9,8},{10,11... | collective-permute-start | bytes 1572872 | tf_op jit(solution)/shard_map/ppermute | solution.py:505
  35.9 1.8 %project_2.1.refs_2_ = bf16[512,1024]{1,0:T(8,128)(2,1)S(1)} custom-call(s32[7]{0:T(128)S(1)} %pad_add_fusion.refs_0_, bf16[512,1024]{1,0:T(8,128)(2,1)S(1)} %get-tuple-element.63.refs_1_, bf16[1024,4096]{1,0:T(8,128)(2,1)S(1)} %copy-done, bf16[512,1024]{1,0:T(8,128)(2,1)S(1)} %project_3.1.refs_2_.refs_3_), custom_call_target="tpu_custom_call" | custom-call | flops 180000000 | tf_op jit(solution)/shard_map/project_2/pallas_call | solution.py:35
  37.7 7.9 %collective-permute-done.6.refs_1_ = bf16[256,1024]{1,0:T(8,128)(2,1)S(1)} collective-permute-done((bf16[256,1024]{1,0:T(8,128)(2,1)S(1)}, bf16[256,1024]{1,0:T(8,128)(2,1)S(1)}, u32[]{:S(2)}, u32[]{:S(2)}) %collective-permute-start.6) | collective-permute-done | bytes 524320 | tf_op jit(solution)/shard_map/ppermute | solution.py:504
  45.8 4.0 %collective-permute-start.8 = (bf16[256,1024]{1,0:T(8,128)(2,1)S(1)}, bf16[256,1024]{1,0:T(8,128)(2,1)S(1)}, u32[]{:S(2)}, u32[]{:S(2)}) collective-permute-start(bf16[256,1024]{1,0:T(8,128)(2,1)S(1)} %get-tuple-element.69), channel_id=1, source_target_pairs={{0,1},{1,0},{2,3},{3,2},{4,5},{5,4},{6,7},{7,6},{8,9},{9,8},{10,11... | collective-permute-start | bytes 1572872 | tf_op jit(solution)/shard_map/ppermute | solution.py:509
  50.5 1.8 %project_1.1.refs_3_ = bf16[512,1024]{1,0:T(8,128)(2,1)S(1)} custom-call(s32[7]{0:T(128)S(1)} %pad_add_fusion.refs_0_, bf16[512,1024]{1,0:T(8,128)(2,1)S(1)} %get-tuple-element.63.refs_1_, bf16[1024,4096]{1,0:T(8,128)(2,1)S(1)} %copy-done, bf16[256,1024]{1,0:T(8,128)(2,1)S(1)} %get-tuple-element.68.refs_3_), custom_call_target="tpu_custom_call" | custom-call | flops 180000000 | tf_op jit(solution)/shard_map/project_1/pallas_call | solution.py:35
  52.3 1.8 %project_0.1.refs_4_.refs_0_ = bf16[512,1024]{1,0:T(8,128)(2,1)S(1)} custom-call(s32[7]{0:T(128)S(1)} %pad_add_fusion.refs_0_, bf16[512,1024]{1,0:T(8,128)(2,1)S(1)} %get-tuple-element.63.refs_1_, bf16[1024,4096]{1,0:T(8,128)(2,1)S(1)} %copy-done, bf16[512,1024]{1,0:T(8,128)(2,1)S(1)} %project_1.1.refs_3_), custom_call_target="tpu_custom_call" | custom-call | flops 180000000 | tf_op jit(solution)/shard_map/project_0/pallas_call | solution.py:35
  54.1 1.8 %back_1.1.refs_4_.refs_3_ = f32[512,1024]{1,0:T(8,128)S(1)} custom-call(s32[7]{0:T(128)S(1)} %pad_add_fusion.refs_0_, bf16[1024,4096]{1,0:T(8,128)(2,1)S(1)} %copy-done, bf16[512,1024]{1,0:T(8,128)(2,1)S(1)} %collective-permute-done.4.refs_1_.refs_2_, f32[512,1024]{1,0:T(8,128)S(1)} %back_own.1.refs_5_.refs_3_, bf16[512,1024]{1,0:T(8,128)(2,1)S(1)} %project_0.1.refs_4_.refs_0_), custom_call_target="tpu_custom_call" | custom-call | flops 180000000 | tf_op jit(solution)/shard_map/back_1/pallas_call | solution.py:35
  57.1 4.0 %collective-permute-start.14 = (bf16[256,1024]{1,0:T(8,128)(2,1)S(1)}, bf16[256,1024]{1,0:T(8,128)(2,1)S(1)}, u32[]{:S(2)}, u32[]{:S(2)}) collective-permute-start(bf16[256,1024]{1,0:T(8,128)(2,1)S(1)} %get-tuple-element.79), channel_id=1, source_target_pairs={{0,1},{1,0},{2,3},{3,2},{4,5},{5,4},{6,7},{7,6},{8,9},{9,8},{10,11... | collective-permute-start | bytes 1572872 | tf_op jit(solution)/shard_map/ppermute | solution.py:514
  62.2 1.8 %back_2.1.refs_2_.refs_5_.refs_6_ = f32[512,1024]{1,0:T(8,128)S(1)} custom-call(s32[7]{0:T(128)S(1)} %pad_add_fusion.refs_0_, bf16[1024,4096]{1,0:T(8,128)(2,1)S(1)} %copy-done, bf16[512,1024]{1,0:T(8,128)(2,1)S(1)} %pick.3.refs_2_, f32[512,1024]{1,0:T(8,128)S(1)} %back_1.1.refs_4_.refs_3_), custom_call_target="tpu_custom_call" | custom-call | flops 180000000 | tf_op jit(solution)/shard_map/back_2/pallas_call | solution.py:35
  64.8 3.3 %collective-permute-done.8.refs_0_.refs_3_ = bf16[256,1024]{1,0:T(8,128)(2,1)S(1)} collective-permute-done((bf16[256,1024]{1,0:T(8,128)(2,1)S(1)}, bf16[256,1024]{1,0:T(8,128)(2,1)S(1)}, u32[]{:S(2)}, u32[]{:S(2)}) %collective-permute-start.8) | collective-permute-done | bytes 524320 | tf_op jit(solution)/shard_map/ppermute | solution.py:509
  68.2 4.0 %collective-permute-start.12 = (bf16[256,1024]{1,0:T(8,128)(2,1)S(1)}, bf16[256,1024]{1,0:T(8,128)(2,1)S(1)}, u32[]{:S(2)}, u32[]{:S(2)}) collective-permute-start(bf16[256,1024]{1,0:T(8,128)(2,1)S(1)} %get-tuple-element.73.refs_9_), channel_id=1, source_target_pairs={{0,1},{1,0},{2,3},{3,2},{4,5},{5,4},{6,7},{7,6},{8,9},{9,8},{10,11... | collective-permute-start | bytes 1572872 | tf_op jit(solution)/shard_map/ppermute | solution.py:520
  72.2 2.2 %attended_grads.2 = (bf16[256,1024]{1,0:T(8,128)(2,1)S(1)}, f32[8,128,128]{2,1,0:T(8,128)S(1)}) custom-call(f32[32,128]{1,0:T(8,128)S(1)} %get-tuple-element.53.refs_0_.refs_2_.refs_1_, f32[512,128]{1,0:T(8,128)S(1)} %get-tuple-element.54.refs_1_.refs_3_.refs_2_, bf16[1024,1024]{1,0:T(8,128)(2,1)S(1)} %block.1.refs_4_.refs_2_.refs_3_, ...), custom_call_target="tpu_custom_call" | custom-call | flops 200000000 | tf_op jit(solution)/shard_map/attended_grads/pallas_call | solution.py:35
  75.1 2.9 %first_grads.1 = (bf16[256,1024]{1,0:T(8,128)(2,1)S(1)}, f32[256,1024]{1,0:T(8,128)S(1)}, f32[256,1024]{1,0:T(8,128)S(1)}) custom-call(s32[512,128]{1,0:T(8,128)S(1)} %get-tuple-element.58.refs_0_, s32[8,512]{1,0:T(8,128)S(1)} %get-tuple-element.81.refs_1_.refs_0_, f32[32,128]{1,0:T(8,128)S(1)} %get-tuple-element.53.refs_0_.refs_2_.refs_1_, ...), custom_call_target="tpu_custom_call" | custom-call | flops 200000000 | tf_op jit(solution)/shard_map/first_grads/pallas_call | solution.py:35
  79.3 2.3 %attended_grads.3 = (bf16[256,1024]{1,0:T(8,128)(2,1)S(1)}, bf16[4,128,128]{2,1,0:T(8,128)(2,1)S(1)}, bf16[4,128,128]{2,1,0:T(8,128)(2,1)S(1)}) custom-call(f32[8,128,128]{2,1,0:T(8,128)S(1)} %get-tuple-element.80.refs_0_, f32[32,128]{1,0:T(8,128)S(1)} %get-tuple-element.53.refs_0_.refs_2_.refs_1_, f32[512,128]{1,0:T(8,128)S(1)} %get-tuple-element.54.refs_1_.refs_3_.refs_2_, ...), custom_call_target="tpu_custom_call" | custom-call | flops 200000000 | tf_op jit(solution)/shard_map/attended_grads/pallas_call | solution.py:35
  85.9 2.9 %query_grad.1 = (bf16[512,1024]{1,0:T(8,128)(2,1)}, f32[8,128]{1,0:T(8,128)S(1)}) custom-call(s32[512,128]{1,0:T(8,128)S(1)} %get-tuple-element.58.refs_0_, f32[32,128]{1,0:T(8,128)S(1)} %get-tuple-element.53.refs_0_.refs_2_.refs_1_, f32[512,128]{1,0:T(8,128)S(1)} %get-tuple-element.54.refs_1_.refs_3_.refs_2_, bf16[512,1024]{1,0:T(8,128)(2,1)S(1)} %copy-done.2, ...), custom_call_target="tpu_custom_call" | custom-call | flops 1000000 | tf_op jit(solution)/shard_map/query_grad/pallas_call | solution.py:35
  91.6 2.4 %key_value_grads.1 = (f32[512,1024]{1,0:T(8,128)S(1)}, f32[512,1024]{1,0:T(8,128)S(1)}) custom-call(s32[8,512]{1,0:T(8,128)S(1)} %get-tuple-element.81.refs_1_.refs_0_, bf16[512,1024]{1,0:T(8,128)(2,1)S(1)} %copy-done.1, bf16[512,1024]{1,0:T(8,128)(2,1)S(1)} %copy-done.2, bf16[512,1024]{1,0:T(8,128)(2,1)S(1)} %copy-done.3, ...), custom_call_target="tpu_custom_call" | custom-call | flops 1000000 | tf_op jit(solution)/shard_map/key_value_grads/pallas_call | solution.py:35
  94.0 2.9 %collective-permute-done.20.refs_1_ = bf16[4,128,128]{2,1,0:T(8,128)(2,1)S(1)} collective-permute-done((bf16[4,128,128]{2,1,0:T(8,128)(2,1)S(1)}, bf16[4,128,128]{2,1,0:T(8,128)(2,1)S(1)}, u32[]{:S(2)}, u32[]{:S(2)}) %collective-permute-start.20) | collective-permute-done | bytes 131104 | tf_op jit(solution)/shard_map/ppermute | solution.py:188
  98.5 2.5 %last_grads.1 = (bf16[512,1024]{1,0:T(8,128)(2,1)}, bf16[512,1024]{1,0:T(8,128)(2,1)}, f32[8,128]{1,0:T(8,128)S(1)}) custom-call(f32[32,128]{1,0:T(8,128)S(1)} %get-tuple-element.53.refs_0_.refs_2_.refs_1_, f32[512,128]{1,0:T(8,128)S(1)} %get-tuple-element.55.refs_1_, bf16[512,1024]{1,0:T(8,128)(2,1)S(1)} %copy-done.2, bf16[512,1024]{1,0:T(8,128)(2,1)S(1)} %copy-done.3, ...), custom_call_target="tpu_custom_call" | custom-call | flops 1000000 | tf_op jit(solution)/shard_map/last_grads/pallas_call | solution.py:35
  (62 shorter events, 31.0 us)
Async XLA Ops:
  0.6 26.9 %collective-permute-start.5 = (bf16[512,1024]{1,0:T(8,128)(2,1)}, bf16[512,1024]{1,0:T(8,128)(2,1)S(1)}, u32[]{:S(2)}, u32[]{:S(2)}) collective-permute-start(bf16[512,1024]{1,0:T(8,128)(2,1)} %refs_2_.12), channel_id=1, source_target_pairs={{1,2},{2,1},{5,6},{6,5},{9,10},{10,9},{13,14},{14,13},{17,18},{18,... | collective-permute-start | bytes 3145736 | tf_op jit(solution)/shard_map/ppermute | solution.py:476
  1.4 28.9 %collective-permute-start.4 = (bf16[512,1024]{1,0:T(8,128)(2,1)}, bf16[512,1024]{1,0:T(8,128)(2,1)S(1)}, u32[]{:S(2)}, u32[]{:S(2)}) collective-permute-start(bf16[512,1024]{1,0:T(8,128)(2,1)} %refs_2_.12), channel_id=1, source_target_pairs={{0,1},{1,0},{2,3},{3,2},{4,5},{5,4},{6,7},{7,6},{8,9},{9,8},{10,11... | collective-permute-start | bytes 3145736 | tf_op jit(solution)/shard_map/ppermute | solution.py:475
  9.5 11.2 %copy-start.4 = (bf16[512,1024]{1,0:T(8,128)(2,1)S(1)}, bf16[512,1024]{1,0:T(8,128)(2,1)}, u32[]{:S(2)}) copy-start(bf16[512,1024]{1,0:T(8,128)(2,1)} %refs_2_.12) | copy-start | bytes 3145732
  10.1 1.4 %collective-permute-start = (bf16[4,128,128]{2,1,0:T(8,128)(2,1)S(1)}, bf16[4,128,128]{2,1,0:T(8,128)(2,1)S(1)}, u32[]{:S(2)}, u32[]{:S(2)}) collective-permute-start(bf16[4,128,128]{2,1,0:T(8,128)(2,1)S(1)} %get-tuple-element.57), channel_id=1, source_target_pairs={{0,4},{4,0},{8,12},{12,8},{16,20},{20,16},{24,28},{28,24},{1,5},{5... | collective-permute-start | bytes 393224 | tf_op jit(solution)/shard_map/ppermute | solution.py:171
  11.5 9.2 %copy-start = (bf16[1024,4096]{1,0:T(8,128)(2,1)S(1)}, bf16[1024,4096]{1,0:T(8,128)(2,1)}, u32[]{:S(2)}) copy-start(bf16[1024,4096]{1,0:T(8,128)(2,1)} %refs_1_.10) | copy-start | bytes 25165828
  11.6 5.6 %collective-permute-start.1 = (bf16[4,128,128]{2,1,0:T(8,128)(2,1)S(1)}, bf16[4,128,128]{2,1,0:T(8,128)(2,1)S(1)}, u32[]{:S(2)}, u32[]{:S(2)}) collective-permute-start(bf16[4,128,128]{2,1,0:T(8,128)(2,1)S(1)} %pair_total.2.refs_4_.refs_2_), channel_id=1, source_target_pairs={{0,8},{4,12},{8,0},{12,4},{16,24},{20,28},{24,16},{28,20},{1,9},{5... | collective-permute-start | bytes 393224 | tf_op jit(solution)/shard_map/ppermute | solution.py:188
  17.3 5.9 %collective-permute-start.2 = (bf16[4,128,128]{2,1,0:T(8,128)(2,1)S(1)}, bf16[4,128,128]{2,1,0:T(8,128)(2,1)S(1)}, u32[]{:S(2)}, u32[]{:S(2)}) collective-permute-start(bf16[4,128,128]{2,1,0:T(8,128)(2,1)S(1)} %get-tuple-element.59), channel_id=1, source_target_pairs={{0,16},{4,20},{8,24},{12,28},{1,17},{5,21},{9,25},{13,29},{2,18},{... | collective-permute-start | bytes 393224 | tf_op jit(solution)/shard_map/ppermute | solution.py:188
  23.3 1.4 %collective-permute-start.3 = (bf16[4,128,128]{2,1,0:T(8,128)(2,1)S(1)}, bf16[4,128,128]{2,1,0:T(8,128)(2,1)S(1)}, u32[]{:S(2)}, u32[]{:S(2)}) collective-permute-start(bf16[4,128,128]{2,1,0:T(8,128)(2,1)S(1)} %get-tuple-element.62), channel_id=1, source_target_pairs={{0,4},{4,0},{8,12},{12,8},{16,20},{20,16},{24,28},{28,24},{1,5},{5... | collective-permute-start | bytes 393224 | tf_op jit(solution)/shard_map/ppermute | solution.py:202
  30.7 14.9 %collective-permute-start.6 = (bf16[256,1024]{1,0:T(8,128)(2,1)S(1)}, bf16[256,1024]{1,0:T(8,128)(2,1)S(1)}, u32[]{:S(2)}, u32[]{:S(2)}) collective-permute-start(bf16[256,1024]{1,0:T(8,128)(2,1)S(1)} %get-tuple-element.66), channel_id=1, source_target_pairs={{0,1},{1,0},{2,3},{3,2},{4,5},{5,4},{6,7},{7,6},{8,9},{9,8},{10,11... | collective-permute-start | bytes 1572872 | tf_op jit(solution)/shard_map/ppermute | solution.py:504
  32.5 13.1 %collective-permute-start.7 = (bf16[256,1024]{1,0:T(8,128)(2,1)S(1)}, bf16[256,1024]{1,0:T(8,128)(2,1)S(1)}, u32[]{:S(2)}, u32[]{:S(2)}) collective-permute-start(bf16[256,1024]{1,0:T(8,128)(2,1)S(1)} %get-tuple-element.67), channel_id=1, source_target_pairs={{1,2},{2,1},{5,6},{6,5},{9,10},{10,9},{13,14},{14,13},{17,18},{18,... | collective-permute-start | bytes 1572872 | tf_op jit(solution)/shard_map/ppermute | solution.py:504
  33.2 23.7 %collective-permute-start.10 = (bf16[256,1024]{1,0:T(8,128)(2,1)S(1)}, bf16[256,1024]{1,0:T(8,128)(2,1)S(1)}, u32[]{:S(2)}, u32[]{:S(2)}) collective-permute-start(bf16[256,1024]{1,0:T(8,128)(2,1)S(1)} %get-tuple-element.70), channel_id=1, source_target_pairs={{0,1},{1,0},{2,3},{3,2},{4,5},{5,4},{6,7},{7,6},{8,9},{9,8},{10,11... | collective-permute-start | bytes 1572872 | tf_op jit(solution)/shard_map/ppermute | solution.py:505
  35.2 21.7 %collective-permute-start.11 = (bf16[256,1024]{1,0:T(8,128)(2,1)S(1)}, bf16[256,1024]{1,0:T(8,128)(2,1)S(1)}, u32[]{:S(2)}, u32[]{:S(2)}) collective-permute-start(bf16[256,1024]{1,0:T(8,128)(2,1)S(1)} %get-tuple-element.71), channel_id=1, source_target_pairs={{1,2},{2,1},{5,6},{6,5},{9,10},{10,9},{13,14},{14,13},{17,18},{18,... | collective-permute-start | bytes 1572872 | tf_op jit(solution)/shard_map/ppermute | solution.py:505
  45.8 22.2 %collective-permute-start.8 = (bf16[256,1024]{1,0:T(8,128)(2,1)S(1)}, bf16[256,1024]{1,0:T(8,128)(2,1)S(1)}, u32[]{:S(2)}, u32[]{:S(2)}) collective-permute-start(bf16[256,1024]{1,0:T(8,128)(2,1)S(1)} %get-tuple-element.69), channel_id=1, source_target_pairs={{0,1},{1,0},{2,3},{3,2},{4,5},{5,4},{6,7},{7,6},{8,9},{9,8},{10,11... | collective-permute-start | bytes 1572872 | tf_op jit(solution)/shard_map/ppermute | solution.py:509
  49.8 18.3 %collective-permute-start.9 = (bf16[256,1024]{1,0:T(8,128)(2,1)S(1)}, bf16[256,1024]{1,0:T(8,128)(2,1)S(1)}, u32[]{:S(2)}, u32[]{:S(2)}) collective-permute-start(bf16[256,1024]{1,0:T(8,128)(2,1)S(1)} %get-tuple-element.68.refs_3_), channel_id=1, source_target_pairs={{1,2},{2,1},{5,6},{6,5},{9,10},{10,9},{13,14},{14,13},{17,18},{18,... | collective-permute-start | bytes 1572872 | tf_op jit(solution)/shard_map/ppermute | solution.py:509
  57.1 22.2 %collective-permute-start.14 = (bf16[256,1024]{1,0:T(8,128)(2,1)S(1)}, bf16[256,1024]{1,0:T(8,128)(2,1)S(1)}, u32[]{:S(2)}, u32[]{:S(2)}) collective-permute-start(bf16[256,1024]{1,0:T(8,128)(2,1)S(1)} %get-tuple-element.79), channel_id=1, source_target_pairs={{0,1},{1,0},{2,3},{3,2},{4,5},{5,4},{6,7},{7,6},{8,9},{9,8},{10,11... | collective-permute-start | bytes 1572872 | tf_op jit(solution)/shard_map/ppermute | solution.py:514
  61.0 20.6 %collective-permute-start.15 = (bf16[256,1024]{1,0:T(8,128)(2,1)S(1)}, bf16[256,1024]{1,0:T(8,128)(2,1)S(1)}, u32[]{:S(2)}, u32[]{:S(2)}) collective-permute-start(bf16[256,1024]{1,0:T(8,128)(2,1)S(1)} %get-tuple-element.72.refs_5_), channel_id=1, source_target_pairs={{1,2},{2,1},{5,6},{6,5},{9,10},{10,9},{13,14},{14,13},{17,18},{18,... | collective-permute-start | bytes 1572872 | tf_op jit(solution)/shard_map/ppermute | solution.py:514
  68.2 32.8 %collective-permute-start.12 = (bf16[256,1024]{1,0:T(8,128)(2,1)S(1)}, bf16[256,1024]{1,0:T(8,128)(2,1)S(1)}, u32[]{:S(2)}, u32[]{:S(2)}) collective-permute-start(bf16[256,1024]{1,0:T(8,128)(2,1)S(1)} %get-tuple-element.73.refs_9_), channel_id=1, source_target_pairs={{0,1},{1,0},{2,3},{3,2},{4,5},{5,4},{6,7},{7,6},{8,9},{9,8},{10,11... | collective-permute-start | bytes 1572872 | tf_op jit(solution)/shard_map/ppermute | solution.py:520
  74.4 26.6 %collective-permute-start.13 = (bf16[256,1024]{1,0:T(8,128)(2,1)S(1)}, bf16[256,1024]{1,0:T(8,128)(2,1)S(1)}, u32[]{:S(2)}, u32[]{:S(2)}) collective-permute-start(bf16[256,1024]{1,0:T(8,128)(2,1)S(1)} %get-tuple-element.78), channel_id=1, source_target_pairs={{1,2},{2,1},{5,6},{6,5},{9,10},{10,9},{13,14},{14,13},{17,18},{18,... | collective-permute-start | bytes 1572872 | tf_op jit(solution)/shard_map/ppermute | solution.py:527
  81.6 2.7 %collective-permute-start.18 = (bf16[4,128,128]{2,1,0:T(8,128)(2,1)S(1)}, bf16[4,128,128]{2,1,0:T(8,128)(2,1)S(1)}, u32[]{:S(2)}, u32[]{:S(2)}) collective-permute-start(bf16[4,128,128]{2,1,0:T(8,128)(2,1)S(1)} %get-tuple-element.83.refs_4_), channel_id=1, source_target_pairs={{0,4},{4,0},{8,12},{12,8},{16,20},{20,16},{24,28},{28,24},{1,5},{5... | collective-permute-start | bytes 393224 | tf_op jit(solution)/shard_map/ppermute | solution.py:171
  81.8 19.2 %collective-permute-start.16 = (bf16[256,1024]{1,0:T(8,128)(2,1)S(1)}, bf16[256,1024]{1,0:T(8,128)(2,1)S(1)}, u32[]{:S(2)}, u32[]{:S(2)}) collective-permute-start(bf16[256,1024]{1,0:T(8,128)(2,1)S(1)} %get-tuple-element.84), channel_id=1, source_target_pairs={{0,1},{1,0},{2,3},{3,2},{4,5},{5,4},{6,7},{7,6},{8,9},{9,8},{10,11... | collective-permute-start | bytes 1572872 | tf_op jit(solution)/shard_map/ppermute | solution.py:538
  83.6 17.4 %collective-permute-start.17 = (bf16[256,1024]{1,0:T(8,128)(2,1)S(1)}, bf16[256,1024]{1,0:T(8,128)(2,1)S(1)}, u32[]{:S(2)}, u32[]{:S(2)}) collective-permute-start(bf16[256,1024]{1,0:T(8,128)(2,1)S(1)} %get-tuple-element.85), channel_id=1, source_target_pairs={{1,2},{2,1},{5,6},{6,5},{9,10},{10,9},{13,14},{14,13},{17,18},{18,... | collective-permute-start | bytes 1572872 | tf_op jit(solution)/shard_map/ppermute | solution.py:538
  84.4 5.7 %collective-permute-start.19 = (bf16[4,128,128]{2,1,0:T(8,128)(2,1)S(1)}, bf16[4,128,128]{2,1,0:T(8,128)(2,1)S(1)}, u32[]{:S(2)}, u32[]{:S(2)}) collective-permute-start(bf16[4,128,128]{2,1,0:T(8,128)(2,1)S(1)} %pair_total.3.refs_9_.refs_2_), channel_id=1, source_target_pairs={{0,8},{4,12},{8,0},{12,4},{16,24},{20,28},{24,16},{28,20},{1,9},{5... | collective-permute-start | bytes 393224 | tf_op jit(solution)/shard_map/ppermute | solution.py:188
  90.1 6.9 %collective-permute-start.20 = (bf16[4,128,128]{2,1,0:T(8,128)(2,1)S(1)}, bf16[4,128,128]{2,1,0:T(8,128)(2,1)S(1)}, u32[]{:S(2)}, u32[]{:S(2)}) collective-permute-start(bf16[4,128,128]{2,1,0:T(8,128)(2,1)S(1)} %get-tuple-element.90.refs_7_), channel_id=1, source_target_pairs={{16,0},{20,4},{24,8},{28,12},{17,1},{21,5},{25,9},{29,13},{18,2},{... | collective-permute-start | bytes 393224 | tf_op jit(solution)/shard_map/ppermute | solution.py:188
  97.1 1.4 %collective-permute-start.21 = (bf16[4,128,128]{2,1,0:T(8,128)(2,1)S(1)}, bf16[4,128,128]{2,1,0:T(8,128)(2,1)S(1)}, u32[]{:S(2)}, u32[]{:S(2)}) collective-permute-start(bf16[4,128,128]{2,1,0:T(8,128)(2,1)S(1)} %get-tuple-element.96), channel_id=1, source_target_pairs={{0,4},{4,0},{8,12},{12,8},{16,20},{20,16},{24,28},{28,24},{1,5},{5... | collective-permute-start | bytes 393224 | tf_op jit(solution)/shard_map/ppermute | solution.py:202
  (3 other events, 7.2 us)

commit v6 on v5

--- a/solution.py
+++ b/solution.py
@@ -18,13 +18,13 @@
     "setup": 100.0, "local_states": 0.8, "intra": 3.0, "back_own": 1.8, "pair_total": 0.1, "exchange_stage": 0.1,
     "exchange_last": 0.1, "normalise": 0.9, "project_3": 1.8, "project_2": 1.8, "project_1": 1.8,
     "project_0": 1.8, "back_1": 1.8, "pick": 0.3, "turn": 0.5, "back_2": 1.8, "attended_grads": 2.0, "first_grads": 2.0, "block": 0.5,
-    "query_grad": 0.01, "key_value_grads": 0.01, "last_grads": 0.01, "mixed": 1.3,
+    "query_grad": 0.01, "key_value_grads": 0.01, "last_grads": 0.01,
 }
 
 I_BLK, I_CORE, I_Z, I_DOCS = 0, 1, 2, 3
 
 
-def kernel(body, name, smem, ins, outs, deps=(), spare=8):
+def kernel(body, name, smem, ins, outs, deps=(), spare=8, hbm_outs=0, scratch=()):
     n, n_dep = len(smem) + len(ins), len(deps)
 
     def inner(*refs):
@@ -36,8 +36,9 @@
         inner,
         name=name,
         in_specs=[spec(pltpu.SMEM)] * len(smem) + [spec(pltpu.VMEM)] * len(ins) + [spec(pl.ANY)] * n_dep,
-        out_specs=[spec(pltpu.VMEM)] * len(outs),
+        out_specs=[spec(pltpu.HBM)] * hbm_outs + [spec(pltpu.VMEM)] * (len(outs) - hbm_outs),
         out_shape=list(outs),
+        scratch_shapes=list(scratch),
         compiler_params=pltpu.CompilerParams(vmem_limit_bytes=size + spare * MIB),
         cost_estimate=pl.CostEstimate(
             flops=int(MICROSECONDS[name] * RATE), bytes_accessed=0, transcendentals=0
@@ -380,16 +381,23 @@
             ref[r0:, at] = new[r0:]
 
 
-def last_body(c_ref, cout_ref, k_ref, v_ref, own_ref, back_ref, kp_ref, vp_ref, kg_ref, vg_ref, mark_ref):
+def last_body(c_ref, cout_ref, k_ref, v_ref, own_ref, back_ref, kp_ref, vp_ref, kg_hbm, vg_hbm, mark_ref, kg_ref, vg_ref, sem):
     mark_ref[...] = jnp.zeros_like(mark_ref)
-    wide = k_ref.shape[1]
     cout = cout_ref[...]
-    for h in range(wide // DH):
-        leaving = pick(c_ref, own_ref, back_ref, h)
-        kg = cout * dot(v_ref[:, head(h)], leaving, 1, 1)
-        vg = cout * dot(k_ref[:, head(h)], leaving, 1, 0)
-        kg_ref[:, head(h)] = (kp_ref[:, head(h)] + kg).astype(BF16)
-        vg_ref[:, head(h)] = (vp_ref[:, head(h)] + vg).astype(BF16)
+    copies = []
+    for i in range(k_ref.shape[1] // TILE):
+        for h in range(i * (TILE // DH), (i + 1) * (TILE // DH)):
+            leaving = pick(c_ref, own_ref, back_ref, h)
+            kg = cout * dot(v_ref[:, head(h)], leaving, 1, 1)
+            vg = cout * dot(k_ref[:, head(h)], leaving, 1, 0)
+            kg_ref[:, head(h)] = (kp_ref[:, head(h)] + kg).astype(BF16)
+            vg_ref[:, head(h)] = (vp_ref[:, head(h)] + vg).astype(BF16)
+        at = slice(i * TILE, (i + 1) * TILE)
+        for j, (src, dst) in enumerate(((kg_ref, kg_hbm), (vg_ref, vg_hbm))):
+            copies.append(pltpu.make_async_copy(src.at[:, at], dst.at[:, at], sem.at[j, i]))
+            copies[-1].start()
+    for copy in copies:
+        copy.wait()
 
 
 def sum_body(*refs):
@@ -432,19 +440,37 @@
     end_body(c_ref, p2_ref.at[rows, :], i2_ref, n3_ref)
 
 
-def turn_again_body(rows, n3_ref, i3_ref, p3_ref, p1_ref, s3_ref, s1_ref):
+def turn_again_body(rows, n3_ref, i3_ref, p3_ref, p1_ref, s1_ref, s3_ref):
     s3_ref[...] = p3_ref[rows, :] + n3_ref[...]
     s1_ref[...] = p1_ref[rows, :] + i3_ref[...]
 
 
-def mixed_body(p_ref, *refs):
-    out_ref = refs[-1]
-    r0 = 0
-    for a_ref, b_ref in zip(refs[:-1:2], refs[1:-1:2], strict=True):
-        rows = slice(r0, r0 + a_ref.shape[0])
-        total = p_ref[rows, :].astype(F32) + a_ref[...].astype(F32) + b_ref[...].astype(F32)
-        out_ref[rows, :] = total.astype(BF16)
-        r0 = rows.stop
+def mix_body(n_dep, p_ref, a_ref, b_ref, *refs):
+    total = p_ref[...].astype(F32) + a_ref[...].astype(F32) + b_ref[...].astype(F32)
+    refs[n_dep][...] = total.astype(BF16)
+    if len(refs) > n_dep + 1:
+        refs[-1][...] = jnp.zeros_like(refs[-1])
+
+
+def mix_half(half, p0, parts, deps, into=None):
+    tok, width = p0.shape
+    lot = tok // 2
+    mine = pl.BlockSpec((lot, width), lambda i: (half, 0))
+    whole = pl.BlockSpec((lot, width), lambda i: (0, 0))
+    extra = list(deps) + ([] if into is None else [into])
+    first = into is None
+    out = pl.pallas_call(
+        functools.partial(mix_body, len(extra)),
+        name="mixed",
+        grid=(1,),
+        in_specs=[mine, whole, whole] + [pl.BlockSpec(memory_space=pl.ANY)] * len(extra),
+        out_specs=[mine] + [pl.BlockSpec((8, DH), lambda i: (0, 0))] * first,
+        out_shape=[like((tok, width), BF16)] + [like((8, DH), F32)] * first,
+        input_output_aliases={} if first else {2 + len(extra): 0},
+        compiler_params=pltpu.CompilerParams(vmem_limit_bytes=12 * MIB),
+        cost_estimate=pl.CostEstimate(flops=RATE, bytes_accessed=0, transcendentals=0),
+    )(p0, *parts, *extra)
+    return out if first else out[0]
 
 
 def shards(q, k, v, lens, w, grad):
@@ -516,7 +542,7 @@
     (g2,) = kernel(ends_body, "pick", [], [coef, n2a, i2a, n2b, i2b], [part], [s2b])
     base = back_project([2], "back_2", [g2], base)
     (w3,) = kernel(functools.partial(block_body, 3), "block", [info], [w], [like((feats, width), BF16)], [base])
-    s3a, s1a = turn_again(0, [w3])
+    s1a, s3a = turn_again(0, [w3])
     n4a = lax.ppermute(s1a, "head", neighbours)
     ag_ins = [g3_inner, base, normed_f, inv, q]
     aga, states = kernel(
@@ -534,33 +560,32 @@
         functools.partial(att_grad_second_body, rows[1]), "attended_grads", [],
         [states, coef, cin, w3, n3b, *ag_ins], [like((tok // 2, feats), BF16), state, state], [qga],
     )
-    s3b, s1b = turn_again(1, [gsend])
+    ggot, gtotal = pair_total(gsend, gkeep, coefb)
+    s1b, s3b = turn_again(1, [gsend])
     n4b, i4b = lax.ppermute(s1b, "head", neighbours), lax.ppermute(s3b, "head", inner)
-    ggot, gtotal = pair_total(gsend, gkeep, coefb)
+    kp, vp = kernel(
+        functools.partial(key_value_body, rows[1]), "key_value_grads", [],
+        [low_t, q, k, v, ag, kga, vga], [wide_f, wide_f], [gtotal],
+    )
     grads = []
 
-    def beside_first(sent):
-        grads.extend(kernel(
+    def beside_second(sent):
+        query_grad, mark = kernel(
             functools.partial(query_grad_body, rows[1]), "query_grad", [],
-            [low, coef, cin, k, v, ag, own, other, qga],
-            [wide_b, like((8, DH), F32)], [sent],
-        ))
-        return grads[1:2]
-
-    def beside_second(sent):
-        grads.extend(kernel(
-            functools.partial(key_value_body, rows[1]), "key_value_grads", [],
-            [low_t, q, k, v, ag, kga, vga], [wide_f, wide_f], [sent],
-        ))
-        return grads[2:3]
-
-    leaving, leaving_other = exchange(gtotal, gkeep, ggot, coefb, False, [beside_first, beside_second])
-    query_grad, _, kp, vp = grads
+            [low, coef, cin, k, v, ag, own, other, qga], [wide_b, like((8, DH), F32)], [sent],
+        )
+        grads.append(query_grad)
+        return [mark]
+
+    leaving, leaving_other = exchange(gtotal, gkeep, ggot, coefb, False, [lambda _: [kp], beside_second])
+    (query_grad,) = grads
+    mixed, mark = mix_half(0, p0, [n4a, i4a], [leaving])
     key_grad, value_grad, mark = kernel(
         last_body, "last_grads", [], [coef, cout, k, v, leaving, leaving_other, kp, vp],
-        [wide_b, wide_b, like((8, DH), F32)],
-    )
-    (mixed,) = kernel(mixed_body, "mixed", [], [p0, n4a, i4a, n4b, i4b], [part], [mark])
+        [wide_b, wide_b, like((8, DH), F32)], [mark], hbm_outs=2,
+        scratch=[pltpu.VMEM((tok, feats), BF16)] * 2 + [pltpu.SemaphoreType.DMA((2, feats // TILE))],
+    )
+    mixed = mix_half(1, p0, [n4b, i4b], [mark], mixed)
     return mixed, query_grad, key_grad, value_grad
 
 

time: 103 us -> 102 us (level)
    pallas_call x0 -> x2, Pallas kernels: none -> 1.97 us  [mix_half(): pl.pallas_call(functools.partial(mix_body, len(extra)), name='mixed', gri...]
    pallas_call x31 -> x30, Pallas kernels: 36.6 us -> 34.8 us  [kernel(): pl.pallas_call(inner, name=name, in_specs=[spec(pltpu.SMEM)] * len(smem)...]
  transfers between devices with their start and end apart: 22 -> 22, of which waited for: 12 -> 12; matrix products, arithmetic and copies ran while one was open for 1% -> 1% of each run, Pallas kernels for 34% -> 35%
where the time goes in v6:
time: 102 us
  Pallas kernels  36.8 us (36%)
  starting transfers between devices  36.7 us (36%)
  waiting for transfers between devices  25.5 us (25%)
    pallas_call x30, Pallas kernels, kernel(): pl.pallas_call(inner, name=name, in_specs=[spec(pltpu.SMEM)] * len(smem)...  34.8 us
    ppermute x4, starting transfers between devices, exchange(): others.append(lax.ppermute(total, 'ctx', pairs))  8.05 us
    ppermute x1, waiting for transfers between devices, shards(): lax.ppermute(n2a, 'head', neighbours)  7.9 us
    ppermute x4, waiting for transfers between devices, exchange(): others.append(lax.ppermute(total, 'ctx', pairs))  6.38 us
    ppermute x1, starting transfers between devices, shards(): g1 = lax.ppermute(grad, 'head', neighbours)  5.85 us
    ppermute x1, starting transfers between devices, shards(): lax.ppermute(n3a, 'head', neighbours)  3.97 us
    ppermute x1, starting transfers between devices, shards(): lax.ppermute(n3b, 'head', neighbours)  3.97 us
    ppermute x1, starting transfers between devices, shards(): n4a = lax.ppermute(s1a, 'head', neighbours)  3.97 us
  transfers between devices with their start and end apart: 22, of which 12 were waited for; matrix products, arithmetic and copies ran while one was open for 1% of the time, Pallas kernels for 35%

profile of v6, /device:TPU:0, one launch (start us, length us, event | category | flops | bytes accessed | tf_op | source)
XLA Modules:
  0.0 101.6 jit_solution(13257680100326410855)
XLA Ops:
  1.4 5.8 %collective-permute-start.4 = (bf16[512,1024]{1,0:T(8,128)(2,1)}, bf16[512,1024]{1,0:T(8,128)(2,1)S(1)}, u32[]{:S(2)}, u32[]{:S(2)}) collective-permute-start(bf16[512,1024]{1,0:T(8,128)(2,1)} %refs_2_.12), channel_id=1, source_target_pairs={{0,1},{1,0},{2,3},{3,2},{4,5},{5,4},{6,7},{7,6},{8,9},{9,8},{10,11... | collective-permute-start | bytes 3145736 | tf_op jit(solution)/shard_map/ppermute | solution.py:501
  13.1 2.5 %intra.1.refs_3_.refs_5_ = f32[512,1024]{1,0:T(8,128)S(1)} custom-call(s32[512,128]{1,0:T(8,128)S(1)} %get-tuple-element.60.refs_0_, bf16[512,1024]{1,0:T(8,128)(2,1)S(1)} %copy-done.1, bf16[512,1024]{1,0:T(8,128)(2,1)S(1)} %copy-done.2, bf16[512,1024]{1,0:T(8,128)(2,1)S(1)} %copy-done.3, bf16[4,128,128]{2,1,0:T(8,128)(2,1)S(1)} %pair_total.2.refs_4_.refs_2_), custom_call_target="tpu_custom_call" | custom-call | flops 300000000 | tf_op jit(solution)/shard_map/intra/pallas_call | solution.py:35
  17.3 3.4 %collective-permute-start.2 = (bf16[4,128,128]{2,1,0:T(8,128)(2,1)S(1)}, bf16[4,128,128]{2,1,0:T(8,128)(2,1)S(1)}, u32[]{:S(2)}, u32[]{:S(2)}) collective-permute-start(bf16[4,128,128]{2,1,0:T(8,128)(2,1)S(1)} %get-tuple-element.61), channel_id=1, source_target_pairs={{0,16},{4,20},{8,24},{12,28},{1,17},{5,21},{9,25},{13,29},{2,18},{... | collective-permute-start | bytes 393224 | tf_op jit(solution)/shard_map/ppermute | solution.py:189
  20.7 1.8 %back_own.1.refs_5_.refs_3_ = f32[512,1024]{1,0:T(8,128)S(1)} custom-call(s32[7]{0:T(128)S(1)} %pad_add_fusion.refs_0_, bf16[1024,4096]{1,0:T(8,128)(2,1)S(1)} %copy-done, bf16[512,1024]{1,0:T(8,128)(2,1)S(1)} %copy-done.4, f32[512,1024]{1,0:T(8,128)S(1)} %intra.1.refs_3_.refs_5_), custom_call_target="tpu_custom_call" | custom-call | flops 180000000 | tf_op jit(solution)/shard_map/back_own/pallas_call | solution.py:35
  25.7 1.8 %project_3.1.refs_2_.refs_3_ = bf16[512,1024]{1,0:T(8,128)(2,1)S(1)} custom-call(s32[7]{0:T(128)S(1)} %pad_add_fusion.refs_0_, bf16[512,1024]{1,0:T(8,128)(2,1)S(1)} %get-tuple-element.65.refs_1_, bf16[1024,4096]{1,0:T(8,128)(2,1)S(1)} %copy-done), custom_call_target="tpu_custom_call" | custom-call | flops 180000000 | tf_op jit(solution)/shard_map/project_3/pallas_call | solution.py:35
  27.6 2.7 %collective-permute-done.4.refs_1_.refs_2_ = bf16[512,1024]{1,0:T(8,128)(2,1)S(1)} collective-permute-done((bf16[512,1024]{1,0:T(8,128)(2,1)}, bf16[512,1024]{1,0:T(8,128)(2,1)S(1)}, u32[]{:S(2)}, u32[]{:S(2)}) %collective-permute-start.4) | collective-permute-done | bytes 1048608 | tf_op jit(solution)/shard_map/ppermute | solution.py:501
  33.2 2.0 %collective-permute-start.8 = (bf16[256,1024]{1,0:T(8,128)(2,1)S(1)}, bf16[256,1024]{1,0:T(8,128)(2,1)S(1)}, u32[]{:S(2)}, u32[]{:S(2)}) collective-permute-start(bf16[256,1024]{1,0:T(8,128)(2,1)S(1)} %get-tuple-element.71), channel_id=1, source_target_pairs={{0,1},{1,0},{2,3},{3,2},{4,5},{5,4},{6,7},{7,6},{8,9},{9,8},{10,11... | collective-permute-start | bytes 1572872 | tf_op jit(solution)/shard_map/ppermute | solution.py:531
  35.9 1.8 %project_2.1.refs_2_ = bf16[512,1024]{1,0:T(8,128)(2,1)S(1)} custom-call(s32[7]{0:T(128)S(1)} %pad_add_fusion.refs_0_, bf16[512,1024]{1,0:T(8,128)(2,1)S(1)} %get-tuple-element.65.refs_1_, bf16[1024,4096]{1,0:T(8,128)(2,1)S(1)} %copy-done, bf16[512,1024]{1,0:T(8,128)(2,1)S(1)} %project_3.1.refs_2_.refs_3_), custom_call_target="tpu_custom_call" | custom-call | flops 180000000 | tf_op jit(solution)/shard_map/project_2/pallas_call | solution.py:35
  37.7 7.9 %collective-permute-done.6.refs_1_ = bf16[256,1024]{1,0:T(8,128)(2,1)S(1)} collective-permute-done((bf16[256,1024]{1,0:T(8,128)(2,1)S(1)}, bf16[256,1024]{1,0:T(8,128)(2,1)S(1)}, u32[]{:S(2)}, u32[]{:S(2)}) %collective-permute-start.6) | collective-permute-done | bytes 524320 | tf_op jit(solution)/shard_map/ppermute | solution.py:530
  45.8 4.0 %collective-permute-start.12 = (bf16[256,1024]{1,0:T(8,128)(2,1)S(1)}, bf16[256,1024]{1,0:T(8,128)(2,1)S(1)}, u32[]{:S(2)}, u32[]{:S(2)}) collective-permute-start(bf16[256,1024]{1,0:T(8,128)(2,1)S(1)} %get-tuple-element.75), channel_id=1, source_target_pairs={{0,1},{1,0},{2,3},{3,2},{4,5},{5,4},{6,7},{7,6},{8,9},{9,8},{10,11... | collective-permute-start | bytes 1572872 | tf_op jit(solution)/shard_map/ppermute | solution.py:535
  50.5 1.8 %project_1.1.refs_3_ = bf16[512,1024]{1,0:T(8,128)(2,1)S(1)} custom-call(s32[7]{0:T(128)S(1)} %pad_add_fusion.refs_0_, bf16[512,1024]{1,0:T(8,128)(2,1)S(1)} %get-tuple-element.65.refs_1_, bf16[1024,4096]{1,0:T(8,128)(2,1)S(1)} %copy-done, bf16[256,1024]{1,0:T(8,128)(2,1)S(1)} %get-tuple-element.70.refs_3_), custom_call_target="tpu_custom_call" | custom-call | flops 180000000 | tf_op jit(solution)/shard_map/project_1/pallas_call | solution.py:35
  52.3 1.8 %project_0.1.refs_4_.p_ref = bf16[512,1024]{1,0:T(8,128)(2,1)S(1)} custom-call(s32[7]{0:T(128)S(1)} %pad_add_fusion.refs_0_, bf16[512,1024]{1,0:T(8,128)(2,1)S(1)} %get-tuple-element.65.refs_1_, bf16[1024,4096]{1,0:T(8,128)(2,1)S(1)} %copy-done, bf16[512,1024]{1,0:T(8,128)(2,1)S(1)} %project_1.1.refs_3_), custom_call_target="tpu_custom_call" | custom-call | flops 180000000 | tf_op jit(solution)/shard_map/project_0/pallas_call | solution.py:35
  54.1 1.8 %back_1.1.refs_4_.refs_3_ = f32[512,1024]{1,0:T(8,128)S(1)} custom-call(s32[7]{0:T(128)S(1)} %pad_add_fusion.refs_0_, bf16[1024,4096]{1,0:T(8,128)(2,1)S(1)} %copy-done, bf16[512,1024]{1,0:T(8,128)(2,1)S(1)} %collective-permute-done.4.refs_1_.refs_2_, f32[512,1024]{1,0:T(8,128)S(1)} %back_own.1.refs_5_.refs_3_, bf16[512,1024]{1,0:T(8,128)(2,1)S(1)} %project_0.1.refs_4_.p_ref), custom_call_target="tpu_custom_call" | custom-call | flops 180000000 | tf_op jit(solution)/shard_map/back_1/pallas_call | solution.py:35
  57.1 4.0 %collective-permute-start.10 = (bf16[256,1024]{1,0:T(8,128)(2,1)S(1)}, bf16[256,1024]{1,0:T(8,128)(2,1)S(1)}, u32[]{:S(2)}, u32[]{:S(2)}) collective-permute-start(bf16[256,1024]{1,0:T(8,128)(2,1)S(1)} %get-tuple-element.73), channel_id=1, source_target_pairs={{0,1},{1,0},{2,3},{3,2},{4,5},{5,4},{6,7},{7,6},{8,9},{9,8},{10,11... | collective-permute-start | bytes 1572872 | tf_op jit(solution)/shard_map/ppermute | solution.py:540
  62.2 1.8 %back_2.1.refs_2_.refs_5_.refs_6_ = f32[512,1024]{1,0:T(8,128)S(1)} custom-call(s32[7]{0:T(128)S(1)} %pad_add_fusion.refs_0_, bf16[1024,4096]{1,0:T(8,128)(2,1)S(1)} %copy-done, bf16[512,1024]{1,0:T(8,128)(2,1)S(1)} %pick.3.refs_2_, f32[512,1024]{1,0:T(8,128)S(1)} %back_1.1.refs_4_.refs_3_), custom_call_target="tpu_custom_call" | custom-call | flops 180000000 | tf_op jit(solution)/shard_map/back_2/pallas_call | solution.py:35
  64.8 3.3 %collective-permute-done.12.refs_0_.refs_3_ = bf16[256,1024]{1,0:T(8,128)(2,1)S(1)} collective-permute-done((bf16[256,1024]{1,0:T(8,128)(2,1)S(1)}, bf16[256,1024]{1,0:T(8,128)(2,1)S(1)}, u32[]{:S(2)}, u32[]{:S(2)}) %collective-permute-start.12) | collective-permute-done | bytes 524320 | tf_op jit(solution)/shard_map/ppermute | solution.py:535
  68.2 4.0 %collective-permute-start.20 = (bf16[256,1024]{1,0:T(8,128)(2,1)S(1)}, bf16[256,1024]{1,0:T(8,128)(2,1)S(1)}, u32[]{:S(2)}, u32[]{:S(2)}) collective-permute-start(bf16[256,1024]{1,0:T(8,128)(2,1)S(1)} %get-tuple-element.78.refs_9_), channel_id=1, source_target_pairs={{0,1},{1,0},{2,3},{3,2},{4,5},{5,4},{6,7},{7,6},{8,9},{9,8},{10,11... | collective-permute-start | bytes 1572872 | tf_op jit(solution)/shard_map/ppermute | solution.py:546
  72.2 2.2 %attended_grads.2 = (bf16[256,1024]{1,0:T(8,128)(2,1)S(1)}, f32[8,128,128]{2,1,0:T(8,128)S(1)}) custom-call(f32[32,128]{1,0:T(8,128)S(1)} %get-tuple-element.55.refs_0_.refs_2_.refs_1_, f32[512,128]{1,0:T(8,128)S(1)} %get-tuple-element.56.refs_1_.refs_3_.refs_2_, bf16[1024,1024]{1,0:T(8,128)(2,1)S(1)} %block.1.refs_4_.refs_2_.refs_3_, ...), custom_call_target="tpu_custom_call" | custom-call | flops 200000000 | tf_op jit(solution)/shard_map/attended_grads/pallas_call | solution.py:35
  75.1 2.9 %first_grads.1 = (bf16[256,1024]{1,0:T(8,128)(2,1)S(1)}, f32[256,1024]{1,0:T(8,128)S(1)}, f32[256,1024]{1,0:T(8,128)S(1)}) custom-call(s32[512,128]{1,0:T(8,128)S(1)} %get-tuple-element.60.refs_0_, s32[8,512]{1,0:T(8,128)S(1)} %get-tuple-element.80.refs_1_.refs_0_, f32[32,128]{1,0:T(8,128)S(1)} %get-tuple-element.55.refs_0_.refs_2_.refs_1_, ...), custom_call_target="tpu_custom_call" | custom-call | flops 200000000 | tf_op jit(solution)/shard_map/first_grads/pallas_call | solution.py:35
  79.3 2.3 %attended_grads.3 = (bf16[256,1024]{1,0:T(8,128)(2,1)S(1)}, bf16[4,128,128]{2,1,0:T(8,128)(2,1)S(1)}, bf16[4,128,128]{2,1,0:T(8,128)(2,1)S(1)}) custom-call(f32[8,128,128]{2,1,0:T(8,128)S(1)} %get-tuple-element.79.refs_0_, f32[32,128]{1,0:T(8,128)S(1)} %get-tuple-element.55.refs_0_.refs_2_.refs_1_, f32[512,128]{1,0:T(8,128)S(1)} %get-tuple-element.56.refs_1_.refs_3_.refs_2_, ...), custom_call_target="tpu_custom_call" | custom-call | flops 200000000 | tf_op jit(solution)/shard_map/attended_grads/pallas_call | solution.py:35
  85.9 2.4 %key_value_grads.1 = (f32[512,1024]{1,0:T(8,128)S(1)}, f32[512,1024]{1,0:T(8,128)S(1)}) custom-call(s32[8,512]{1,0:T(8,128)S(1)} %get-tuple-element.80.refs_1_.refs_0_, bf16[512,1024]{1,0:T(8,128)(2,1)S(1)} %copy-done.1, bf16[512,1024]{1,0:T(8,128)(2,1)S(1)} %copy-done.2, bf16[512,1024]{1,0:T(8,128)(2,1)S(1)} %copy-done.3, ...), custom_call_target="tpu_custom_call" | custom-call | flops 1000000 | tf_op jit(solution)/shard_map/key_value_grads/pallas_call | solution.py:35
  91.6 2.9 %query_grad.1 = (bf16[512,1024]{1,0:T(8,128)(2,1)}, f32[8,128]{1,0:T(8,128)S(1)}) custom-call(s32[512,128]{1,0:T(8,128)S(1)} %get-tuple-element.60.refs_0_, f32[32,128]{1,0:T(8,128)S(1)} %get-tuple-element.55.refs_0_.refs_2_.refs_1_, f32[512,128]{1,0:T(8,128)S(1)} %get-tuple-element.56.refs_1_.refs_3_.refs_2_, bf16[512,1024]{1,0:T(8,128)(2,1)S(1)} %copy-done.2, ...), custom_call_target="tpu_custom_call" | custom-call | flops 1000000 | tf_op jit(solution)/shard_map/query_grad/pallas_call | solution.py:35
  94.5 2.4 %collective-permute-done.18.refs_1_ = bf16[4,128,128]{2,1,0:T(8,128)(2,1)S(1)} collective-permute-done((bf16[4,128,128]{2,1,0:T(8,128)(2,1)S(1)}, bf16[4,128,128]{2,1,0:T(8,128)(2,1)S(1)}, u32[]{:S(2)}, u32[]{:S(2)}) %collective-permute-start.18) | collective-permute-done | bytes 131104 | tf_op jit(solution)/shard_map/ppermute | solution.py:189
  98.5 2.1 %last_grads.1 = (bf16[512,1024]{1,0:T(8,128)(2,1)}, bf16[512,1024]{1,0:T(8,128)(2,1)}, f32[8,128]{1,0:T(8,128)S(1)}) custom-call(f32[32,128]{1,0:T(8,128)S(1)} %get-tuple-element.55.refs_0_.refs_2_.refs_1_, f32[512,128]{1,0:T(8,128)S(1)} %get-tuple-element.57.refs_1_, bf16[512,1024]{1,0:T(8,128)(2,1)S(1)} %copy-done.2, bf16[512,1024]{1,0:T(8,128)(2,1)S(1)} %copy-done.3, ...), custom_call_target="tpu_custom_call" | custom-call | flops 1000000 | tf_op jit(solution)/shard_map/last_grads/pallas_call | solution.py:35
  (63 shorter events, 31.1 us)
Async XLA Ops:
  0.6 26.9 %collective-permute-start.5 = (bf16[512,1024]{1,0:T(8,128)(2,1)}, bf16[512,1024]{1,0:T(8,128)(2,1)S(1)}, u32[]{:S(2)}, u32[]{:S(2)}) collective-permute-start(bf16[512,1024]{1,0:T(8,128)(2,1)} %refs_2_.12), channel_id=1, source_target_pairs={{1,2},{2,1},{5,6},{6,5},{9,10},{10,9},{13,14},{14,13},{17,18},{18,... | collective-permute-start | bytes 3145736 | tf_op jit(solution)/shard_map/ppermute | solution.py:502
  1.4 28.9 %collective-permute-start.4 = (bf16[512,1024]{1,0:T(8,128)(2,1)}, bf16[512,1024]{1,0:T(8,128)(2,1)S(1)}, u32[]{:S(2)}, u32[]{:S(2)}) collective-permute-start(bf16[512,1024]{1,0:T(8,128)(2,1)} %refs_2_.12), channel_id=1, source_target_pairs={{0,1},{1,0},{2,3},{3,2},{4,5},{5,4},{6,7},{7,6},{8,9},{9,8},{10,11... | collective-permute-start | bytes 3145736 | tf_op jit(solution)/shard_map/ppermute | solution.py:501
  9.5 11.2 %copy-start.4 = (bf16[512,1024]{1,0:T(8,128)(2,1)S(1)}, bf16[512,1024]{1,0:T(8,128)(2,1)}, u32[]{:S(2)}) copy-start(bf16[512,1024]{1,0:T(8,128)(2,1)} %refs_2_.12) | copy-start | bytes 3145732
  10.1 1.4 %collective-permute-start = (bf16[4,128,128]{2,1,0:T(8,128)(2,1)S(1)}, bf16[4,128,128]{2,1,0:T(8,128)(2,1)S(1)}, u32[]{:S(2)}, u32[]{:S(2)}) collective-permute-start(bf16[4,128,128]{2,1,0:T(8,128)(2,1)S(1)} %get-tuple-element.59), channel_id=1, source_target_pairs={{0,4},{4,0},{8,12},{12,8},{16,20},{20,16},{24,28},{28,24},{1,5},{5... | collective-permute-start | bytes 393224 | tf_op jit(solution)/shard_map/ppermute | solution.py:172
  11.5 9.2 %copy-start = (bf16[1024,4096]{1,0:T(8,128)(2,1)S(1)}, bf16[1024,4096]{1,0:T(8,128)(2,1)}, u32[]{:S(2)}) copy-start(bf16[1024,4096]{1,0:T(8,128)(2,1)} %refs_1_.10) | copy-start | bytes 25165828
  11.6 5.6 %collective-permute-start.1 = (bf16[4,128,128]{2,1,0:T(8,128)(2,1)S(1)}, bf16[4,128,128]{2,1,0:T(8,128)(2,1)S(1)}, u32[]{:S(2)}, u32[]{:S(2)}) collective-permute-start(bf16[4,128,128]{2,1,0:T(8,128)(2,1)S(1)} %pair_total.2.refs_4_.refs_2_), channel_id=1, source_target_pairs={{0,8},{4,12},{8,0},{12,4},{16,24},{20,28},{24,16},{28,20},{1,9},{5... | collective-permute-start | bytes 393224 | tf_op jit(solution)/shard_map/ppermute | solution.py:189
  17.3 5.9 %collective-permute-start.2 = (bf16[4,128,128]{2,1,0:T(8,128)(2,1)S(1)}, bf16[4,128,128]{2,1,0:T(8,128)(2,1)S(1)}, u32[]{:S(2)}, u32[]{:S(2)}) collective-permute-start(bf16[4,128,128]{2,1,0:T(8,128)(2,1)S(1)} %get-tuple-element.61), channel_id=1, source_target_pairs={{0,16},{4,20},{8,24},{12,28},{1,17},{5,21},{9,25},{13,29},{2,18},{... | collective-permute-start | bytes 393224 | tf_op jit(solution)/shard_map/ppermute | solution.py:189
  23.3 1.4 %collective-permute-start.3 = (bf16[4,128,128]{2,1,0:T(8,128)(2,1)S(1)}, bf16[4,128,128]{2,1,0:T(8,128)(2,1)S(1)}, u32[]{:S(2)}, u32[]{:S(2)}) collective-permute-start(bf16[4,128,128]{2,1,0:T(8,128)(2,1)S(1)} %get-tuple-element.64), channel_id=1, source_target_pairs={{0,4},{4,0},{8,12},{12,8},{16,20},{20,16},{24,28},{28,24},{1,5},{5... | collective-permute-start | bytes 393224 | tf_op jit(solution)/shard_map/ppermute | solution.py:203
  30.7 14.9 %collective-permute-start.6 = (bf16[256,1024]{1,0:T(8,128)(2,1)S(1)}, bf16[256,1024]{1,0:T(8,128)(2,1)S(1)}, u32[]{:S(2)}, u32[]{:S(2)}) collective-permute-start(bf16[256,1024]{1,0:T(8,128)(2,1)S(1)} %get-tuple-element.68), channel_id=1, source_target_pairs={{0,1},{1,0},{2,3},{3,2},{4,5},{5,4},{6,7},{7,6},{8,9},{9,8},{10,11... | collective-permute-start | bytes 1572872 | tf_op jit(solution)/shard_map/ppermute | solution.py:530
  32.5 13.1 %collective-permute-start.7 = (bf16[256,1024]{1,0:T(8,128)(2,1)S(1)}, bf16[256,1024]{1,0:T(8,128)(2,1)S(1)}, u32[]{:S(2)}, u32[]{:S(2)}) collective-permute-start(bf16[256,1024]{1,0:T(8,128)(2,1)S(1)} %get-tuple-element.69), channel_id=1, source_target_pairs={{1,2},{2,1},{5,6},{6,5},{9,10},{10,9},{13,14},{14,13},{17,18},{18,... | collective-permute-start | bytes 1572872 | tf_op jit(solution)/shard_map/ppermute | solution.py:530
  33.2 23.7 %collective-permute-start.8 = (bf16[256,1024]{1,0:T(8,128)(2,1)S(1)}, bf16[256,1024]{1,0:T(8,128)(2,1)S(1)}, u32[]{:S(2)}, u32[]{:S(2)}) collective-permute-start(bf16[256,1024]{1,0:T(8,128)(2,1)S(1)} %get-tuple-element.71), channel_id=1, source_target_pairs={{0,1},{1,0},{2,3},{3,2},{4,5},{5,4},{6,7},{7,6},{8,9},{9,8},{10,11... | collective-permute-start | bytes 1572872 | tf_op jit(solution)/shard_map/ppermute | solution.py:531
  35.2 21.7 %collective-permute-start.9 = (bf16[256,1024]{1,0:T(8,128)(2,1)S(1)}, bf16[256,1024]{1,0:T(8,128)(2,1)S(1)}, u32[]{:S(2)}, u32[]{:S(2)}) collective-permute-start(bf16[256,1024]{1,0:T(8,128)(2,1)S(1)} %get-tuple-element.72), channel_id=1, source_target_pairs={{1,2},{2,1},{5,6},{6,5},{9,10},{10,9},{13,14},{14,13},{17,18},{18,... | collective-permute-start | bytes 1572872 | tf_op jit(solution)/shard_map/ppermute | solution.py:531
  45.8 22.2 %collective-permute-start.12 = (bf16[256,1024]{1,0:T(8,128)(2,1)S(1)}, bf16[256,1024]{1,0:T(8,128)(2,1)S(1)}, u32[]{:S(2)}, u32[]{:S(2)}) collective-permute-start(bf16[256,1024]{1,0:T(8,128)(2,1)S(1)} %get-tuple-element.75), channel_id=1, source_target_pairs={{0,1},{1,0},{2,3},{3,2},{4,5},{5,4},{6,7},{7,6},{8,9},{9,8},{10,11... | collective-permute-start | bytes 1572872 | tf_op jit(solution)/shard_map/ppermute | solution.py:535
  49.8 18.3 %collective-permute-start.13 = (bf16[256,1024]{1,0:T(8,128)(2,1)S(1)}, bf16[256,1024]{1,0:T(8,128)(2,1)S(1)}, u32[]{:S(2)}, u32[]{:S(2)}) collective-permute-start(bf16[256,1024]{1,0:T(8,128)(2,1)S(1)} %get-tuple-element.70.refs_3_), channel_id=1, source_target_pairs={{1,2},{2,1},{5,6},{6,5},{9,10},{10,9},{13,14},{14,13},{17,18},{18,... | collective-permute-start | bytes 1572872 | tf_op jit(solution)/shard_map/ppermute | solution.py:535
  57.1 22.2 %collective-permute-start.10 = (bf16[256,1024]{1,0:T(8,128)(2,1)S(1)}, bf16[256,1024]{1,0:T(8,128)(2,1)S(1)}, u32[]{:S(2)}, u32[]{:S(2)}) collective-permute-start(bf16[256,1024]{1,0:T(8,128)(2,1)S(1)} %get-tuple-element.73), channel_id=1, source_target_pairs={{0,1},{1,0},{2,3},{3,2},{4,5},{5,4},{6,7},{7,6},{8,9},{9,8},{10,11... | collective-permute-start | bytes 1572872 | tf_op jit(solution)/shard_map/ppermute | solution.py:540
  61.0 20.6 %collective-permute-start.11 = (bf16[256,1024]{1,0:T(8,128)(2,1)S(1)}, bf16[256,1024]{1,0:T(8,128)(2,1)S(1)}, u32[]{:S(2)}, u32[]{:S(2)}) collective-permute-start(bf16[256,1024]{1,0:T(8,128)(2,1)S(1)} %get-tuple-element.74.refs_5_), channel_id=1, source_target_pairs={{1,2},{2,1},{5,6},{6,5},{9,10},{10,9},{13,14},{14,13},{17,18},{18,... | collective-permute-start | bytes 1572872 | tf_op jit(solution)/shard_map/ppermute | solution.py:540
  68.2 29.0 %collective-permute-start.20 = (bf16[256,1024]{1,0:T(8,128)(2,1)S(1)}, bf16[256,1024]{1,0:T(8,128)(2,1)S(1)}, u32[]{:S(2)}, u32[]{:S(2)}) collective-permute-start(bf16[256,1024]{1,0:T(8,128)(2,1)S(1)} %get-tuple-element.78.refs_9_), channel_id=1, source_target_pairs={{0,1},{1,0},{2,3},{3,2},{4,5},{5,4},{6,7},{7,6},{8,9},{9,8},{10,11... | collective-permute-start | bytes 1572872 | tf_op jit(solution)/shard_map/ppermute | solution.py:546
  74.4 22.8 %collective-permute-start.21 = (bf16[256,1024]{1,0:T(8,128)(2,1)S(1)}, bf16[256,1024]{1,0:T(8,128)(2,1)S(1)}, u32[]{:S(2)}, u32[]{:S(2)}) collective-permute-start(bf16[256,1024]{1,0:T(8,128)(2,1)S(1)} %get-tuple-element.99), channel_id=1, source_target_pairs={{1,2},{2,1},{5,6},{6,5},{9,10},{10,9},{13,14},{14,13},{17,18},{18,... | collective-permute-start | bytes 1572872 | tf_op jit(solution)/shard_map/ppermute | solution.py:553
  81.6 2.7 %collective-permute-start.16 = (bf16[4,128,128]{2,1,0:T(8,128)(2,1)S(1)}, bf16[4,128,128]{2,1,0:T(8,128)(2,1)S(1)}, u32[]{:S(2)}, u32[]{:S(2)}) collective-permute-start(bf16[4,128,128]{2,1,0:T(8,128)(2,1)S(1)} %get-tuple-element.83.refs_4_), channel_id=1, source_target_pairs={{0,4},{4,0},{8,12},{12,8},{16,20},{20,16},{24,28},{28,24},{1,5},{5... | collective-permute-start | bytes 393224 | tf_op jit(solution)/shard_map/ppermute | solution.py:172
  81.8 18.8 %collective-permute-start.14 = (bf16[256,1024]{1,0:T(8,128)(2,1)S(1)}, bf16[256,1024]{1,0:T(8,128)(2,1)S(1)}, u32[]{:S(2)}, u32[]{:S(2)}) collective-permute-start(bf16[256,1024]{1,0:T(8,128)(2,1)S(1)} %get-tuple-element.84), channel_id=1, source_target_pairs={{0,1},{1,0},{2,3},{3,2},{4,5},{5,4},{6,7},{7,6},{8,9},{9,8},{10,11... | collective-permute-start | bytes 1572872 | tf_op jit(solution)/shard_map/ppermute | solution.py:565
  83.6 17.0 %collective-permute-start.15 = (bf16[256,1024]{1,0:T(8,128)(2,1)S(1)}, bf16[256,1024]{1,0:T(8,128)(2,1)S(1)}, u32[]{:S(2)}, u32[]{:S(2)}) collective-permute-start(bf16[256,1024]{1,0:T(8,128)(2,1)S(1)} %get-tuple-element.85), channel_id=1, source_target_pairs={{1,2},{2,1},{5,6},{6,5},{9,10},{10,9},{13,14},{14,13},{17,18},{18,... | collective-permute-start | bytes 1572872 | tf_op jit(solution)/shard_map/ppermute | solution.py:565
  84.4 5.7 %collective-permute-start.17 = (bf16[4,128,128]{2,1,0:T(8,128)(2,1)S(1)}, bf16[4,128,128]{2,1,0:T(8,128)(2,1)S(1)}, u32[]{:S(2)}, u32[]{:S(2)}) collective-permute-start(bf16[4,128,128]{2,1,0:T(8,128)(2,1)S(1)} %pair_total.3.refs_7_.refs_2_), channel_id=1, source_target_pairs={{0,8},{4,12},{8,0},{12,4},{16,24},{20,28},{24,16},{28,20},{1,9},{5... | collective-permute-start | bytes 393224 | tf_op jit(solution)/shard_map/ppermute | solution.py:189
  90.1 6.9 %collective-permute-start.18 = (bf16[4,128,128]{2,1,0:T(8,128)(2,1)S(1)}, bf16[4,128,128]{2,1,0:T(8,128)(2,1)S(1)}, u32[]{:S(2)}, u32[]{:S(2)}) collective-permute-start(bf16[4,128,128]{2,1,0:T(8,128)(2,1)S(1)} %get-tuple-element.92.refs_9_), channel_id=1, source_target_pairs={{16,0},{20,4},{24,8},{28,12},{17,1},{21,5},{25,9},{29,13},{18,2},{... | collective-permute-start | bytes 393224 | tf_op jit(solution)/shard_map/ppermute | solution.py:189
  97.1 1.4 %collective-permute-start.19 = (bf16[4,128,128]{2,1,0:T(8,128)(2,1)S(1)}, bf16[4,128,128]{2,1,0:T(8,128)(2,1)S(1)}, u32[]{:S(2)}, u32[]{:S(2)}) collective-permute-start(bf16[4,128,128]{2,1,0:T(8,128)(2,1)S(1)} %get-tuple-element.96), channel_id=1, source_target_pairs={{0,4},{4,0},{8,12},{12,8},{16,20},{20,16},{24,28},{28,24},{1,5},{5... | collective-permute-start | bytes 393224 | tf_op jit(solution)/shard_map/ppermute | solution.py:203
  (3 other events, 7.2 us)

commit v7 on v6

--- a/solution.py
+++ b/solution.py
@@ -182,11 +182,7 @@
     for m, r, last in stages(n, forward):
         others = []
         for x in range(1, r):
-            pairs = [
-                (i, i ^ (x * m)) for i in range(n)
-                if not last or ((i // m % r) < (i // m % r ^ x)) == forward
-            ]
-            others.append(lax.ppermute(total, "ctx", pairs))
+            others.append(lax.ppermute(total, "ctx", [(i, i ^ (x * m)) for i in range(n)]))
         deps = beside.pop(0)(total) if beside else ()
         body = functools.partial(stage_body, row, r, last, bool(entering))
         if last:

time: 102 us -> 102 us (level)
  starting transfers between devices: 36.7 us -> 35.2 us
    ppermute x4, starting transfers between devices: 8.05 us -> 6.28 us  [exchange(): lax.ppermute(total, 'ctx', [(i, i ^ x * m) for i in range(n)])]
  transfers between devices with their start and end apart: 22 -> 22, of which waited for: 12 -> 13; matrix products, arithmetic and copies ran while one was open for 1% -> 1% of each run, Pallas kernels for 35% -> 35%
where the time goes in v7:
time: 102 us; the launch traced here: 101 us
  Pallas kernels  36.8 us (36%)
  starting transfers between devices  35.2 us (35%)
  waiting for transfers between devices  26.3 us (26%)
    pallas_call x30, Pallas kernels, kernel(): pl.pallas_call(inner, name=name, in_specs=[spec(pltpu.SMEM)] * len(smem)...  34.8 us
    ppermute x1, waiting for transfers between devices, shards(): lax.ppermute(n2a, 'head', neighbours)  7.9 us
    ppermute x4, starting transfers between devices, exchange(): lax.ppermute(total, 'ctx', [(i, i ^ x * m) for i in range(n)])  6.28 us
    ppermute x1, starting transfers between devices, shards(): g1 = lax.ppermute(grad, 'head', neighbours)  5.85 us
    ppermute x4, waiting for transfers between devices, exchange(): lax.ppermute(total, 'ctx', [(i, i ^ x * m) for i in range(n)])  5.46 us
    ppermute x1, starting transfers between devices, shards(): lax.ppermute(n3a, 'head', neighbours)  3.97 us
    ppermute x1, starting transfers between devices, shards(): lax.ppermute(n3b, 'head', neighbours)  3.97 us
    ppermute x1, starting transfers between devices, shards(): n4a = lax.ppermute(s1a, 'head', neighbours)  3.97 us
  transfers between devices with their start and end apart: 22, of which 13 were waited for; matrix products, arithmetic and copies ran while one was open for 1% of the time, Pallas kernels for 35%

profile of v7, /device:TPU:0, one launch (start us, length us, event | category | flops | bytes accessed | tf_op | source)
XLA Modules:
  0.0 100.7 jit_solution(1908809294772616967)
XLA Ops:
  1.4 5.8 %collective-permute-start.4 = (bf16[512,1024]{1,0:T(8,128)(2,1)}, bf16[512,1024]{1,0:T(8,128)(2,1)S(1)}, u32[]{:S(2)}, u32[]{:S(2)}) collective-permute-start(bf16[512,1024]{1,0:T(8,128)(2,1)} %refs_2_.12), channel_id=1, source_target_pairs={{0,1},{1,0},{2,3},{3,2},{4,5},{5,4},{6,7},{7,6},{8,9},{9,8},{10,11... | collective-permute-start | bytes 3145736 | tf_op jit(solution)/shard_map/ppermute | solution.py:497
  13.1 2.5 %intra.1.refs_3_.refs_5_ = f32[512,1024]{1,0:T(8,128)S(1)} custom-call(s32[512,128]{1,0:T(8,128)S(1)} %get-tuple-element.60.refs_0_, bf16[512,1024]{1,0:T(8,128)(2,1)S(1)} %copy-done.1, bf16[512,1024]{1,0:T(8,128)(2,1)S(1)} %copy-done.2, bf16[512,1024]{1,0:T(8,128)(2,1)S(1)} %copy-done.3, bf16[4,128,128]{2,1,0:T(8,128)(2,1)S(1)} %pair_total.2.refs_4_.refs_2_), custom_call_target="tpu_custom_call" | custom-call | flops 300000000 | tf_op jit(solution)/shard_map/intra/pallas_call | solution.py:35
  18.8 1.8 %back_own.1.refs_5_.refs_3_ = f32[512,1024]{1,0:T(8,128)S(1)} custom-call(s32[7]{0:T(128)S(1)} %pad_add_fusion.refs_0_, bf16[1024,4096]{1,0:T(8,128)(2,1)S(1)} %copy-done, bf16[512,1024]{1,0:T(8,128)(2,1)S(1)} %copy-done.4, f32[512,1024]{1,0:T(8,128)S(1)} %intra.1.refs_3_.refs_5_), custom_call_target="tpu_custom_call" | custom-call | flops 180000000 | tf_op jit(solution)/shard_map/back_own/pallas_call | solution.py:35
  24.8 1.8 %project_3.1.refs_2_.refs_3_ = bf16[512,1024]{1,0:T(8,128)(2,1)S(1)} custom-call(s32[7]{0:T(128)S(1)} %pad_add_fusion.refs_0_, bf16[512,1024]{1,0:T(8,128)(2,1)S(1)} %get-tuple-element.65.refs_1_, bf16[1024,4096]{1,0:T(8,128)(2,1)S(1)} %copy-done), custom_call_target="tpu_custom_call" | custom-call | flops 180000000 | tf_op jit(solution)/shard_map/project_3/pallas_call | solution.py:35
  26.7 3.6 %collective-permute-done.4.refs_1_.refs_2_ = bf16[512,1024]{1,0:T(8,128)(2,1)S(1)} collective-permute-done((bf16[512,1024]{1,0:T(8,128)(2,1)}, bf16[512,1024]{1,0:T(8,128)(2,1)S(1)}, u32[]{:S(2)}, u32[]{:S(2)}) %collective-permute-start.4) | collective-permute-done | bytes 1048608 | tf_op jit(solution)/shard_map/ppermute | solution.py:497
  30.7 1.8 %collective-permute-start.6 = (bf16[256,1024]{1,0:T(8,128)(2,1)S(1)}, bf16[256,1024]{1,0:T(8,128)(2,1)S(1)}, u32[]{:S(2)}, u32[]{:S(2)}) collective-permute-start(bf16[256,1024]{1,0:T(8,128)(2,1)S(1)} %get-tuple-element.68), channel_id=1, source_target_pairs={{0,1},{1,0},{2,3},{3,2},{4,5},{5,4},{6,7},{7,6},{8,9},{9,8},{10,11... | collective-permute-start | bytes 1572872 | tf_op jit(solution)/shard_map/ppermute | solution.py:526
  33.2 2.0 %collective-permute-start.8 = (bf16[256,1024]{1,0:T(8,128)(2,1)S(1)}, bf16[256,1024]{1,0:T(8,128)(2,1)S(1)}, u32[]{:S(2)}, u32[]{:S(2)}) collective-permute-start(bf16[256,1024]{1,0:T(8,128)(2,1)S(1)} %get-tuple-element.71), channel_id=1, source_target_pairs={{0,1},{1,0},{2,3},{3,2},{4,5},{5,4},{6,7},{7,6},{8,9},{9,8},{10,11... | collective-permute-start | bytes 1572872 | tf_op jit(solution)/shard_map/ppermute | solution.py:527
  35.9 1.8 %project_2.1.refs_2_ = bf16[512,1024]{1,0:T(8,128)(2,1)S(1)} custom-call(s32[7]{0:T(128)S(1)} %pad_add_fusion.refs_0_, bf16[512,1024]{1,0:T(8,128)(2,1)S(1)} %get-tuple-element.65.refs_1_, bf16[1024,4096]{1,0:T(8,128)(2,1)S(1)} %copy-done, bf16[512,1024]{1,0:T(8,128)(2,1)S(1)} %project_3.1.refs_2_.refs_3_), custom_call_target="tpu_custom_call" | custom-call | flops 180000000 | tf_op jit(solution)/shard_map/project_2/pallas_call | solution.py:35
  37.7 7.9 %collective-permute-done.6.refs_1_ = bf16[256,1024]{1,0:T(8,128)(2,1)S(1)} collective-permute-done((bf16[256,1024]{1,0:T(8,128)(2,1)S(1)}, bf16[256,1024]{1,0:T(8,128)(2,1)S(1)}, u32[]{:S(2)}, u32[]{:S(2)}) %collective-permute-start.6) | collective-permute-done | bytes 524320 | tf_op jit(solution)/shard_map/ppermute | solution.py:526
  45.8 4.0 %collective-permute-start.12 = (bf16[256,1024]{1,0:T(8,128)(2,1)S(1)}, bf16[256,1024]{1,0:T(8,128)(2,1)S(1)}, u32[]{:S(2)}, u32[]{:S(2)}) collective-permute-start(bf16[256,1024]{1,0:T(8,128)(2,1)S(1)} %get-tuple-element.75), channel_id=1, source_target_pairs={{0,1},{1,0},{2,3},{3,2},{4,5},{5,4},{6,7},{7,6},{8,9},{9,8},{10,11... | collective-permute-start | bytes 1572872 | tf_op jit(solution)/shard_map/ppermute | solution.py:531
  50.5 1.8 %project_1.1.refs_3_ = bf16[512,1024]{1,0:T(8,128)(2,1)S(1)} custom-call(s32[7]{0:T(128)S(1)} %pad_add_fusion.refs_0_, bf16[512,1024]{1,0:T(8,128)(2,1)S(1)} %get-tuple-element.65.refs_1_, bf16[1024,4096]{1,0:T(8,128)(2,1)S(1)} %copy-done, bf16[256,1024]{1,0:T(8,128)(2,1)S(1)} %get-tuple-element.70.refs_3_), custom_call_target="tpu_custom_call" | custom-call | flops 180000000 | tf_op jit(solution)/shard_map/project_1/pallas_call | solution.py:35
  52.3 1.8 %project_0.1.refs_4_.p_ref = bf16[512,1024]{1,0:T(8,128)(2,1)S(1)} custom-call(s32[7]{0:T(128)S(1)} %pad_add_fusion.refs_0_, bf16[512,1024]{1,0:T(8,128)(2,1)S(1)} %get-tuple-element.65.refs_1_, bf16[1024,4096]{1,0:T(8,128)(2,1)S(1)} %copy-done, bf16[512,1024]{1,0:T(8,128)(2,1)S(1)} %project_1.1.refs_3_), custom_call_target="tpu_custom_call" | custom-call | flops 180000000 | tf_op jit(solution)/shard_map/project_0/pallas_call | solution.py:35
  54.1 1.8 %back_1.1.refs_4_.refs_3_ = f32[512,1024]{1,0:T(8,128)S(1)} custom-call(s32[7]{0:T(128)S(1)} %pad_add_fusion.refs_0_, bf16[1024,4096]{1,0:T(8,128)(2,1)S(1)} %copy-done, bf16[512,1024]{1,0:T(8,128)(2,1)S(1)} %collective-permute-done.4.refs_1_.refs_2_, f32[512,1024]{1,0:T(8,128)S(1)} %back_own.1.refs_5_.refs_3_, bf16[512,1024]{1,0:T(8,128)(2,1)S(1)} %project_0.1.refs_4_.p_ref), custom_call_target="tpu_custom_call" | custom-call | flops 180000000 | tf_op jit(solution)/shard_map/back_1/pallas_call | solution.py:35
  57.1 4.0 %collective-permute-start.10 = (bf16[256,1024]{1,0:T(8,128)(2,1)S(1)}, bf16[256,1024]{1,0:T(8,128)(2,1)S(1)}, u32[]{:S(2)}, u32[]{:S(2)}) collective-permute-start(bf16[256,1024]{1,0:T(8,128)(2,1)S(1)} %get-tuple-element.73), channel_id=1, source_target_pairs={{0,1},{1,0},{2,3},{3,2},{4,5},{5,4},{6,7},{7,6},{8,9},{9,8},{10,11... | collective-permute-start | bytes 1572872 | tf_op jit(solution)/shard_map/ppermute | solution.py:536
  62.2 1.8 %back_2.1.refs_2_.refs_5_.refs_6_ = f32[512,1024]{1,0:T(8,128)S(1)} custom-call(s32[7]{0:T(128)S(1)} %pad_add_fusion.refs_0_, bf16[1024,4096]{1,0:T(8,128)(2,1)S(1)} %copy-done, bf16[512,1024]{1,0:T(8,128)(2,1)S(1)} %pick.3.refs_2_, f32[512,1024]{1,0:T(8,128)S(1)} %back_1.1.refs_4_.refs_3_), custom_call_target="tpu_custom_call" | custom-call | flops 180000000 | tf_op jit(solution)/shard_map/back_2/pallas_call | solution.py:35
  64.8 3.3 %collective-permute-done.12.refs_0_.refs_3_ = bf16[256,1024]{1,0:T(8,128)(2,1)S(1)} collective-permute-done((bf16[256,1024]{1,0:T(8,128)(2,1)S(1)}, bf16[256,1024]{1,0:T(8,128)(2,1)S(1)}, u32[]{:S(2)}, u32[]{:S(2)}) %collective-permute-start.12) | collective-permute-done | bytes 524320 | tf_op jit(solution)/shard_map/ppermute | solution.py:531
  68.2 4.0 %collective-permute-start.20 = (bf16[256,1024]{1,0:T(8,128)(2,1)S(1)}, bf16[256,1024]{1,0:T(8,128)(2,1)S(1)}, u32[]{:S(2)}, u32[]{:S(2)}) collective-permute-start(bf16[256,1024]{1,0:T(8,128)(2,1)S(1)} %get-tuple-element.78.refs_9_), channel_id=1, source_target_pairs={{0,1},{1,0},{2,3},{3,2},{4,5},{5,4},{6,7},{7,6},{8,9},{9,8},{10,11... | collective-permute-start | bytes 1572872 | tf_op jit(solution)/shard_map/ppermute | solution.py:542
  72.2 2.2 %attended_grads.2 = (bf16[256,1024]{1,0:T(8,128)(2,1)S(1)}, f32[8,128,128]{2,1,0:T(8,128)S(1)}) custom-call(f32[32,128]{1,0:T(8,128)S(1)} %get-tuple-element.55.refs_0_.refs_2_.refs_1_, f32[512,128]{1,0:T(8,128)S(1)} %get-tuple-element.56.refs_1_.refs_3_.refs_2_, bf16[1024,1024]{1,0:T(8,128)(2,1)S(1)} %block.1.refs_4_.refs_2_.refs_3_, ...), custom_call_target="tpu_custom_call" | custom-call | flops 200000000 | tf_op jit(solution)/shard_map/attended_grads/pallas_call | solution.py:35
  75.1 2.9 %first_grads.1 = (bf16[256,1024]{1,0:T(8,128)(2,1)S(1)}, f32[256,1024]{1,0:T(8,128)S(1)}, f32[256,1024]{1,0:T(8,128)S(1)}) custom-call(s32[512,128]{1,0:T(8,128)S(1)} %get-tuple-element.60.refs_0_, s32[8,512]{1,0:T(8,128)S(1)} %get-tuple-element.80.refs_1_.refs_0_, f32[32,128]{1,0:T(8,128)S(1)} %get-tuple-element.55.refs_0_.refs_2_.refs_1_, ...), custom_call_target="tpu_custom_call" | custom-call | flops 200000000 | tf_op jit(solution)/shard_map/first_grads/pallas_call | solution.py:35
  79.3 2.3 %attended_grads.3 = (bf16[256,1024]{1,0:T(8,128)(2,1)S(1)}, bf16[4,128,128]{2,1,0:T(8,128)(2,1)S(1)}, bf16[4,128,128]{2,1,0:T(8,128)(2,1)S(1)}) custom-call(f32[8,128,128]{2,1,0:T(8,128)S(1)} %get-tuple-element.79.refs_0_, f32[32,128]{1,0:T(8,128)S(1)} %get-tuple-element.55.refs_0_.refs_2_.refs_1_, f32[512,128]{1,0:T(8,128)S(1)} %get-tuple-element.56.refs_1_.refs_3_.refs_2_, ...), custom_call_target="tpu_custom_call" | custom-call | flops 200000000 | tf_op jit(solution)/shard_map/attended_grads/pallas_call | solution.py:35
  81.8 1.8 %collective-permute-start.14 = (bf16[256,1024]{1,0:T(8,128)(2,1)S(1)}, bf16[256,1024]{1,0:T(8,128)(2,1)S(1)}, u32[]{:S(2)}, u32[]{:S(2)}) collective-permute-start(bf16[256,1024]{1,0:T(8,128)(2,1)S(1)} %get-tuple-element.84), channel_id=1, source_target_pairs={{0,1},{1,0},{2,3},{3,2},{4,5},{5,4},{6,7},{7,6},{8,9},{9,8},{10,11... | collective-permute-start | bytes 1572872 | tf_op jit(solution)/shard_map/ppermute | solution.py:561
  86.1 2.4 %key_value_grads.1 = (f32[512,1024]{1,0:T(8,128)S(1)}, f32[512,1024]{1,0:T(8,128)S(1)}) custom-call(s32[8,512]{1,0:T(8,128)S(1)} %get-tuple-element.80.refs_1_.refs_0_, bf16[512,1024]{1,0:T(8,128)(2,1)S(1)} %copy-done.1, bf16[512,1024]{1,0:T(8,128)(2,1)S(1)} %copy-done.2, bf16[512,1024]{1,0:T(8,128)(2,1)S(1)} %copy-done.3, ...), custom_call_target="tpu_custom_call" | custom-call | flops 1000000 | tf_op jit(solution)/shard_map/key_value_grads/pallas_call | solution.py:35
  91.9 2.9 %query_grad.1 = (bf16[512,1024]{1,0:T(8,128)(2,1)}, f32[8,128]{1,0:T(8,128)S(1)}) custom-call(s32[512,128]{1,0:T(8,128)S(1)} %get-tuple-element.60.refs_0_, f32[32,128]{1,0:T(8,128)S(1)} %get-tuple-element.55.refs_0_.refs_2_.refs_1_, f32[512,128]{1,0:T(8,128)S(1)} %get-tuple-element.56.refs_1_.refs_3_.refs_2_, bf16[512,1024]{1,0:T(8,128)(2,1)S(1)} %copy-done.2, ...), custom_call_target="tpu_custom_call" | custom-call | flops 1000000 | tf_op jit(solution)/shard_map/query_grad/pallas_call | solution.py:35
  96.9 2.1 %last_grads.1 = (bf16[512,1024]{1,0:T(8,128)(2,1)}, bf16[512,1024]{1,0:T(8,128)(2,1)}, f32[8,128]{1,0:T(8,128)S(1)}) custom-call(f32[32,128]{1,0:T(8,128)S(1)} %get-tuple-element.55.refs_0_.refs_2_.refs_1_, f32[512,128]{1,0:T(8,128)S(1)} %get-tuple-element.57.refs_1_, bf16[512,1024]{1,0:T(8,128)(2,1)S(1)} %copy-done.2, bf16[512,1024]{1,0:T(8,128)(2,1)S(1)} %copy-done.3, ...), custom_call_target="tpu_custom_call" | custom-call | flops 1000000 | tf_op jit(solution)/shard_map/last_grads/pallas_call | solution.py:35
  (63 shorter events, 31.6 us)
Async XLA Ops:
  0.6 26.0 %collective-permute-start.5 = (bf16[512,1024]{1,0:T(8,128)(2,1)}, bf16[512,1024]{1,0:T(8,128)(2,1)S(1)}, u32[]{:S(2)}, u32[]{:S(2)}) collective-permute-start(bf16[512,1024]{1,0:T(8,128)(2,1)} %refs_2_.12), channel_id=1, source_target_pairs={{1,2},{2,1},{5,6},{6,5},{9,10},{10,9},{13,14},{14,13},{17,18},{18,... | collective-permute-start | bytes 3145736 | tf_op jit(solution)/shard_map/ppermute | solution.py:498
  1.4 28.9 %collective-permute-start.4 = (bf16[512,1024]{1,0:T(8,128)(2,1)}, bf16[512,1024]{1,0:T(8,128)(2,1)S(1)}, u32[]{:S(2)}, u32[]{:S(2)}) collective-permute-start(bf16[512,1024]{1,0:T(8,128)(2,1)} %refs_2_.12), channel_id=1, source_target_pairs={{0,1},{1,0},{2,3},{3,2},{4,5},{5,4},{6,7},{7,6},{8,9},{9,8},{10,11... | collective-permute-start | bytes 3145736 | tf_op jit(solution)/shard_map/ppermute | solution.py:497
  9.5 9.4 %copy-start.4 = (bf16[512,1024]{1,0:T(8,128)(2,1)S(1)}, bf16[512,1024]{1,0:T(8,128)(2,1)}, u32[]{:S(2)}) copy-start(bf16[512,1024]{1,0:T(8,128)(2,1)} %refs_2_.12) | copy-start | bytes 3145732
  10.1 1.4 %collective-permute-start = (bf16[4,128,128]{2,1,0:T(8,128)(2,1)S(1)}, bf16[4,128,128]{2,1,0:T(8,128)(2,1)S(1)}, u32[]{:S(2)}, u32[]{:S(2)}) collective-permute-start(bf16[4,128,128]{2,1,0:T(8,128)(2,1)S(1)} %get-tuple-element.59), channel_id=1, source_target_pairs={{0,4},{4,0},{8,12},{12,8},{16,20},{20,16},{24,28},{28,24},{1,5},{5... | collective-permute-start | bytes 393224 | tf_op jit(solution)/shard_map/ppermute | solution.py:172
  11.5 7.3 %copy-start = (bf16[1024,4096]{1,0:T(8,128)(2,1)S(1)}, bf16[1024,4096]{1,0:T(8,128)(2,1)}, u32[]{:S(2)}) copy-start(bf16[1024,4096]{1,0:T(8,128)(2,1)} %refs_1_.10) | copy-start | bytes 25165828
  11.6 5.6 %collective-permute-start.1 = (bf16[4,128,128]{2,1,0:T(8,128)(2,1)S(1)}, bf16[4,128,128]{2,1,0:T(8,128)(2,1)S(1)}, u32[]{:S(2)}, u32[]{:S(2)}) collective-permute-start(bf16[4,128,128]{2,1,0:T(8,128)(2,1)S(1)} %pair_total.2.refs_4_.refs_2_), channel_id=1, source_target_pairs={{0,8},{4,12},{8,0},{12,4},{16,24},{20,28},{24,16},{28,20},{1,9},{5... | collective-permute-start | bytes 393224 | tf_op jit(solution)/shard_map/ppermute | solution.py:185
  17.3 5.0 %collective-permute-start.2 = (bf16[4,128,128]{2,1,0:T(8,128)(2,1)S(1)}, bf16[4,128,128]{2,1,0:T(8,128)(2,1)S(1)}, u32[]{:S(2)}, u32[]{:S(2)}) collective-permute-start(bf16[4,128,128]{2,1,0:T(8,128)(2,1)S(1)} %get-tuple-element.61), channel_id=1, source_target_pairs={{0,16},{4,20},{8,24},{12,28},{16,0},{20,4},{24,8},{28,12},{1,17},{... | collective-permute-start | bytes 393224 | tf_op jit(solution)/shard_map/ppermute | solution.py:185
  22.4 1.4 %collective-permute-start.3 = (bf16[4,128,128]{2,1,0:T(8,128)(2,1)S(1)}, bf16[4,128,128]{2,1,0:T(8,128)(2,1)S(1)}, u32[]{:S(2)}, u32[]{:S(2)}) collective-permute-start(bf16[4,128,128]{2,1,0:T(8,128)(2,1)S(1)} %get-tuple-element.64), channel_id=1, source_target_pairs={{0,4},{4,0},{8,12},{12,8},{16,20},{20,16},{24,28},{28,24},{1,5},{5... | collective-permute-start | bytes 393224 | tf_op jit(solution)/shard_map/ppermute | solution.py:199
  30.7 14.9 %collective-permute-start.6 = (bf16[256,1024]{1,0:T(8,128)(2,1)S(1)}, bf16[256,1024]{1,0:T(8,128)(2,1)S(1)}, u32[]{:S(2)}, u32[]{:S(2)}) collective-permute-start(bf16[256,1024]{1,0:T(8,128)(2,1)S(1)} %get-tuple-element.68), channel_id=1, source_target_pairs={{0,1},{1,0},{2,3},{3,2},{4,5},{5,4},{6,7},{7,6},{8,9},{9,8},{10,11... | collective-permute-start | bytes 1572872 | tf_op jit(solution)/shard_map/ppermute | solution.py:526
  32.5 13.1 %collective-permute-start.7 = (bf16[256,1024]{1,0:T(8,128)(2,1)S(1)}, bf16[256,1024]{1,0:T(8,128)(2,1)S(1)}, u32[]{:S(2)}, u32[]{:S(2)}) collective-permute-start(bf16[256,1024]{1,0:T(8,128)(2,1)S(1)} %get-tuple-element.69), channel_id=1, source_target_pairs={{1,2},{2,1},{5,6},{6,5},{9,10},{10,9},{13,14},{14,13},{17,18},{18,... | collective-permute-start | bytes 1572872 | tf_op jit(solution)/shard_map/ppermute | solution.py:526
  33.2 23.7 %collective-permute-start.8 = (bf16[256,1024]{1,0:T(8,128)(2,1)S(1)}, bf16[256,1024]{1,0:T(8,128)(2,1)S(1)}, u32[]{:S(2)}, u32[]{:S(2)}) collective-permute-start(bf16[256,1024]{1,0:T(8,128)(2,1)S(1)} %get-tuple-element.71), channel_id=1, source_target_pairs={{0,1},{1,0},{2,3},{3,2},{4,5},{5,4},{6,7},{7,6},{8,9},{9,8},{10,11... | collective-permute-start | bytes 1572872 | tf_op jit(solution)/shard_map/ppermute | solution.py:527
  35.2 21.7 %collective-permute-start.9 = (bf16[256,1024]{1,0:T(8,128)(2,1)S(1)}, bf16[256,1024]{1,0:T(8,128)(2,1)S(1)}, u32[]{:S(2)}, u32[]{:S(2)}) collective-permute-start(bf16[256,1024]{1,0:T(8,128)(2,1)S(1)} %get-tuple-element.72), channel_id=1, source_target_pairs={{1,2},{2,1},{5,6},{6,5},{9,10},{10,9},{13,14},{14,13},{17,18},{18,... | collective-permute-start | bytes 1572872 | tf_op jit(solution)/shard_map/ppermute | solution.py:527
  45.8 22.2 %collective-permute-start.12 = (bf16[256,1024]{1,0:T(8,128)(2,1)S(1)}, bf16[256,1024]{1,0:T(8,128)(2,1)S(1)}, u32[]{:S(2)}, u32[]{:S(2)}) collective-permute-start(bf16[256,1024]{1,0:T(8,128)(2,1)S(1)} %get-tuple-element.75), channel_id=1, source_target_pairs={{0,1},{1,0},{2,3},{3,2},{4,5},{5,4},{6,7},{7,6},{8,9},{9,8},{10,11... | collective-permute-start | bytes 1572872 | tf_op jit(solution)/shard_map/ppermute | solution.py:531
  49.8 18.3 %collective-permute-start.13 = (bf16[256,1024]{1,0:T(8,128)(2,1)S(1)}, bf16[256,1024]{1,0:T(8,128)(2,1)S(1)}, u32[]{:S(2)}, u32[]{:S(2)}) collective-permute-start(bf16[256,1024]{1,0:T(8,128)(2,1)S(1)} %get-tuple-element.70.refs_3_), channel_id=1, source_target_pairs={{1,2},{2,1},{5,6},{6,5},{9,10},{10,9},{13,14},{14,13},{17,18},{18,... | collective-permute-start | bytes 1572872 | tf_op jit(solution)/shard_map/ppermute | solution.py:531
  57.1 22.2 %collective-permute-start.10 = (bf16[256,1024]{1,0:T(8,128)(2,1)S(1)}, bf16[256,1024]{1,0:T(8,128)(2,1)S(1)}, u32[]{:S(2)}, u32[]{:S(2)}) collective-permute-start(bf16[256,1024]{1,0:T(8,128)(2,1)S(1)} %get-tuple-element.73), channel_id=1, source_target_pairs={{0,1},{1,0},{2,3},{3,2},{4,5},{5,4},{6,7},{7,6},{8,9},{9,8},{10,11... | collective-permute-start | bytes 1572872 | tf_op jit(solution)/shard_map/ppermute | solution.py:536
  61.0 20.6 %collective-permute-start.11 = (bf16[256,1024]{1,0:T(8,128)(2,1)S(1)}, bf16[256,1024]{1,0:T(8,128)(2,1)S(1)}, u32[]{:S(2)}, u32[]{:S(2)}) collective-permute-start(bf16[256,1024]{1,0:T(8,128)(2,1)S(1)} %get-tuple-element.74.refs_5_), channel_id=1, source_target_pairs={{1,2},{2,1},{5,6},{6,5},{9,10},{10,9},{13,14},{14,13},{17,18},{18,... | collective-permute-start | bytes 1572872 | tf_op jit(solution)/shard_map/ppermute | solution.py:536
  68.2 27.4 %collective-permute-start.20 = (bf16[256,1024]{1,0:T(8,128)(2,1)S(1)}, bf16[256,1024]{1,0:T(8,128)(2,1)S(1)}, u32[]{:S(2)}, u32[]{:S(2)}) collective-permute-start(bf16[256,1024]{1,0:T(8,128)(2,1)S(1)} %get-tuple-element.78.refs_9_), channel_id=1, source_target_pairs={{0,1},{1,0},{2,3},{3,2},{4,5},{5,4},{6,7},{7,6},{8,9},{9,8},{10,11... | collective-permute-start | bytes 1572872 | tf_op jit(solution)/shard_map/ppermute | solution.py:542
  74.4 21.2 %collective-permute-start.21 = (bf16[256,1024]{1,0:T(8,128)(2,1)S(1)}, bf16[256,1024]{1,0:T(8,128)(2,1)S(1)}, u32[]{:S(2)}, u32[]{:S(2)}) collective-permute-start(bf16[256,1024]{1,0:T(8,128)(2,1)S(1)} %get-tuple-element.99), channel_id=1, source_target_pairs={{1,2},{2,1},{5,6},{6,5},{9,10},{10,9},{13,14},{14,13},{17,18},{18,... | collective-permute-start | bytes 1572872 | tf_op jit(solution)/shard_map/ppermute | solution.py:549
  81.6 2.9 %collective-permute-start.16 = (bf16[4,128,128]{2,1,0:T(8,128)(2,1)S(1)}, bf16[4,128,128]{2,1,0:T(8,128)(2,1)S(1)}, u32[]{:S(2)}, u32[]{:S(2)}) collective-permute-start(bf16[4,128,128]{2,1,0:T(8,128)(2,1)S(1)} %get-tuple-element.83.refs_4_), channel_id=1, source_target_pairs={{0,4},{4,0},{8,12},{12,8},{16,20},{20,16},{24,28},{28,24},{1,5},{5... | collective-permute-start | bytes 393224 | tf_op jit(solution)/shard_map/ppermute | solution.py:172
  81.8 17.9 %collective-permute-start.14 = (bf16[256,1024]{1,0:T(8,128)(2,1)S(1)}, bf16[256,1024]{1,0:T(8,128)(2,1)S(1)}, u32[]{:S(2)}, u32[]{:S(2)}) collective-permute-start(bf16[256,1024]{1,0:T(8,128)(2,1)S(1)} %get-tuple-element.84), channel_id=1, source_target_pairs={{0,1},{1,0},{2,3},{3,2},{4,5},{5,4},{6,7},{7,6},{8,9},{9,8},{10,11... | collective-permute-start | bytes 1572872 | tf_op jit(solution)/shard_map/ppermute | solution.py:561
  83.6 16.1 %collective-permute-start.15 = (bf16[256,1024]{1,0:T(8,128)(2,1)S(1)}, bf16[256,1024]{1,0:T(8,128)(2,1)S(1)}, u32[]{:S(2)}, u32[]{:S(2)}) collective-permute-start(bf16[256,1024]{1,0:T(8,128)(2,1)S(1)} %get-tuple-element.85), channel_id=1, source_target_pairs={{1,2},{2,1},{5,6},{6,5},{9,10},{10,9},{13,14},{14,13},{17,18},{18,... | collective-permute-start | bytes 1572872 | tf_op jit(solution)/shard_map/ppermute | solution.py:561
  84.6 5.7 %collective-permute-start.17 = (bf16[4,128,128]{2,1,0:T(8,128)(2,1)S(1)}, bf16[4,128,128]{2,1,0:T(8,128)(2,1)S(1)}, u32[]{:S(2)}, u32[]{:S(2)}) collective-permute-start(bf16[4,128,128]{2,1,0:T(8,128)(2,1)S(1)} %pair_total.3.refs_7_.refs_2_), channel_id=1, source_target_pairs={{0,8},{4,12},{8,0},{12,4},{16,24},{20,28},{24,16},{28,20},{1,9},{5... | collective-permute-start | bytes 393224 | tf_op jit(solution)/shard_map/ppermute | solution.py:185
  90.3 5.0 %collective-permute-start.18 = (bf16[4,128,128]{2,1,0:T(8,128)(2,1)S(1)}, bf16[4,128,128]{2,1,0:T(8,128)(2,1)S(1)}, u32[]{:S(2)}, u32[]{:S(2)}) collective-permute-start(bf16[4,128,128]{2,1,0:T(8,128)(2,1)S(1)} %get-tuple-element.92.refs_9_), channel_id=1, source_target_pairs={{0,16},{4,20},{8,24},{12,28},{16,0},{20,4},{24,8},{28,12},{1,17},{... | collective-permute-start | bytes 393224 | tf_op jit(solution)/shard_map/ppermute | solution.py:185
  95.5 1.4 %collective-permute-start.19 = (bf16[4,128,128]{2,1,0:T(8,128)(2,1)S(1)}, bf16[4,128,128]{2,1,0:T(8,128)(2,1)S(1)}, u32[]{:S(2)}, u32[]{:S(2)}) collective-permute-start(bf16[4,128,128]{2,1,0:T(8,128)(2,1)S(1)} %get-tuple-element.96), channel_id=1, source_target_pairs={{0,4},{4,0},{8,12},{12,8},{16,20},{20,16},{24,28},{28,24},{1,5},{5... | collective-permute-start | bytes 393224 | tf_op jit(solution)/shard_map/ppermute | solution.py:199
  (3 other events, 7.2 us)

commit v8 on v7

--- a/solution.py
+++ b/solution.py
@@ -441,8 +441,8 @@
     s1_ref[...] = p1_ref[rows, :] + i3_ref[...]
 
 
-def mix_body(n_dep, p_ref, a_ref, b_ref, *refs):
-    total = p_ref[...].astype(F32) + a_ref[...].astype(F32) + b_ref[...].astype(F32)
+def mix_body(n_dep, rows, p_ref, a_ref, b_ref, *refs):
+    total = p_ref[rows, :].astype(F32) + a_ref[...].astype(F32) + b_ref[...].astype(F32)
     refs[n_dep][...] = total.astype(BF16)
     if len(refs) > n_dep + 1:
         refs[-1][...] = jnp.zeros_like(refs[-1])
@@ -452,14 +452,14 @@
     tok, width = p0.shape
     lot = tok // 2
     mine = pl.BlockSpec((lot, width), lambda i: (half, 0))
-    whole = pl.BlockSpec((lot, width), lambda i: (0, 0))
+    whole = pl.BlockSpec(memory_space=pltpu.VMEM)
     extra = list(deps) + ([] if into is None else [into])
     first = into is None
     out = pl.pallas_call(
-        functools.partial(mix_body, len(extra)),
+        functools.partial(mix_body, len(extra), slice(half * lot, (half + 1) * lot)),
         name="mixed",
         grid=(1,),
-        in_specs=[mine, whole, whole] + [pl.BlockSpec(memory_space=pl.ANY)] * len(extra),
+        in_specs=[whole] * 3 + [pl.BlockSpec(memory_space=pl.ANY)] * len(extra),
         out_specs=[mine] + [pl.BlockSpec((8, DH), lambda i: (0, 0))] * first,
         out_shape=[like((tok, width), BF16)] + [like((8, DH), F32)] * first,
         input_output_aliases={} if first else {2 + len(extra): 0},

time: 102 us -> 102 us (level)
  no operation moved by 1% of the time
where the time goes in v8:
time: 102 us; the launch traced here: 101 us
  Pallas kernels  36.8 us (36%)
  starting transfers between devices  35.2 us (35%)
  waiting for transfers between devices  26.3 us (26%)
    pallas_call x30, Pallas kernels, kernel(): pl.pallas_call(inner, name=name, in_specs=[spec(pltpu.SMEM)] * len(smem)...  34.8 us
    ppermute x1, waiting for transfers between devices, shards(): lax.ppermute(n2a, 'head', neighbours)  7.9 us
    ppermute x4, starting transfers between devices, exchange(): lax.ppermute(total, 'ctx', [(i, i ^ x * m) for i in range(n)])  6.28 us
    ppermute x1, starting transfers between devices, shards(): g1 = lax.ppermute(grad, 'head', neighbours)  5.85 us
    ppermute x4, waiting for transfers between devices, exchange(): lax.ppermute(total, 'ctx', [(i, i ^ x * m) for i in range(n)])  5.46 us
    ppermute x1, starting transfers between devices, shards(): lax.ppermute(n3a, 'head', neighbours)  3.97 us
    ppermute x1, starting transfers between devices, shards(): lax.ppermute(n3b, 'head', neighbours)  3.97 us
    ppermute x1, starting transfers between devices, shards(): n4a = lax.ppermute(s1a, 'head', neighbours)  3.97 us
  transfers between devices with their start and end apart: 22, of which 13 were waited for; matrix products, arithmetic and copies ran while one was open for 1% of the time, Pallas kernels for 35%

profile of v8, /device:TPU:0, one launch (start us, length us, event | category | flops | bytes accessed | tf_op | source)
XLA Modules:
  0.0 100.7 jit_solution(1908809294772616967)
XLA Ops:
  1.4 5.8 %collective-permute-start.4 = (bf16[512,1024]{1,0:T(8,128)(2,1)}, bf16[512,1024]{1,0:T(8,128)(2,1)S(1)}, u32[]{:S(2)}, u32[]{:S(2)}) collective-permute-start(bf16[512,1024]{1,0:T(8,128)(2,1)} %refs_2_.12), channel_id=1, source_target_pairs={{0,1},{1,0},{2,3},{3,2},{4,5},{5,4},{6,7},{7,6},{8,9},{9,8},{10,11... | collective-permute-start | bytes 3145736 | tf_op jit(solution)/shard_map/ppermute | solution.py:497
  13.1 2.5 %intra.1.refs_3_.refs_5_ = f32[512,1024]{1,0:T(8,128)S(1)} custom-call(s32[512,128]{1,0:T(8,128)S(1)} %get-tuple-element.60.refs_0_, bf16[512,1024]{1,0:T(8,128)(2,1)S(1)} %copy-done.1, bf16[512,1024]{1,0:T(8,128)(2,1)S(1)} %copy-done.2, bf16[512,1024]{1,0:T(8,128)(2,1)S(1)} %copy-done.3, bf16[4,128,128]{2,1,0:T(8,128)(2,1)S(1)} %pair_total.2.refs_4_.refs_2_), custom_call_target="tpu_custom_call" | custom-call | flops 300000000 | tf_op jit(solution)/shard_map/intra/pallas_call | solution.py:35
  18.8 1.8 %back_own.1.refs_5_.refs_3_ = f32[512,1024]{1,0:T(8,128)S(1)} custom-call(s32[7]{0:T(128)S(1)} %pad_add_fusion.refs_0_, bf16[1024,4096]{1,0:T(8,128)(2,1)S(1)} %copy-done, bf16[512,1024]{1,0:T(8,128)(2,1)S(1)} %copy-done.4, f32[512,1024]{1,0:T(8,128)S(1)} %intra.1.refs_3_.refs_5_), custom_call_target="tpu_custom_call" | custom-call | flops 180000000 | tf_op jit(solution)/shard_map/back_own/pallas_call | solution.py:35
  24.8 1.8 %project_3.1.refs_2_.refs_3_ = bf16[512,1024]{1,0:T(8,128)(2,1)S(1)} custom-call(s32[7]{0:T(128)S(1)} %pad_add_fusion.refs_0_, bf16[512,1024]{1,0:T(8,128)(2,1)S(1)} %get-tuple-element.65.refs_1_, bf16[1024,4096]{1,0:T(8,128)(2,1)S(1)} %copy-done), custom_call_target="tpu_custom_call" | custom-call | flops 180000000 | tf_op jit(solution)/shard_map/project_3/pallas_call | solution.py:35
  26.7 3.6 %collective-permute-done.4.refs_1_.refs_2_ = bf16[512,1024]{1,0:T(8,128)(2,1)S(1)} collective-permute-done((bf16[512,1024]{1,0:T(8,128)(2,1)}, bf16[512,1024]{1,0:T(8,128)(2,1)S(1)}, u32[]{:S(2)}, u32[]{:S(2)}) %collective-permute-start.4) | collective-permute-done | bytes 1048608 | tf_op jit(solution)/shard_map/ppermute | solution.py:497
  30.7 1.8 %collective-permute-start.6 = (bf16[256,1024]{1,0:T(8,128)(2,1)S(1)}, bf16[256,1024]{1,0:T(8,128)(2,1)S(1)}, u32[]{:S(2)}, u32[]{:S(2)}) collective-permute-start(bf16[256,1024]{1,0:T(8,128)(2,1)S(1)} %get-tuple-element.68), channel_id=1, source_target_pairs={{0,1},{1,0},{2,3},{3,2},{4,5},{5,4},{6,7},{7,6},{8,9},{9,8},{10,11... | collective-permute-start | bytes 1572872 | tf_op jit(solution)/shard_map/ppermute | solution.py:526
  33.2 2.0 %collective-permute-start.8 = (bf16[256,1024]{1,0:T(8,128)(2,1)S(1)}, bf16[256,1024]{1,0:T(8,128)(2,1)S(1)}, u32[]{:S(2)}, u32[]{:S(2)}) collective-permute-start(bf16[256,1024]{1,0:T(8,128)(2,1)S(1)} %get-tuple-element.71), channel_id=1, source_target_pairs={{0,1},{1,0},{2,3},{3,2},{4,5},{5,4},{6,7},{7,6},{8,9},{9,8},{10,11... | collective-permute-start | bytes 1572872 | tf_op jit(solution)/shard_map/ppermute | solution.py:527
  35.9 1.8 %project_2.1.refs_2_ = bf16[512,1024]{1,0:T(8,128)(2,1)S(1)} custom-call(s32[7]{0:T(128)S(1)} %pad_add_fusion.refs_0_, bf16[512,1024]{1,0:T(8,128)(2,1)S(1)} %get-tuple-element.65.refs_1_, bf16[1024,4096]{1,0:T(8,128)(2,1)S(1)} %copy-done, bf16[512,1024]{1,0:T(8,128)(2,1)S(1)} %project_3.1.refs_2_.refs_3_), custom_call_target="tpu_custom_call" | custom-call | flops 180000000 | tf_op jit(solution)/shard_map/project_2/pallas_call | solution.py:35
  37.7 7.9 %collective-permute-done.6.refs_1_ = bf16[256,1024]{1,0:T(8,128)(2,1)S(1)} collective-permute-done((bf16[256,1024]{1,0:T(8,128)(2,1)S(1)}, bf16[256,1024]{1,0:T(8,128)(2,1)S(1)}, u32[]{:S(2)}, u32[]{:S(2)}) %collective-permute-start.6) | collective-permute-done | bytes 524320 | tf_op jit(solution)/shard_map/ppermute | solution.py:526
  45.8 4.0 %collective-permute-start.12 = (bf16[256,1024]{1,0:T(8,128)(2,1)S(1)}, bf16[256,1024]{1,0:T(8,128)(2,1)S(1)}, u32[]{:S(2)}, u32[]{:S(2)}) collective-permute-start(bf16[256,1024]{1,0:T(8,128)(2,1)S(1)} %get-tuple-element.75), channel_id=1, source_target_pairs={{0,1},{1,0},{2,3},{3,2},{4,5},{5,4},{6,7},{7,6},{8,9},{9,8},{10,11... | collective-permute-start | bytes 1572872 | tf_op jit(solution)/shard_map/ppermute | solution.py:531
  50.5 1.8 %project_1.1.refs_3_ = bf16[512,1024]{1,0:T(8,128)(2,1)S(1)} custom-call(s32[7]{0:T(128)S(1)} %pad_add_fusion.refs_0_, bf16[512,1024]{1,0:T(8,128)(2,1)S(1)} %get-tuple-element.65.refs_1_, bf16[1024,4096]{1,0:T(8,128)(2,1)S(1)} %copy-done, bf16[256,1024]{1,0:T(8,128)(2,1)S(1)} %get-tuple-element.70.refs_3_), custom_call_target="tpu_custom_call" | custom-call | flops 180000000 | tf_op jit(solution)/shard_map/project_1/pallas_call | solution.py:35
  52.3 1.8 %project_0.1.refs_4_.p_ref = bf16[512,1024]{1,0:T(8,128)(2,1)S(1)} custom-call(s32[7]{0:T(128)S(1)} %pad_add_fusion.refs_0_, bf16[512,1024]{1,0:T(8,128)(2,1)S(1)} %get-tuple-element.65.refs_1_, bf16[1024,4096]{1,0:T(8,128)(2,1)S(1)} %copy-done, bf16[512,1024]{1,0:T(8,128)(2,1)S(1)} %project_1.1.refs_3_), custom_call_target="tpu_custom_call" | custom-call | flops 180000000 | tf_op jit(solution)/shard_map/project_0/pallas_call | solution.py:35
  54.1 1.8 %back_1.1.refs_4_.refs_3_ = f32[512,1024]{1,0:T(8,128)S(1)} custom-call(s32[7]{0:T(128)S(1)} %pad_add_fusion.refs_0_, bf16[1024,4096]{1,0:T(8,128)(2,1)S(1)} %copy-done, bf16[512,1024]{1,0:T(8,128)(2,1)S(1)} %collective-permute-done.4.refs_1_.refs_2_, f32[512,1024]{1,0:T(8,128)S(1)} %back_own.1.refs_5_.refs_3_, bf16[512,1024]{1,0:T(8,128)(2,1)S(1)} %project_0.1.refs_4_.p_ref), custom_call_target="tpu_custom_call" | custom-call | flops 180000000 | tf_op jit(solution)/shard_map/back_1/pallas_call | solution.py:35
  57.1 4.0 %collective-permute-start.10 = (bf16[256,1024]{1,0:T(8,128)(2,1)S(1)}, bf16[256,1024]{1,0:T(8,128)(2,1)S(1)}, u32[]{:S(2)}, u32[]{:S(2)}) collective-permute-start(bf16[256,1024]{1,0:T(8,128)(2,1)S(1)} %get-tuple-element.73), channel_id=1, source_target_pairs={{0,1},{1,0},{2,3},{3,2},{4,5},{5,4},{6,7},{7,6},{8,9},{9,8},{10,11... | collective-permute-start | bytes 1572872 | tf_op jit(solution)/shard_map/ppermute | solution.py:536
  62.2 1.8 %back_2.1.refs_2_.refs_5_.refs_6_ = f32[512,1024]{1,0:T(8,128)S(1)} custom-call(s32[7]{0:T(128)S(1)} %pad_add_fusion.refs_0_, bf16[1024,4096]{1,0:T(8,128)(2,1)S(1)} %copy-done, bf16[512,1024]{1,0:T(8,128)(2,1)S(1)} %pick.3.refs_2_, f32[512,1024]{1,0:T(8,128)S(1)} %back_1.1.refs_4_.refs_3_), custom_call_target="tpu_custom_call" | custom-call | flops 180000000 | tf_op jit(solution)/shard_map/back_2/pallas_call | solution.py:35
  64.8 3.3 %collective-permute-done.12.refs_0_.refs_3_ = bf16[256,1024]{1,0:T(8,128)(2,1)S(1)} collective-permute-done((bf16[256,1024]{1,0:T(8,128)(2,1)S(1)}, bf16[256,1024]{1,0:T(8,128)(2,1)S(1)}, u32[]{:S(2)}, u32[]{:S(2)}) %collective-permute-start.12) | collective-permute-done | bytes 524320 | tf_op jit(solution)/shard_map/ppermute | solution.py:531
  68.2 4.0 %collective-permute-start.20 = (bf16[256,1024]{1,0:T(8,128)(2,1)S(1)}, bf16[256,1024]{1,0:T(8,128)(2,1)S(1)}, u32[]{:S(2)}, u32[]{:S(2)}) collective-permute-start(bf16[256,1024]{1,0:T(8,128)(2,1)S(1)} %get-tuple-element.78.refs_9_), channel_id=1, source_target_pairs={{0,1},{1,0},{2,3},{3,2},{4,5},{5,4},{6,7},{7,6},{8,9},{9,8},{10,11... | collective-permute-start | bytes 1572872 | tf_op jit(solution)/shard_map/ppermute | solution.py:542
  72.2 2.2 %attended_grads.2 = (bf16[256,1024]{1,0:T(8,128)(2,1)S(1)}, f32[8,128,128]{2,1,0:T(8,128)S(1)}) custom-call(f32[32,128]{1,0:T(8,128)S(1)} %get-tuple-element.55.refs_0_.refs_2_.refs_1_, f32[512,128]{1,0:T(8,128)S(1)} %get-tuple-element.56.refs_1_.refs_3_.refs_2_, bf16[1024,1024]{1,0:T(8,128)(2,1)S(1)} %block.1.refs_4_.refs_2_.refs_3_, ...), custom_call_target="tpu_custom_call" | custom-call | flops 200000000 | tf_op jit(solution)/shard_map/attended_grads/pallas_call | solution.py:35
  75.1 2.9 %first_grads.1 = (bf16[256,1024]{1,0:T(8,128)(2,1)S(1)}, f32[256,1024]{1,0:T(8,128)S(1)}, f32[256,1024]{1,0:T(8,128)S(1)}) custom-call(s32[512,128]{1,0:T(8,128)S(1)} %get-tuple-element.60.refs_0_, s32[8,512]{1,0:T(8,128)S(1)} %get-tuple-element.80.refs_1_.refs_0_, f32[32,128]{1,0:T(8,128)S(1)} %get-tuple-element.55.refs_0_.refs_2_.refs_1_, ...), custom_call_target="tpu_custom_call" | custom-call | flops 200000000 | tf_op jit(solution)/shard_map/first_grads/pallas_call | solution.py:35
  79.3 2.3 %attended_grads.3 = (bf16[256,1024]{1,0:T(8,128)(2,1)S(1)}, bf16[4,128,128]{2,1,0:T(8,128)(2,1)S(1)}, bf16[4,128,128]{2,1,0:T(8,128)(2,1)S(1)}) custom-call(f32[8,128,128]{2,1,0:T(8,128)S(1)} %get-tuple-element.79.refs_0_, f32[32,128]{1,0:T(8,128)S(1)} %get-tuple-element.55.refs_0_.refs_2_.refs_1_, f32[512,128]{1,0:T(8,128)S(1)} %get-tuple-element.56.refs_1_.refs_3_.refs_2_, ...), custom_call_target="tpu_custom_call" | custom-call | flops 200000000 | tf_op jit(solution)/shard_map/attended_grads/pallas_call | solution.py:35
  81.8 1.8 %collective-permute-start.14 = (bf16[256,1024]{1,0:T(8,128)(2,1)S(1)}, bf16[256,1024]{1,0:T(8,128)(2,1)S(1)}, u32[]{:S(2)}, u32[]{:S(2)}) collective-permute-start(bf16[256,1024]{1,0:T(8,128)(2,1)S(1)} %get-tuple-element.84), channel_id=1, source_target_pairs={{0,1},{1,0},{2,3},{3,2},{4,5},{5,4},{6,7},{7,6},{8,9},{9,8},{10,11... | collective-permute-start | bytes 1572872 | tf_op jit(solution)/shard_map/ppermute | solution.py:561
  86.1 2.4 %key_value_grads.1 = (f32[512,1024]{1,0:T(8,128)S(1)}, f32[512,1024]{1,0:T(8,128)S(1)}) custom-call(s32[8,512]{1,0:T(8,128)S(1)} %get-tuple-element.80.refs_1_.refs_0_, bf16[512,1024]{1,0:T(8,128)(2,1)S(1)} %copy-done.1, bf16[512,1024]{1,0:T(8,128)(2,1)S(1)} %copy-done.2, bf16[512,1024]{1,0:T(8,128)(2,1)S(1)} %copy-done.3, ...), custom_call_target="tpu_custom_call" | custom-call | flops 1000000 | tf_op jit(solution)/shard_map/key_value_grads/pallas_call | solution.py:35
  91.9 2.9 %query_grad.1 = (bf16[512,1024]{1,0:T(8,128)(2,1)}, f32[8,128]{1,0:T(8,128)S(1)}) custom-call(s32[512,128]{1,0:T(8,128)S(1)} %get-tuple-element.60.refs_0_, f32[32,128]{1,0:T(8,128)S(1)} %get-tuple-element.55.refs_0_.refs_2_.refs_1_, f32[512,128]{1,0:T(8,128)S(1)} %get-tuple-element.56.refs_1_.refs_3_.refs_2_, bf16[512,1024]{1,0:T(8,128)(2,1)S(1)} %copy-done.2, ...), custom_call_target="tpu_custom_call" | custom-call | flops 1000000 | tf_op jit(solution)/shard_map/query_grad/pallas_call | solution.py:35
  96.9 2.1 %last_grads.1 = (bf16[512,1024]{1,0:T(8,128)(2,1)}, bf16[512,1024]{1,0:T(8,128)(2,1)}, f32[8,128]{1,0:T(8,128)S(1)}) custom-call(f32[32,128]{1,0:T(8,128)S(1)} %get-tuple-element.55.refs_0_.refs_2_.refs_1_, f32[512,128]{1,0:T(8,128)S(1)} %get-tuple-element.57.refs_1_, bf16[512,1024]{1,0:T(8,128)(2,1)S(1)} %copy-done.2, bf16[512,1024]{1,0:T(8,128)(2,1)S(1)} %copy-done.3, ...), custom_call_target="tpu_custom_call" | custom-call | flops 1000000 | tf_op jit(solution)/shard_map/last_grads/pallas_call | solution.py:35
  (63 shorter events, 31.6 us)
Async XLA Ops:
  0.6 26.0 %collective-permute-start.5 = (bf16[512,1024]{1,0:T(8,128)(2,1)}, bf16[512,1024]{1,0:T(8,128)(2,1)S(1)}, u32[]{:S(2)}, u32[]{:S(2)}) collective-permute-start(bf16[512,1024]{1,0:T(8,128)(2,1)} %refs_2_.12), channel_id=1, source_target_pairs={{1,2},{2,1},{5,6},{6,5},{9,10},{10,9},{13,14},{14,13},{17,18},{18,... | collective-permute-start | bytes 3145736 | tf_op jit(solution)/shard_map/ppermute | solution.py:498
  1.4 28.9 %collective-permute-start.4 = (bf16[512,1024]{1,0:T(8,128)(2,1)}, bf16[512,1024]{1,0:T(8,128)(2,1)S(1)}, u32[]{:S(2)}, u32[]{:S(2)}) collective-permute-start(bf16[512,1024]{1,0:T(8,128)(2,1)} %refs_2_.12), channel_id=1, source_target_pairs={{0,1},{1,0},{2,3},{3,2},{4,5},{5,4},{6,7},{7,6},{8,9},{9,8},{10,11... | collective-permute-start | bytes 3145736 | tf_op jit(solution)/shard_map/ppermute | solution.py:497
  9.5 9.4 %copy-start.4 = (bf16[512,1024]{1,0:T(8,128)(2,1)S(1)}, bf16[512,1024]{1,0:T(8,128)(2,1)}, u32[]{:S(2)}) copy-start(bf16[512,1024]{1,0:T(8,128)(2,1)} %refs_2_.12) | copy-start | bytes 3145732
  10.1 1.4 %collective-permute-start = (bf16[4,128,128]{2,1,0:T(8,128)(2,1)S(1)}, bf16[4,128,128]{2,1,0:T(8,128)(2,1)S(1)}, u32[]{:S(2)}, u32[]{:S(2)}) collective-permute-start(bf16[4,128,128]{2,1,0:T(8,128)(2,1)S(1)} %get-tuple-element.59), channel_id=1, source_target_pairs={{0,4},{4,0},{8,12},{12,8},{16,20},{20,16},{24,28},{28,24},{1,5},{5... | collective-permute-start | bytes 393224 | tf_op jit(solution)/shard_map/ppermute | solution.py:172
  11.5 7.3 %copy-start = (bf16[1024,4096]{1,0:T(8,128)(2,1)S(1)}, bf16[1024,4096]{1,0:T(8,128)(2,1)}, u32[]{:S(2)}) copy-start(bf16[1024,4096]{1,0:T(8,128)(2,1)} %refs_1_.10) | copy-start | bytes 25165828
  11.6 5.6 %collective-permute-start.1 = (bf16[4,128,128]{2,1,0:T(8,128)(2,1)S(1)}, bf16[4,128,128]{2,1,0:T(8,128)(2,1)S(1)}, u32[]{:S(2)}, u32[]{:S(2)}) collective-permute-start(bf16[4,128,128]{2,1,0:T(8,128)(2,1)S(1)} %pair_total.2.refs_4_.refs_2_), channel_id=1, source_target_pairs={{0,8},{4,12},{8,0},{12,4},{16,24},{20,28},{24,16},{28,20},{1,9},{5... | collective-permute-start | bytes 393224 | tf_op jit(solution)/shard_map/ppermute | solution.py:185
  17.3 5.0 %collective-permute-start.2 = (bf16[4,128,128]{2,1,0:T(8,128)(2,1)S(1)}, bf16[4,128,128]{2,1,0:T(8,128)(2,1)S(1)}, u32[]{:S(2)}, u32[]{:S(2)}) collective-permute-start(bf16[4,128,128]{2,1,0:T(8,128)(2,1)S(1)} %get-tuple-element.61), channel_id=1, source_target_pairs={{0,16},{4,20},{8,24},{12,28},{16,0},{20,4},{24,8},{28,12},{1,17},{... | collective-permute-start | bytes 393224 | tf_op jit(solution)/shard_map/ppermute | solution.py:185
  22.4 1.4 %collective-permute-start.3 = (bf16[4,128,128]{2,1,0:T(8,128)(2,1)S(1)}, bf16[4,128,128]{2,1,0:T(8,128)(2,1)S(1)}, u32[]{:S(2)}, u32[]{:S(2)}) collective-permute-start(bf16[4,128,128]{2,1,0:T(8,128)(2,1)S(1)} %get-tuple-element.64), channel_id=1, source_target_pairs={{0,4},{4,0},{8,12},{12,8},{16,20},{20,16},{24,28},{28,24},{1,5},{5... | collective-permute-start | bytes 393224 | tf_op jit(solution)/shard_map/ppermute | solution.py:199
  30.7 14.9 %collective-permute-start.6 = (bf16[256,1024]{1,0:T(8,128)(2,1)S(1)}, bf16[256,1024]{1,0:T(8,128)(2,1)S(1)}, u32[]{:S(2)}, u32[]{:S(2)}) collective-permute-start(bf16[256,1024]{1,0:T(8,128)(2,1)S(1)} %get-tuple-element.68), channel_id=1, source_target_pairs={{0,1},{1,0},{2,3},{3,2},{4,5},{5,4},{6,7},{7,6},{8,9},{9,8},{10,11... | collective-permute-start | bytes 1572872 | tf_op jit(solution)/shard_map/ppermute | solution.py:526
  32.5 13.1 %collective-permute-start.7 = (bf16[256,1024]{1,0:T(8,128)(2,1)S(1)}, bf16[256,1024]{1,0:T(8,128)(2,1)S(1)}, u32[]{:S(2)}, u32[]{:S(2)}) collective-permute-start(bf16[256,1024]{1,0:T(8,128)(2,1)S(1)} %get-tuple-element.69), channel_id=1, source_target_pairs={{1,2},{2,1},{5,6},{6,5},{9,10},{10,9},{13,14},{14,13},{17,18},{18,... | collective-permute-start | bytes 1572872 | tf_op jit(solution)/shard_map/ppermute | solution.py:526
  33.2 23.7 %collective-permute-start.8 = (bf16[256,1024]{1,0:T(8,128)(2,1)S(1)}, bf16[256,1024]{1,0:T(8,128)(2,1)S(1)}, u32[]{:S(2)}, u32[]{:S(2)}) collective-permute-start(bf16[256,1024]{1,0:T(8,128)(2,1)S(1)} %get-tuple-element.71), channel_id=1, source_target_pairs={{0,1},{1,0},{2,3},{3,2},{4,5},{5,4},{6,7},{7,6},{8,9},{9,8},{10,11... | collective-permute-start | bytes 1572872 | tf_op jit(solution)/shard_map/ppermute | solution.py:527
  35.2 21.7 %collective-permute-start.9 = (bf16[256,1024]{1,0:T(8,128)(2,1)S(1)}, bf16[256,1024]{1,0:T(8,128)(2,1)S(1)}, u32[]{:S(2)}, u32[]{:S(2)}) collective-permute-start(bf16[256,1024]{1,0:T(8,128)(2,1)S(1)} %get-tuple-element.72), channel_id=1, source_target_pairs={{1,2},{2,1},{5,6},{6,5},{9,10},{10,9},{13,14},{14,13},{17,18},{18,... | collective-permute-start | bytes 1572872 | tf_op jit(solution)/shard_map/ppermute | solution.py:527
  45.8 22.2 %collective-permute-start.12 = (bf16[256,1024]{1,0:T(8,128)(2,1)S(1)}, bf16[256,1024]{1,0:T(8,128)(2,1)S(1)}, u32[]{:S(2)}, u32[]{:S(2)}) collective-permute-start(bf16[256,1024]{1,0:T(8,128)(2,1)S(1)} %get-tuple-element.75), channel_id=1, source_target_pairs={{0,1},{1,0},{2,3},{3,2},{4,5},{5,4},{6,7},{7,6},{8,9},{9,8},{10,11... | collective-permute-start | bytes 1572872 | tf_op jit(solution)/shard_map/ppermute | solution.py:531
  49.8 18.3 %collective-permute-start.13 = (bf16[256,1024]{1,0:T(8,128)(2,1)S(1)}, bf16[256,1024]{1,0:T(8,128)(2,1)S(1)}, u32[]{:S(2)}, u32[]{:S(2)}) collective-permute-start(bf16[256,1024]{1,0:T(8,128)(2,1)S(1)} %get-tuple-element.70.refs_3_), channel_id=1, source_target_pairs={{1,2},{2,1},{5,6},{6,5},{9,10},{10,9},{13,14},{14,13},{17,18},{18,... | collective-permute-start | bytes 1572872 | tf_op jit(solution)/shard_map/ppermute | solution.py:531
  57.1 22.2 %collective-permute-start.10 = (bf16[256,1024]{1,0:T(8,128)(2,1)S(1)}, bf16[256,1024]{1,0:T(8,128)(2,1)S(1)}, u32[]{:S(2)}, u32[]{:S(2)}) collective-permute-start(bf16[256,1024]{1,0:T(8,128)(2,1)S(1)} %get-tuple-element.73), channel_id=1, source_target_pairs={{0,1},{1,0},{2,3},{3,2},{4,5},{5,4},{6,7},{7,6},{8,9},{9,8},{10,11... | collective-permute-start | bytes 1572872 | tf_op jit(solution)/shard_map/ppermute | solution.py:536
  61.0 20.6 %collective-permute-start.11 = (bf16[256,1024]{1,0:T(8,128)(2,1)S(1)}, bf16[256,1024]{1,0:T(8,128)(2,1)S(1)}, u32[]{:S(2)}, u32[]{:S(2)}) collective-permute-start(bf16[256,1024]{1,0:T(8,128)(2,1)S(1)} %get-tuple-element.74.refs_5_), channel_id=1, source_target_pairs={{1,2},{2,1},{5,6},{6,5},{9,10},{10,9},{13,14},{14,13},{17,18},{18,... | collective-permute-start | bytes 1572872 | tf_op jit(solution)/shard_map/ppermute | solution.py:536
  68.2 27.4 %collective-permute-start.20 = (bf16[256,1024]{1,0:T(8,128)(2,1)S(1)}, bf16[256,1024]{1,0:T(8,128)(2,1)S(1)}, u32[]{:S(2)}, u32[]{:S(2)}) collective-permute-start(bf16[256,1024]{1,0:T(8,128)(2,1)S(1)} %get-tuple-element.78.refs_9_), channel_id=1, source_target_pairs={{0,1},{1,0},{2,3},{3,2},{4,5},{5,4},{6,7},{7,6},{8,9},{9,8},{10,11... | collective-permute-start | bytes 1572872 | tf_op jit(solution)/shard_map/ppermute | solution.py:542
  74.4 21.2 %collective-permute-start.21 = (bf16[256,1024]{1,0:T(8,128)(2,1)S(1)}, bf16[256,1024]{1,0:T(8,128)(2,1)S(1)}, u32[]{:S(2)}, u32[]{:S(2)}) collective-permute-start(bf16[256,1024]{1,0:T(8,128)(2,1)S(1)} %get-tuple-element.99), channel_id=1, source_target_pairs={{1,2},{2,1},{5,6},{6,5},{9,10},{10,9},{13,14},{14,13},{17,18},{18,... | collective-permute-start | bytes 1572872 | tf_op jit(solution)/shard_map/ppermute | solution.py:549
  81.6 2.9 %collective-permute-start.16 = (bf16[4,128,128]{2,1,0:T(8,128)(2,1)S(1)}, bf16[4,128,128]{2,1,0:T(8,128)(2,1)S(1)}, u32[]{:S(2)}, u32[]{:S(2)}) collective-permute-start(bf16[4,128,128]{2,1,0:T(8,128)(2,1)S(1)} %get-tuple-element.83.refs_4_), channel_id=1, source_target_pairs={{0,4},{4,0},{8,12},{12,8},{16,20},{20,16},{24,28},{28,24},{1,5},{5... | collective-permute-start | bytes 393224 | tf_op jit(solution)/shard_map/ppermute | solution.py:172
  81.8 17.9 %collective-permute-start.14 = (bf16[256,1024]{1,0:T(8,128)(2,1)S(1)}, bf16[256,1024]{1,0:T(8,128)(2,1)S(1)}, u32[]{:S(2)}, u32[]{:S(2)}) collective-permute-start(bf16[256,1024]{1,0:T(8,128)(2,1)S(1)} %get-tuple-element.84), channel_id=1, source_target_pairs={{0,1},{1,0},{2,3},{3,2},{4,5},{5,4},{6,7},{7,6},{8,9},{9,8},{10,11... | collective-permute-start | bytes 1572872 | tf_op jit(solution)/shard_map/ppermute | solution.py:561
  83.6 16.1 %collective-permute-start.15 = (bf16[256,1024]{1,0:T(8,128)(2,1)S(1)}, bf16[256,1024]{1,0:T(8,128)(2,1)S(1)}, u32[]{:S(2)}, u32[]{:S(2)}) collective-permute-start(bf16[256,1024]{1,0:T(8,128)(2,1)S(1)} %get-tuple-element.85), channel_id=1, source_target_pairs={{1,2},{2,1},{5,6},{6,5},{9,10},{10,9},{13,14},{14,13},{17,18},{18,... | collective-permute-start | bytes 1572872 | tf_op jit(solution)/shard_map/ppermute | solution.py:561
  84.6 5.7 %collective-permute-start.17 = (bf16[4,128,128]{2,1,0:T(8,128)(2,1)S(1)}, bf16[4,128,128]{2,1,0:T(8,128)(2,1)S(1)}, u32[]{:S(2)}, u32[]{:S(2)}) collective-permute-start(bf16[4,128,128]{2,1,0:T(8,128)(2,1)S(1)} %pair_total.3.refs_7_.refs_2_), channel_id=1, source_target_pairs={{0,8},{4,12},{8,0},{12,4},{16,24},{20,28},{24,16},{28,20},{1,9},{5... | collective-permute-start | bytes 393224 | tf_op jit(solution)/shard_map/ppermute | solution.py:185
  90.3 5.0 %collective-permute-start.18 = (bf16[4,128,128]{2,1,0:T(8,128)(2,1)S(1)}, bf16[4,128,128]{2,1,0:T(8,128)(2,1)S(1)}, u32[]{:S(2)}, u32[]{:S(2)}) collective-permute-start(bf16[4,128,128]{2,1,0:T(8,128)(2,1)S(1)} %get-tuple-element.92.refs_9_), channel_id=1, source_target_pairs={{0,16},{4,20},{8,24},{12,28},{16,0},{20,4},{24,8},{28,12},{1,17},{... | collective-permute-start | bytes 393224 | tf_op jit(solution)/shard_map/ppermute | solution.py:185
  95.5 1.4 %collective-permute-start.19 = (bf16[4,128,128]{2,1,0:T(8,128)(2,1)S(1)}, bf16[4,128,128]{2,1,0:T(8,128)(2,1)S(1)}, u32[]{:S(2)}, u32[]{:S(2)}) collective-permute-start(bf16[4,128,128]{2,1,0:T(8,128)(2,1)S(1)} %get-tuple-element.96), channel_id=1, source_target_pairs={{0,4},{4,0},{8,12},{12,8},{16,20},{20,16},{24,28},{28,24},{1,5},{5... | collective-permute-start | bytes 393224 | tf_op jit(solution)/shard_map/ppermute | solution.py:199
  (3 other events, 7.2 us)
